TPU v7x, 512 devices: a whole 4x8x8 slice. The times are simulated.
512 devices in a mesh: ctx: 16 (over z, core), exp: 32 (over y, x).
Axes of the slice: x: 4, y: 8, z: 8, core: 2. Of those that a mesh axis runs over, the one named last changes fastest.
Arguments:
- tokens: bfloat16 [65536, 2048], P(('ctx', 'exp')), may hold values from -6 to 6
- cotangent: bfloat16 [65536, 2048], P(('ctx', 'exp')), may hold values from -6 to 6
- expert_ids: int32 [2, 65536, 1], P(None, ('ctx', 'exp')), may hold values from 0 to 31
- weight_in: bfloat16 [32, 2048, 256], P('exp', 'ctx'), may hold values from -0.125 to 0.125
- weight_out: bfloat16 [32, 256, 2048], P('exp', None, 'ctx'), may hold values from -0.375 to 0.375
- router: bfloat16 [2048, 32], P('ctx', 'exp'), may hold values from -0.125 to 0.125
Outputs:
- grad_in: float32 [32, 2048, 256], P('exp', 'ctx')
- grad_out: float32 [32, 256, 2048], P('exp', None, 'ctx')
Inputs may be any that keep to these rules, and one draw needn't show every extreme that they name: `expert_ids`: each token chooses one expert in each recurrence; every expert is chosen by some token.
All inputs are finite; a program needn't handle non-finite values.
Results may differ from a plain program's by a relative error of at most 0.023.
Values may be sent and summed in bfloat16 or wider, within the bound.
No kernel may reach another device: no remote copies, remote signals or barrier semaphores. Data moves between devices by JAX's collectives and lax.ppermute only.
A program may use at most 64 MiB of HBM per device.

v0:
```python
import jax
import jax.numpy as jnp
from jax import lax
from jax.sharding import PartitionSpec as P

epsilon = 1e-06


def normalize(state):
    scale_row = jnp.sqrt(jnp.mean(state * state, axis=-1, keepdims=True) + epsilon)
    return (state / scale_row, scale_row)


def norm_backward(upstream, unit, scale_row):
    return (upstream - unit * jnp.mean(upstream * unit, axis=-1, keepdims=True)) / scale_row


def slot_plan(chosen, groups, capacity):
    token_count = chosen.shape[0]
    experts_row = lax.broadcasted_iota(jnp.int32, (token_count, groups), 1)
    onehot = (chosen[:, None] == experts_row).astype(jnp.int32)
    before = jnp.cumsum(onehot, axis=0) - onehot
    position = jnp.sum(before * onehot, axis=1)
    total_slots = groups * capacity
    slot = jnp.where(position < capacity, chosen * capacity + position, total_slots)
    table = jnp.full((total_slots + 1,), token_count, jnp.int32)
    table = table.at[slot].set(lax.iota(jnp.int32, token_count))[:total_slots]
    return (slot, table)


def take_rows(values, table):
    padded = jnp.concatenate([values, jnp.zeros((1, values.shape[1]), values.dtype)], axis=0)
    return padded[table]


def back_rows(buffer, slot):
    padded = jnp.concatenate([buffer, jnp.zeros((1, buffer.shape[1]), buffer.dtype)], axis=0)
    return padded[slot]


def send_owner(rows):
    return lax.all_to_all(rows, "exp", split_axis=0, concat_axis=0, tiled=True)


def send_source(rows):
    return lax.all_to_all(rows, "exp", split_axis=0, concat_axis=0, tiled=True)


def expert_forward(rows, weight_a, weight_b, column):
    before_relu = jnp.dot(rows, weight_a, preferred_element_type=jnp.float32)
    positive = jnp.maximum(before_relu, 0.0)
    hidden = (positive * positive).astype(jnp.bfloat16)
    expert_out = jnp.dot(hidden, weight_b, preferred_element_type=jnp.float32)
    logit = jnp.dot(rows, column, preferred_element_type=jnp.float32)
    gate_value = jax.nn.sigmoid(logit)
    return (before_relu, hidden, expert_out, gate_value)


def expert_backward(upstream, weight_b, parts):
    before_relu, hidden, expert_out, gate_value = parts
    upper = upstream.astype(jnp.float32)
    grad_expert = (gate_value * upper).astype(jnp.bfloat16)
    grad_gate = jnp.sum(upper * expert_out, axis=1, keepdims=True)
    grad_logit = grad_gate * gate_value * (1.0 - gate_value)
    grad_hidden = lax.dot_general(
        grad_expert, weight_b, (((1,), (1,)), ((), ())), preferred_element_type=jnp.float32
    )
    grad_pre = (grad_hidden * 2.0 * jnp.maximum(before_relu, 0.0)).astype(jnp.bfloat16)
    return (grad_expert, grad_pre, grad_logit)


def outer_rows(left, right):
    return lax.dot_general(
        left, right, (((0,), (0,)), ((), ())), preferred_element_type=jnp.float32
    )


def on_device(tokens, cotangent, expert_ids, weight_in, weight_out, router):
    groups = lax.axis_size("exp")
    token_count = tokens.shape[0]
    capacity = 3 * token_count // (4 * groups)
    first_slot, first_table = slot_plan(expert_ids[0, :, 0], groups, capacity)
    second_slot, second_table = slot_plan(expert_ids[1, :, 0], groups, capacity)
    full_in, full_out, column = (
        lax.all_gather(weight_in, "ctx", axis=1, tiled=True),
        lax.all_gather(weight_out, "ctx", axis=2, tiled=True),
        lax.all_gather(router, "ctx", axis=0, tiled=True),
    )
    weight_a = full_in[0]
    weight_b = full_out[0]
    state_zero = tokens.astype(jnp.float32)
    unit_zero, scale_zero = normalize(state_zero)
    rows_zero = send_owner(take_rows(unit_zero.astype(jnp.bfloat16), first_table))
    parts_zero = expert_forward(rows_zero, weight_a, weight_b, column)
    mixed = send_source((parts_zero[3] * parts_zero[2]).astype(jnp.bfloat16))
    state_one = state_zero + back_rows(mixed, first_slot).astype(jnp.float32)
    unit_one, scale_one = normalize(state_one)
    routed_one = take_rows(unit_one.astype(jnp.bfloat16), second_table)
    upstream_rows = take_rows(cotangent, second_table)
    rows_one, upstream_one = (
        lax.all_to_all(routed_one, "exp", split_axis=0, concat_axis=0, tiled=True),
        lax.all_to_all(upstream_rows, "exp", split_axis=0, concat_axis=0, tiled=True),
    )
    parts_one = expert_forward(rows_one, weight_a, weight_b, column)
    gout_one, gpre_one, logit_one = expert_backward(upstream_one, weight_b, parts_one)
    flowing = lax.dot_general(
        gpre_one, weight_a, (((1,), (1,)), ((), ())), preferred_element_type=jnp.float32
    )
    grad_rows = (flowing + logit_one * column[:, 0].astype(jnp.float32)[None, :]).astype(
        jnp.bfloat16
    )
    grad_unit = back_rows(send_source(grad_rows), second_slot).astype(jnp.float32)
    grad_state = cotangent.astype(jnp.float32) + norm_backward(grad_unit, unit_one, scale_one)
    upstream_zero = send_owner(take_rows(grad_state.astype(jnp.bfloat16), first_table))
    gout_zero, gpre_zero, logit_zero = expert_backward(upstream_zero, weight_b, parts_zero)
    wide_rows = jnp.concatenate([rows_zero, rows_one], axis=0)
    wide_grads = jnp.concatenate([gout_zero, gout_one], axis=0)
    narrow_hidden = jnp.concatenate([parts_zero[1], parts_one[1]], axis=0)
    narrow_pre = jnp.concatenate([gpre_zero, gpre_one], axis=0)
    part_in = outer_rows(wide_rows, narrow_pre)
    part_out = outer_rows(narrow_hidden, wide_grads)
    grad_in, grad_out = (
        lax.psum_scatter(
            part_in[None].astype(jnp.bfloat16), "ctx", scatter_dimension=1, tiled=True
        ).astype(jnp.float32),
        lax.psum_scatter(
            part_out[None].astype(jnp.bfloat16), "ctx", scatter_dimension=2, tiled=True
        ).astype(jnp.float32),
    )
    return (grad_in, grad_out)


def solution(mesh):
    placed = (
        P(("ctx", "exp"), None),
        P(("ctx", "exp"), None),
        P(None, ("ctx", "exp"), None),
        P("exp", "ctx", None),
        P("exp", None, "ctx"),
        P("ctx", "exp"),
    )
    return jax.shard_map(
        on_device,
        mesh=mesh,
        in_specs=placed,
        out_specs=(P("exp", "ctx", None), P("exp", None, "ctx")),
        check_vma=False,
    )
```

profile of v0, /device:TPU:1, one launch (start us, length us, event | category | flops | bytes accessed | tf_op | source)
XLA Modules:
  0.0 367.6 jit_solution(8977786849808920177)
XLA Ops:
  8.7 1.2 fusion.21
  10.7 1.2 fusion.22
  15.5 10.5 %all-to-all-start = ((bf16[32,3,2048]{2,1,0:T(4,128)(2,1)}), bf16[32,3,2048]{2,1,0:T(4,128)(2,1)S(1)}, u32[]{:S(2)}, u32[]{:S(2)}) async-start(bf16[32,3,2048]{2,1,0:T(4,128)(2,1)} %all_to_all.44), calls=%async_computation | async-start | bytes 1048576 | tf_op jit(solution)/shard_map/all_to_all | solution.py:42
  26.0 23.8 %all_gather.9 = bf16[2048,1]{0,1:T(2,128)(2,1)S(1)} all-gather(bf16[128,1]{0,1:T(2,128)(2,1)S(1)} %copy-done.26), channel_id=1, replica_groups=mesh['ctx'=16,'exp'=32] {'ctx'}, dimensions={0}, use_global_device_ids=true | all-gather | bytes 4352 | tf_op jit(solution)/shard_map/all_gather | solution.py:87
  50.4 7.7 %all-gather.3.cloned.1.call-done = bf16[1,2048,256]{2,1,0:T(8,128)(2,1)} async-done(((bf16[1,128,256]{2,1,0:T(8,128)(2,1)}), bf16[1,2048,256]{2,1,0:T(8,128)(2,1)}) %all-gather.3.cloned.1.call-update) | async-done | bytes 1048592 | tf_op jit(solution)/shard_map/all_gather | solution.py:85
  58.1 2.2 multiply_convert_fusion.5
  60.3 38.8 %all-gather.5.cloned.1.call-done = bf16[1,256,2048]{2,1,0:T(8,128)(2,1)} async-done(((bf16[1,256,128]{2,1,0:T(8,128)(2,1)}), bf16[1,256,2048]{2,1,0:T(8,128)(2,1)}) %all-gather.5.cloned.1.call-update) | async-done | bytes 1048592 | tf_op jit(solution)/shard_map/all_gather | solution.py:86
  99.1 1.6 fusion.2
  101.7 9.2 %all-to-all-start.1 = ((bf16[32,3,2048]{2,1,0:T(4,128)(2,1)}), bf16[32,3,2048]{2,1,0:T(4,128)(2,1)S(1)}, u32[]{:S(2)}, u32[]{:S(2)}) async-start(bf16[32,3,2048]{2,1,0:T(4,128)(2,1)} %all_to_all.47), calls=%async_computation.1 | async-start | bytes 1048576 | tf_op jit(solution)/shard_map/all_to_all | solution.py:46
  113.9 13.6 %all-to-all-done.1 = bf16[32,3,2048]{2,1,0:T(4,128)(2,1)S(1)} async-done(((bf16[32,3,2048]{2,1,0:T(4,128)(2,1)}), bf16[32,3,2048]{2,1,0:T(4,128)(2,1)S(1)}, u32[]{:S(2)}, u32[]{:S(2)}) %all-to-all-start.1) | async-done | bytes 393248 | tf_op jit(solution)/shard_map/all_to_all | solution.py:46
  127.5 5.1 %all-to-all-start.3 = ((bf16[32,3,2048]{2,1,0:T(4,128)(2,1)}), bf16[32,3,2048]{2,1,0:T(4,128)(2,1)}, u32[]{:S(2)}, u32[]{:S(2)}) async-start(bf16[32,3,2048]{2,1,0:T(4,128)(2,1)} %all_to_all.53), calls=%async_computation.3 | async-start | bytes 1048576 | tf_op jit(solution)/shard_map/all_to_all | solution.py:102
  136.4 11.2 %all-to-all-done.3 = bf16[32,3,2048]{2,1,0:T(4,128)(2,1)} async-done(((bf16[32,3,2048]{2,1,0:T(4,128)(2,1)}), bf16[32,3,2048]{2,1,0:T(4,128)(2,1)}, u32[]{:S(2)}, u32[]{:S(2)}) %all-to-all-start.3) | async-done | bytes 393248 | tf_op jit(solution)/shard_map/all_to_all | solution.py:102
  147.6 6.5 %all-to-all-start.2 = ((bf16[32,3,2048]{2,1,0:T(4,128)(2,1)}), bf16[32,3,2048]{2,1,0:T(4,128)(2,1)}, u32[]{:S(2)}, u32[]{:S(2)}) async-start(bf16[32,3,2048]{2,1,0:T(4,128)(2,1)} %all_to_all.50), calls=%async_computation.2 | async-start | bytes 1048576 | tf_op jit(solution)/shard_map/all_to_all | solution.py:101
  154.8 2.1 reshape.149
  156.9 12.2 %all-to-all-done.2 = bf16[32,3,2048]{2,1,0:T(4,128)(2,1)} async-done(((bf16[32,3,2048]{2,1,0:T(4,128)(2,1)}), bf16[32,3,2048]{2,1,0:T(4,128)(2,1)}, u32[]{:S(2)}, u32[]{:S(2)}) %all-to-all-start.2) | async-done | bytes 393248 | tf_op jit(solution)/shard_map/all_to_all | solution.py:101
  169.1 2.0 all_to_all.52
  171.2 2.0 multiply_convert_fusion.4
  175.1 2.1 multiply_convert_fusion.1
  177.2 2.0 convert_element_type.115
  179.2 1.5 fusion.7
  182.6 2.1 all_to_all.55
  184.6 6.5 %all-to-all-start.4 = ((bf16[32,3,2048]{2,1,0:T(4,128)(2,1)}), bf16[32,3,2048]{2,1,0:T(4,128)(2,1)S(1)}, u32[]{:S(2)}, u32[]{:S(2)}) async-start(bf16[32,3,2048]{2,1,0:T(4,128)(2,1)} %all_to_all.55), calls=%async_computation.4 | async-start | bytes 1048576 | tf_op jit(solution)/shard_map/all_to_all | solution.py:46
  191.2 14.8 %all-to-all-done.4 = bf16[32,3,2048]{2,1,0:T(4,128)(2,1)S(1)} async-done(((bf16[32,3,2048]{2,1,0:T(4,128)(2,1)}), bf16[32,3,2048]{2,1,0:T(4,128)(2,1)S(1)}, u32[]{:S(2)}, u32[]{:S(2)}) %all-to-all-start.4) | async-done | bytes 393248 | tf_op jit(solution)/shard_map/all_to_all | solution.py:46
  212.6 6.5 %all-to-all-start.5 = ((bf16[32,3,2048]{2,1,0:T(4,128)(2,1)}), bf16[32,3,2048]{2,1,0:T(4,128)(2,1)S(1)}, u32[]{:S(2)}, u32[]{:S(2)}) async-start(bf16[32,3,2048]{2,1,0:T(4,128)(2,1)} %all_to_all.58), calls=%async_computation.5 | async-start | bytes 1048576 | tf_op jit(solution)/shard_map/all_to_all | solution.py:42
  219.2 14.7 %all-to-all-done.5 = bf16[32,3,2048]{2,1,0:T(4,128)(2,1)S(1)} async-done(((bf16[32,3,2048]{2,1,0:T(4,128)(2,1)}), bf16[32,3,2048]{2,1,0:T(4,128)(2,1)S(1)}, u32[]{:S(2)}, u32[]{:S(2)}) %all-to-all-start.5) | async-done | bytes 393248 | tf_op jit(solution)/shard_map/all_to_all | solution.py:42
  234.8 2.3 fusion.1
  237.0 4.6 %copy.8 = bf16[1,256,2048]{1,0,2:T(2,128)(2,1)S(1)} copy(bf16[1,256,2048]{2,1,0:T(8,128)(2,1)} %fusion.1) | data formatting | bytes 2097152
  243.0 1.4 multiply_convert_fusion
  245.2 1.5 fusion
  246.7 51.2 %reduce-scatter.7.cloned.1.call-done = bf16[128,256]{1,0:T(8,128)(2,1)} async-done(((bf16[2048,256]{1,0:T(8,128)(2,1)}), bf16[128,256]{1,0:T(8,128)(2,1)}) %reduce-scatter.7.cloned.1.call-update) | async-done | bytes 65552
  299.6 59.9 %reduce-scatter.5.cloned.1.call-done = bf16[1,128,256]{2,1,0:T(8,128)(2,1)} async-done(((bf16[1,2048,256]{2,1,0:T(8,128)(2,1)}), bf16[1,128,256]{2,1,0:T(8,128)(2,1)}) %reduce-scatter.5.cloned.1.call-update) | async-done | bytes 65552 | tf_op jit(solution)/shard_map/reduce_scatter | solution.py:123
  359.5 1.5 convert_element_type.130
  (124 shorter events, 29.7 us)
Async XLA Ops:
  7.2 50.9 %all-gather.3.cloned.1.call-start = ((), (), s32[]{:S(2)}) async-start(), calls=%async_computation.8 | async-start | bytes 1114112 | tf_op jit(solution)/shard_map/all_gather | solution.py:85
  7.9 91.2 %all-gather.5.cloned.1.call-start = ((), (), s32[]{:S(2)}) async-start(), calls=%async_computation.9 | async-start | bytes 1114112 | tf_op jit(solution)/shard_map/all_gather | solution.py:86
  8.6 3.9 %copy-start.21 = (s32[2,128,1]{1,2,0:T(1,128)S(1)}, s32[2,128,1]{1,2,0:T(1,128)}, u32[]{:S(2)}) copy-start(s32[2,128,1]{1,2,0:T(1,128)} %param.8) | copy-start | bytes 3076
  12.6 98.4 %copy-start.23 = (s32[128]{0:T(128)}, s32[128]{0:T(128)S(1)}, u32[]{:S(2)}) copy-start(s32[128]{0:T(128)S(1)} %get-tuple-element.2) | copy-start | bytes 1540
  14.5 11.6 %copy-start.26 = (bf16[128,1]{0,1:T(2,128)(2,1)S(1)}, bf16[128,1]{0,1:T(2,128)(2,1)}, u32[]{:S(2)}) copy-start(bf16[128,1]{0,1:T(2,128)(2,1)} %param.11) | copy-start | bytes 772
  15.5 34.3 %all-to-all-start = ((bf16[32,3,2048]{2,1,0:T(4,128)(2,1)}), bf16[32,3,2048]{2,1,0:T(4,128)(2,1)S(1)}, u32[]{:S(2)}, u32[]{:S(2)}) async-start(bf16[32,3,2048]{2,1,0:T(4,128)(2,1)} %all_to_all.44), calls=%async_computation | async-start | bytes 1048576 | tf_op jit(solution)/shard_map/all_to_all | solution.py:42
  50.4 51.4 %copy-start.19 = (f32[96]{0:T(128)}, f32[96]{0:T(128)S(1)}, u32[]{:S(2)}) copy-start(f32[96]{0:T(128)S(1)} %fusion.16) | copy-start | bytes 1156
  60.3 41.5 %copy-start.10 = (bf16[96,256]{1,0:T(8,128)(2,1)}, bf16[96,256]{1,0:T(8,128)(2,1)S(1)}, u32[]{:S(2)}) copy-start(bf16[96,256]{1,0:T(8,128)(2,1)S(1)} %get-tuple-element.6) | copy-start | bytes 147460
  99.1 11.8 %copy-start.6 = (bf16[128,2048]{1,0:T(8,128)(2,1)S(1)}, bf16[128,2048]{1,0:T(8,128)(2,1)}, u32[]{:S(2)}) copy-start(bf16[128,2048]{1,0:T(8,128)(2,1)} %param.7) | copy-start | bytes 1572868
  101.7 25.8 %all-to-all-start.1 = ((bf16[32,3,2048]{2,1,0:T(4,128)(2,1)}), bf16[32,3,2048]{2,1,0:T(4,128)(2,1)S(1)}, u32[]{:S(2)}, u32[]{:S(2)}) async-start(bf16[32,3,2048]{2,1,0:T(4,128)(2,1)} %all_to_all.47), calls=%async_computation.1 | async-start | bytes 1048576 | tf_op jit(solution)/shard_map/all_to_all | solution.py:46
  127.5 20.2 %all-to-all-start.3 = ((bf16[32,3,2048]{2,1,0:T(4,128)(2,1)}), bf16[32,3,2048]{2,1,0:T(4,128)(2,1)}, u32[]{:S(2)}, u32[]{:S(2)}) async-start(bf16[32,3,2048]{2,1,0:T(4,128)(2,1)} %all_to_all.53), calls=%async_computation.3 | async-start | bytes 1048576 | tf_op jit(solution)/shard_map/all_to_all | solution.py:102
  132.9 1.0 copy-start
  134.3 1.1 copy-start.17
  136.4 34.7 %copy-start.2 = (bf16[1,2048,256]{2,1,0:T(8,128)(2,1)S(1)}, bf16[1,2048,256]{2,1,0:T(8,128)(2,1)}, u32[]{:S(2)}) copy-start(bf16[1,2048,256]{2,1,0:T(8,128)(2,1)} %all-gather.3.cloned.1.call-done) | copy-start | bytes 3145732
  147.6 21.5 %all-to-all-start.2 = ((bf16[32,3,2048]{2,1,0:T(4,128)(2,1)}), bf16[32,3,2048]{2,1,0:T(4,128)(2,1)}, u32[]{:S(2)}, u32[]{:S(2)}) async-start(bf16[32,3,2048]{2,1,0:T(4,128)(2,1)} %all_to_all.50), calls=%async_computation.2 | async-start | bytes 1048576 | tf_op jit(solution)/shard_map/all_to_all | solution.py:101
  156.9 16.3 %copy-start.1 = (bf16[1,256,2048]{2,1,0:T(8,128)(2,1)S(1)}, bf16[1,256,2048]{2,1,0:T(8,128)(2,1)}, u32[]{:S(2)}) copy-start(bf16[1,256,2048]{2,1,0:T(8,128)(2,1)} %all-gather.5.cloned.1.call-done) | copy-start | bytes 3145732
  171.2 2.1 copy-start.3
  171.2 2.5 copy-start.8
  173.2 1.2 copy-start.11
  177.2 4.1 %copy-start.15 = (f32[2048]{0:T(1024)S(1)}, f32[2048]{0:T(1024)}, u32[]{:S(2)}) copy-start(f32[2048]{0:T(1024)} %convert_element_type.120) | copy-start | bytes 24580
  177.2 4.1 %copy-start.25 = (f32[96]{0:T(128)S(1)}, f32[96]{0:T(128)}, u32[]{:S(2)}) copy-start(f32[96]{0:T(128)} %get-tuple-element.10) | copy-start | bytes 1156
  181.4 9.8 %copy-start.24 = (s32[128]{0:T(128)S(1)}, s32[128]{0:T(128)}, u32[]{:S(2)}) copy-start(s32[128]{0:T(128)} %copy-done.23) | copy-start | bytes 1540
  184.6 21.3 %all-to-all-start.4 = ((bf16[32,3,2048]{2,1,0:T(4,128)(2,1)}), bf16[32,3,2048]{2,1,0:T(4,128)(2,1)S(1)}, u32[]{:S(2)}, u32[]{:S(2)}) async-start(bf16[32,3,2048]{2,1,0:T(4,128)(2,1)} %all_to_all.55), calls=%async_computation.4 | async-start | bytes 1048576 | tf_op jit(solution)/shard_map/all_to_all | solution.py:46
  211.5 7.6 %copy-start.4 = (f32[96,2048]{1,0:T(8,128)S(1)}, f32[96,2048]{1,0:T(8,128)}, u32[]{:S(2)}) copy-start(f32[96,2048]{1,0:T(8,128)} %reshape.149) | copy-start | bytes 2359300
  211.5 7.6 %copy-start.22 = (f32[96]{0:T(128)S(1)}, f32[96]{0:T(128)}, u32[]{:S(2)}) copy-start(f32[96]{0:T(128)} %get-tuple-element.11) | copy-start | bytes 1156
  212.6 21.7 %copy-start.20 = (f32[96]{0:T(128)S(1)}, f32[96]{0:T(128)}, u32[]{:S(2)}) copy-start(f32[96]{0:T(128)} %copy-done.19) | copy-start | bytes 1156
  212.6 21.4 %all-to-all-start.5 = ((bf16[32,3,2048]{2,1,0:T(4,128)(2,1)}), bf16[32,3,2048]{2,1,0:T(4,128)(2,1)S(1)}, u32[]{:S(2)}, u32[]{:S(2)}) async-start(bf16[32,3,2048]{2,1,0:T(4,128)(2,1)} %all_to_all.58), calls=%async_computation.5 | async-start | bytes 1048576 | tf_op jit(solution)/shard_map/all_to_all | solution.py:42
  219.0 78.8 %reduce-scatter.7.cloned.1.call-start = ((), (), s32[]{:S(2)}) async-start(), calls=%async_computation.11 | async-start | bytes 1114112
  242.8 1.9 copy-start.12
  242.8 116.7 %reduce-scatter.5.cloned.1.call-start = ((), (), s32[]{:S(2)}) async-start(), calls=%async_computation.10 | async-start | bytes 1114112 | tf_op jit(solution)/shard_map/reduce_scatter | solution.py:123
  243.0 2.2 copy-start.9
  243.0 2.2 copy-start.14
  (5 other events, 4.3 us)
Sparse Core Ops, SparseCore 0:
  10.1 47.9 all-gather.2
  60.2 38.9 all-gather.4
  243.0 54.8 reduce-scatter.6
  300.8 58.7 reduce-scatter.4
where the time goes:
time: 371 us; the launch traced here: 368 us
  waiting for transfers between devices  226 us (61%)
  starting transfers between devices  44.4 us (12%)
  local copies, waits for them, and re-layouts  34.4 us (9%)
  blocking collectives  23.8 us (6%)
  between operations  14.3 us (4%)
  matrix products  14.1 us (4%)
  other arithmetic  10.9 us (3%)
    reduce_scatter x1, waiting for transfers between devices, on_device(): lax.psum_scatter(part_in[None].astype(jnp.bfloat16), 'ctx', scatter_dimen...  59.9 us
    unnamed x5, waiting for transfers between devices  52.6 us
    all_gather x1, waiting for transfers between devices, on_device(): lax.all_gather(weight_out, 'ctx', axis=2, tiled=True)  38.8 us
    all_to_all x2, waiting for transfers between devices, send_source(): return lax.all_to_all(rows, 'exp', split_axis=0, concat_axis=0, tiled=True)  28.4 us
    all_gather x1, blocking collectives, on_device(): lax.all_gather(router, 'ctx', axis=0, tiled=True)  23.8 us
    all_to_all x2, starting transfers between devices, send_owner(): return lax.all_to_all(rows, 'exp', split_axis=0, concat_axis=0, tiled=True)  17 us
    all_to_all x2, starting transfers between devices, send_source(): return lax.all_to_all(rows, 'exp', split_axis=0, concat_axis=0, tiled=True)  15.7 us
    all_to_all x2, waiting for transfers between devices, send_owner(): return lax.all_to_all(rows, 'exp', split_axis=0, concat_axis=0, tiled=True)  14.7 us
  transfers between devices with their start and end apart: 10, of which 9 were waited for; matrix products, arithmetic and copies ran while one was open for 6% of the time, Pallas kernels for 0%

commit v1 on v0

v1 whole, which is shorter than its diff:
```python
import functools

import jax
import jax.numpy as jnp
from jax import lax
from jax.experimental import pallas as pl
from jax.experimental.pallas import tpu as pltpu
from jax.sharding import PartitionSpec as P

epsilon = 1e-06
TOK, D, G, EXPERTS, CAP = 128, 2048, 256, 32, 3
SLOTS = EXPERTS * CAP
LANE = 128
CHUNKS = D // LANE
PEER = CAP * CHUNKS
CHIPS = 8
SHARD = 2 * G + 16
bf16, f32 = jnp.bfloat16, jnp.float32


def iota(shape, dimension):
    return lax.broadcasted_iota(jnp.int32, shape, dimension)


def choose(ids):
    hit = iota((EXPERTS, TOK), 0) == ids
    earlier = jnp.where(iota((TOK, TOK), 0) < iota((TOK, TOK), 1), 1.0, 0.0).astype(bf16)
    before = jnp.dot(jnp.where(hit, 1.0, 0.0).astype(bf16), earlier, preferred_element_type=f32)
    position = jnp.sum(jnp.where(hit, before, 0.0), axis=0, keepdims=True).astype(jnp.int32)
    slot = jnp.where(position < CAP, position * EXPERTS + ids, -1)
    return jnp.where(iota((SLOTS, TOK), 0) == slot, 1.0, 0.0).astype(bf16)


def to_slots(pick, rows):
    return jnp.dot(pick, rows, preferred_element_type=f32)


def to_tokens(pick, rows):
    return lax.dot_general(pick, rows, (((0,), (0,)), ((), ())), preferred_element_type=f32)


def pack(rows, wide, stride=PEER, first=0):
    for r in range(CAP):
        for k in range(CHUNKS):
            wide[pl.ds(first + r * CHUNKS + k, EXPERTS, stride=stride), :] = rows[
                r * EXPERTS : (r + 1) * EXPERTS, k * LANE : (k + 1) * LANE
            ]


def unpack(wide, dense, stride=PEER, first=0):
    for r in range(CAP):
        for k in range(CHUNKS):
            dense[r * EXPERTS : (r + 1) * EXPERTS, k * LANE : (k + 1) * LANE] = wide[
                pl.ds(first + r * CHUNKS + k, EXPERTS, stride=stride), :
            ].astype(dense.dtype)


def normalize(state):
    scale = jnp.sqrt(jnp.mean(state * state, axis=-1, keepdims=True) + epsilon)
    return state / scale, scale


def weights_of(gathered, wa, wb, column):
    for c in range(2 * CHIPS):
        at, to = c * SHARD, c * LANE
        wa[to : to + LANE, :LANE] = gathered[at : at + LANE, :]
        wa[to : to + LANE, LANE:] = gathered[at + LANE : at + 2 * LANE, :]
        wb[:, to : to + LANE] = gathered[at + G : at + 2 * G, :]
        column[:, to : to + LANE] = gathered[at + 2 * G : at + 2 * G + 1, :].astype(f32)


def forward(rows, wa, wb, column):
    before = jnp.dot(rows, wa[...], preferred_element_type=f32)
    positive = jnp.maximum(before, 0.0)
    hidden = (positive * positive).astype(bf16)
    expert_out = jnp.dot(hidden, wb[...], preferred_element_type=f32)
    logit = jnp.sum(rows.astype(f32) * column[...], axis=1, keepdims=True)
    gate = 1.0 / (1.0 + jnp.exp(-logit))
    return positive, hidden, expert_out, gate


def backward(upstream, wb, positive, gate):
    upper = upstream.astype(f32)
    grad_expert = (gate * upper).astype(bf16)
    grad_hidden = lax.dot_general(
        grad_expert, wb[...], (((1,), (1,)), ((), ())), preferred_element_type=f32
    )
    grad_pre = (grad_hidden * 2.0 * positive).astype(bf16)
    return upper, grad_expert, grad_pre


def dispatch_kernel(tokens, cotangent, ids, out, wide):
    unit, _ = normalize(tokens[...].astype(f32))
    pack(to_slots(choose(ids[0:1, :]), unit.astype(bf16)), wide, 2 * PEER, 0)
    pack(to_slots(choose(ids[1:2, :]), cotangent[...]), wide, 2 * PEER, PEER)
    out[...] = wide[...].astype(bf16)


def arrive_kernel(taken, rows, upstream, wide):
    wide[...] = taken[...].astype(f32)
    unpack(wide, rows, 2 * PEER, 0)
    unpack(wide, upstream, 2 * PEER, PEER)


def first_kernel(rows, gathered, out, positive_out, hidden_out, gate_out, wa, wb, column, wide):
    weights_of(gathered, wa, wb, column)
    positive, hidden, expert_out, gate = forward(rows[...], wa, wb, column)
    pack((gate * expert_out), wide)
    out[...] = wide[...].astype(bf16)
    positive_out[...] = positive
    hidden_out[...] = hidden
    gate_out[...] = jnp.broadcast_to(gate, (SLOTS, LANE))


def middle_kernel(tokens, ids, mixed, out, state_out, wide, dense):
    wide[...] = mixed[...].astype(f32)
    unpack(wide, dense)
    state = tokens[...].astype(f32) + to_tokens(choose(ids[0:1, :]), dense[...])
    state_out[...] = state
    unit, _ = normalize(state)
    pack(to_slots(choose(ids[1:2, :]), unit.astype(bf16)), wide)
    out[...] = wide[...].astype(bf16)


def second_kernel(
    taken, upstream, gathered, out, rows, expert_grad, pre_grad, hidden_out, wa, wb, column, wide
):
    wide[...] = taken[...].astype(f32)
    unpack(wide, rows)
    weights_of(gathered, wa, wb, column)
    positive, hidden, expert_out, gate = forward(rows[...], wa, wb, column)
    upper, grad_expert, grad_pre = backward(upstream[...], wb, positive, gate)
    grad_gate = jnp.sum(upper * expert_out, axis=1, keepdims=True)
    grad_logit = grad_gate * gate * (1.0 - gate)
    flowing = lax.dot_general(
        grad_pre, wa[...], (((1,), (1,)), ((), ())), preferred_element_type=f32
    )
    pack(flowing + grad_logit * column[...], wide)
    out[...] = wide[...].astype(bf16)
    expert_grad[...] = grad_expert
    pre_grad[...] = grad_pre
    hidden_out[...] = hidden


def return_kernel(cotangent, state, ids, taken, out, wide, dense):
    wide[...] = taken[...].astype(f32)
    unpack(wide, dense)
    unit, scale = normalize(state[...])
    grad = to_tokens(choose(ids[1:2, :]), dense[...])
    inner = jnp.mean(grad * unit, axis=-1, keepdims=True)
    upstream = cotangent[...].astype(f32) + (grad - unit * inner) / scale
    pack(to_slots(choose(ids[0:1, :]), upstream.astype(bf16)), wide)
    out[...] = wide[...].astype(bf16)


def weight_kernel(
    taken, gathered, rows_zero, positive, hidden_zero, gate,
    rows_one, expert_one, pre_one, hidden_one,
    mine, other, wide, dense, wb, part
):
    wide[...] = taken[...].astype(f32)
    unpack(wide, dense)
    for c in range(2 * CHIPS):
        wb[:, c * LANE : (c + 1) * LANE] = gathered[c * SHARD + G : c * SHARD + 2 * G, :]
    _, grad_expert, grad_pre = backward(dense[...], wb, positive[...], gate[:, :1])
    over_rows = (((0,), (0,)), ((), ()))
    part[:G, :] = lax.dot_general(
        grad_pre, rows_zero[...], over_rows, preferred_element_type=f32
    ) + lax.dot_general(pre_one[...], rows_one[...], over_rows, preferred_element_type=f32)
    part[G:, :] = lax.dot_general(
        hidden_zero[...], grad_expert, over_rows, preferred_element_type=f32
    ) + lax.dot_general(hidden_one[...], expert_one[...], over_rows, preferred_element_type=f32)
    core = lax.rem(lax.axis_index("ctx"), 2)
    for z in range(CHIPS):
        here = pl.multiple_of((2 * z + core) * LANE, LANE)
        there = pl.multiple_of((2 * z + 1 - core) * LANE, LANE)
        mine[z] = part[:, pl.ds(here, LANE)].astype(bf16)
        other[z] = part[:, pl.ds(there, LANE)].astype(bf16)


def pair_kernel(mine, other, out):
    out[...] = (mine[...].astype(f32) + other[...].astype(f32)).astype(bf16)


def total_kernel(parts, grad_in, grad_out):
    total = parts[0].astype(f32)
    for z in range(1, CHIPS):
        total = total + parts[z].astype(f32)
    grad_in[0] = total[:G, :].T
    grad_out[0] = total[G:, :]


def call(kernel, outs, scratch=(), **params):
    return pl.pallas_call(
        kernel,
        out_shape=[jax.ShapeDtypeStruct(s, t) for s, t in outs],
        scratch_shapes=[pltpu.VMEM(s, t) for s, t in scratch],
        compiler_params=pltpu.CompilerParams(vmem_limit_bytes=24 << 20, **params),
    )


PACKED = ((EXPERTS * PEER, LANE), bf16)
WIDE = ((EXPERTS * PEER, LANE), f32)
DENSE = ((SLOTS, D), bf16)
NARROW = ((SLOTS, G), bf16)
WEIGHTS = (((D, G), bf16), ((G, D), bf16), ((1, D), f32))


def over_exp(buffer):
    shaped = buffer.reshape(EXPERTS, -1, LANE)
    return lax.all_to_all(shaped, "exp", 0, 0, tiled=True).reshape(buffer.shape)


def on_device(tokens, cotangent, expert_ids, weight_in, weight_out, router):
    chips = lax.axis_size("ctx") // 2
    ids = expert_ids[:, :, 0]
    shard = jnp.concatenate(
        [
            weight_in[0, :, :LANE],
            weight_in[0, :, LANE:],
            weight_out[0],
            jnp.pad(router.reshape(1, LANE), ((0, 15), (0, 0))),
        ],
        axis=0,
    )
    gathered = lax.all_gather(shard, "ctx", axis=0, tiled=True)
    wide_two = ((2 * EXPERTS * PEER, LANE), f32)
    (leaving,) = call(dispatch_kernel, [((2 * EXPERTS * PEER, LANE), bf16)], [wide_two])(
        tokens, cotangent, ids
    )
    rows_zero, upstream_one = call(arrive_kernel, [DENSE, DENSE], [wide_two])(over_exp(leaving))
    mixed, positive, hidden_zero, gate = call(
        first_kernel,
        [PACKED, ((SLOTS, G), f32), NARROW, ((SLOTS, LANE), f32)],
        [*WEIGHTS, WIDE],
    )(rows_zero, gathered)
    leaving, state_one = call(middle_kernel, [PACKED, ((TOK, D), f32)], [WIDE, DENSE])(
        tokens, ids, over_exp(mixed)
    )
    leaving, rows_one, expert_one, pre_one, hidden_one = call(
        second_kernel, [PACKED, DENSE, DENSE, NARROW, NARROW], [*WEIGHTS, WIDE]
    )(over_exp(leaving), upstream_one, gathered)
    (leaving,) = call(return_kernel, [PACKED], [WIDE, DENSE])(
        cotangent, state_one, ids, over_exp(leaving)
    )
    block = ((CHIPS, 2 * G, LANE), bf16)
    mine, other = call(
        weight_kernel, [block, block], [WIDE, DENSE, WEIGHTS[1], ((2 * G, D), f32)]
    )(
        over_exp(leaving), gathered, rows_zero, positive, hidden_zero, gate,
        rows_one, expert_one, pre_one, hidden_one,
    )
    across = [(2 * z + c, 2 * z + 1 - c) for z in range(chips) for c in range(2)]
    (pair,) = call(pair_kernel, [block])(mine, lax.ppermute(other, "ctx", across))
    columns = [[2 * z + c for z in range(chips)] for c in range(2)]
    parts = lax.all_to_all(pair, "ctx", 0, 0, tiled=True, axis_index_groups=columns)
    grad_in, grad_out = call(total_kernel, [((1, LANE, G), f32), ((1, G, LANE), f32)])(parts)
    return (grad_in, grad_out)


def solution(mesh):
    placed = (
        P(("ctx", "exp"), None),
        P(("ctx", "exp"), None),
        P(None, ("ctx", "exp"), None),
        P("exp", "ctx", None),
        P("exp", None, "ctx"),
        P("ctx", "exp"),
    )
    return jax.shard_map(
        on_device,
        mesh=mesh,
        in_specs=placed,
        out_specs=(P("exp", "ctx", None), P("exp", None, "ctx")),
        check_vma=False,
    )
```

time: 371 us -> 194 us (0.52)
  waiting for transfers between devices: 226 us -> 15.3 us
  blocking collectives: 23.8 us -> 139 us
  starting transfers between devices: 44.4 us -> 6.16 us
  local copies, waits for them, and re-layouts: 34.4 us -> 5.16 us
  matrix products: 14.1 us -> 0 us
  Pallas kernels: 0 us -> 11.8 us
  other arithmetic: 10.9 us -> 1.51 us
    all_to_all x0 -> x6, blocking collectives: none -> 139 us  [the longest x5 108 us: over_exp(): return lax.all_to_all(shaped, 'exp', 0, 0, tiled=True).reshape(buffer.shape)]
    all_to_all x6 -> x0, waiting for transfers between devices: 66.6 us -> none  [the longest x2 28.4 us: send_source(): return lax.all_to_all(rows, 'exp', split_axis=0, concat_axis=0, tiled=True)]
    reduce_scatter x1 -> x0, waiting for transfers between devices: 59.9 us -> none  [on_device(): lax.psum_scatter(part_in[None].astype(jnp.bfloat16), 'ctx', scatter_dimen...]
    unnamed x5 -> x1, waiting for transfers between devices: 52.6 us -> 0.02 us
    all_to_all x6 -> x0, starting transfers between devices: 44.2 us -> none  [the longest x2 17 us: send_owner(): return lax.all_to_all(rows, 'exp', split_axis=0, concat_axis=0, tiled=True)]
    all_gather x2 -> x1, waiting for transfers between devices: 46.5 us -> 13 us  [on_device(): gathered = lax.all_gather(shard, 'ctx', axis=0, tiled=True)]
    all_gather x1 -> x0, blocking collectives: 23.8 us -> none  [on_device(): lax.all_gather(router, 'ctx', axis=0, tiled=True)]
    dot_general x11 -> x0, matrix products: 14.1 us -> none  [the longest x2 4.22 us: expert_forward(): before_relu = jnp.dot(rows, weight_a, preferred_element_type=jnp.float32)]
  transfers between devices with their start and end apart: 10 -> 2, of which waited for: 9 -> 2; matrix products, arithmetic and copies ran while one was open for 6% -> 0% of each run, Pallas kernels for 0% -> 1%
where the time goes in v1:
time: 194 us; the launch traced here: 193 us
  blocking collectives  139 us (72%)
  waiting for transfers between devices  15.3 us (8%)
  between operations  14.1 us (7%)
  Pallas kernels  11.8 us (6%)
  starting transfers between devices  6.16 us (3%)
  local copies, waits for them, and re-layouts  5.16 us (3%)
    all_to_all x5, blocking collectives, over_exp(): return lax.all_to_all(shaped, 'exp', 0, 0, tiled=True).reshape(buffer.shape)  108 us
    all_to_all x1, blocking collectives, on_device(): lax.all_to_all(pair, 'ctx', 0, 0, tiled=True, axis_index_groups=columns)  31.6 us
    all_gather x1, waiting for transfers between devices, on_device(): gathered = lax.all_gather(shard, 'ctx', axis=0, tiled=True)  13 us
    ppermute x1, starting transfers between devices, on_device(): pair, = call(pair_kernel, [block])(mine, lax.ppermute(other, 'ctx', across))  6.12 us
    unnamed x16, local copies, waits for them, and re-layouts  4.38 us
  transfers between devices with their start and end apart: 2, of which 2 were waited for; matrix products, arithmetic and copies ran while one was open for 0% of the time, Pallas kernels for 1%

profile of v1, /device:TPU:1, one launch (start us, length us, event | category | flops | bytes accessed | tf_op | source)
XLA Modules:
  0.0 193.4 jit_solution(17648557497164554448)
XLA Ops:
  7.2 0.0 all-gather.2.cloned.1.call-start
  7.2 0.8 slice_bitcast_fusion.1
  8.0 1.5 fusion.1
  9.5 0.0 all-gather.2.cloned.1.call-update
  9.5 0.0 copy-start.2
  9.5 1.0 copy-done.2
  10.6 1.0 copy-done.4
  11.6 0.7 copy-done.6
  12.3 1.5 shard_map.77
  13.8 31.4 %all_to_all.30 = bf16[32,96,128]{2,1,0:T(8,128)(2,1)S(1)} all-to-all(bf16[32,96,128]{2,1,0:T(8,128)(2,1)S(1)} %bitcast.18), channel_id=1, replica_groups=mesh['ctx'=16,'exp'=32] {'exp'}, dimensions={0} | all-to-all | bytes 1572864 | tf_op jit(solution)/shard_map/all_to_all | solution.py:211
  45.1 1.0 shard_map.78
  46.1 13.0 %all-gather.2.cloned.1.call-done.gathered = bf16[8448,128]{1,0:T(8,128)(2,1)} async-done(((bf16[528,128]{1,0:T(8,128)(2,1)}), bf16[8448,128]{1,0:T(8,128)(2,1)}) %all-gather.2.cloned.1.call-update) | async-done | bytes 2162704 | tf_op jit(solution)/shard_map/all_gather | solution.py:226
  59.1 1.6 copy-done
  60.7 0.9 shard_map.79
  61.7 23.2 %all_to_all.31 = bf16[32,48,128]{2,1,0:T(8,128)(2,1)S(1)} all-to-all(bf16[32,48,128]{2,1,0:T(8,128)(2,1)S(1)} %bitcast.25), channel_id=1, replica_groups=mesh['ctx'=16,'exp'=32] {'exp'}, dimensions={0} | all-to-all | bytes 786432 | tf_op jit(solution)/shard_map/all_to_all | solution.py:211
  84.8 0.0 copy-done.3
  84.9 0.0 copy-done.7
  84.9 1.2 shard_map.80
  86.0 0.0 copy-start.5
  86.0 17.5 %all_to_all.32 = bf16[32,48,128]{2,1,0:T(8,128)(2,1)S(1)} all-to-all(bf16[32,48,128]{2,1,0:T(8,128)(2,1)S(1)} %bitcast.26), channel_id=1, replica_groups=mesh['ctx'=16,'exp'=32] {'exp'}, dimensions={0} | all-to-all | bytes 786432 | tf_op jit(solution)/shard_map/all_to_all | solution.py:211
  103.6 0.0 copy-done.1
  103.6 2.1 %shard_map.81 = (bf16[1536,128]{1,0:T(8,128)(2,1)S(1)}, bf16[96,2048]{1,0:T(8,128)(2,1)S(1)}, bf16[96,2048]{1,0:T(8,128)(2,1)S(1)}, bf16[96,256]{1,0:T(8,128)(2,1)S(1)}, bf16[96,256]{1,0:T(8,128)(2,1)S(1)}) custom-call(bf16[1536,128]{1,0:T(8,128)(2,1)S(1)} %bitcast.20, bf16[96,2048]{1,0:T(8,128)(2,1)S(1)} %get-tuple-element.21.upstream, ...), custom_call_target="tpu_custom_call" | custom-call | tf_op jit(solution)/shard_map/pallas_call | solution.py:240
  105.6 18.1 %all_to_all.33 = bf16[32,48,128]{2,1,0:T(8,128)(2,1)S(1)} all-to-all(bf16[32,48,128]{2,1,0:T(8,128)(2,1)S(1)} %bitcast.24), channel_id=1, replica_groups=mesh['ctx'=16,'exp'=32] {'exp'}, dimensions={0} | all-to-all | bytes 786432 | tf_op jit(solution)/shard_map/all_to_all | solution.py:211
  123.7 0.0 copy-done.5
  123.7 1.2 shard_map.82
  125.0 17.6 %all_to_all.34 = bf16[32,48,128]{2,1,0:T(8,128)(2,1)S(1)} all-to-all(bf16[32,48,128]{2,1,0:T(8,128)(2,1)S(1)} %bitcast.22), channel_id=1, replica_groups=mesh['ctx'=16,'exp'=32] {'exp'}, dimensions={0} | all-to-all | bytes 786432 | tf_op jit(solution)/shard_map/all_to_all | solution.py:211
  142.6 2.9 %shard_map.83 = (bf16[8,512,128]{2,1,0:T(8,128)(2,1)S(1)}, bf16[8,512,128]{2,1,0:T(8,128)(2,1)S(1)}) custom-call(bf16[1536,128]{1,0:T(8,128)(2,1)S(1)} %bitcast.23, bf16[8448,128]{1,0:T(8,128)(2,1)S(1)} %copy-done.1, bf16[96,2048]{1,0:T(8,128)(2,1)S(1)} %get-tuple-element.17.rows.rows_zero, f32[96,256]{1,0:T(8,128)S(1)} %get-tuple-element.23.positive, ...), custom_call_target="tpu_custom_call" | custom-call | tf_op jit(solution)/shard_map/pallas_call | solution.py:247
  145.5 6.1 %collective-permute-start = (bf16[8,512,128]{2,1,0:T(8,128)(2,1)S(1)}, bf16[8,512,128]{2,1,0:T(8,128)(2,1)S(1)}, u32[]{:S(2)}, u32[]{:S(2)}) collective-permute-start(bf16[8,512,128]{2,1,0:T(8,128)(2,1)S(1)} %get-tuple-element.31), channel_id=1, source_target_pairs={{0,32},{32,0},{64,96},{96,64},{128,160},{160,128},{192,224},{224,1... | collective-permute-start | bytes 3145736 | tf_op jit(solution)/shard_map/ppermute | solution.py:254
  151.6 2.3 %collective-permute-done.other = bf16[8,512,128]{2,1,0:T(8,128)(2,1)S(1)} collective-permute-done((bf16[8,512,128]{2,1,0:T(8,128)(2,1)S(1)}, bf16[8,512,128]{2,1,0:T(8,128)(2,1)S(1)}, u32[]{:S(2)}, u32[]{:S(2)}) %collective-permute-start) | collective-permute-done | bytes 1048608 | tf_op jit(solution)/shard_map/ppermute | solution.py:254
  153.9 0.2 shard_map.84
  154.1 31.6 %all_to_all.35.parts = bf16[8,512,128]{2,1,0:T(8,128)(2,1)S(1)} all-to-all(bf16[8,512,128]{2,1,0:T(8,128)(2,1)S(1)} %shard_map.84), channel_id=1, replica_groups={{0,64,128,192,256,320,384,448},{32,96,160,224,288,352,416,480},{1,65,12..., dimensions={0} | all-to-all | bytes 2097152 | tf_op jit(solution)/shard_map/all_to_all | solution.py:256
  185.7 0.8 shard_map.85
  (6 shorter events, 0.0 us)
Async XLA Ops:
  7.2 52.0 %all-gather.2.cloned.1.call-start = ((), (), s32[]{:S(2)}) async-start(), calls=%async_computation.6 | async-start | bytes 2297856 | tf_op jit(solution)/shard_map/all_gather | solution.py:226
  9.5 1.0 copy-start.2
  10.6 1.0 copy-start.4
  11.6 0.7 copy-start.6
  45.1 39.7 %copy-start.3 = (bf16[128,2048]{1,0:T(8,128)(2,1)S(1)}, bf16[128,2048]{1,0:T(8,128)(2,1)}, u32[]{:S(2)}) copy-start(bf16[128,2048]{1,0:T(8,128)(2,1)} %tokens.3) | copy-start | bytes 1572868
  45.1 39.7 %copy-start.7 = (s32[2,128,1]{1,2,0:T(1,128)S(1)}, s32[2,128,1]{1,2,0:T(1,128)}, u32[]{:S(2)}) copy-start(s32[2,128,1]{1,2,0:T(1,128)} %param.8) | copy-start | bytes 3076
  59.1 1.6 copy-start
  60.7 42.8 %copy-start.1 = (bf16[8448,128]{1,0:T(8,128)(2,1)S(1)}, bf16[8448,128]{1,0:T(8,128)(2,1)}, u32[]{:S(2)}) copy-start(bf16[8448,128]{1,0:T(8,128)(2,1)} %all-gather.2.cloned.1.call-done.gathered) | copy-start | bytes 6488068
  86.0 37.7 %copy-start.5 = (bf16[128,2048]{1,0:T(8,128)(2,1)S(1)}, bf16[128,2048]{1,0:T(8,128)(2,1)}, u32[]{:S(2)}) copy-start(bf16[128,2048]{1,0:T(8,128)(2,1)} %cotangent.3) | copy-start | bytes 1572868
  145.5 8.4 %collective-permute-start = (bf16[8,512,128]{2,1,0:T(8,128)(2,1)S(1)}, bf16[8,512,128]{2,1,0:T(8,128)(2,1)S(1)}, u32[]{:S(2)}, u32[]{:S(2)}) collective-permute-start(bf16[8,512,128]{2,1,0:T(8,128)(2,1)S(1)} %get-tuple-element.31), channel_id=1, source_target_pairs={{0,32},{32,0},{64,96},{96,64},{128,160},{160,128},{192,224},{224,1... | collective-permute-start | bytes 3145736 | tf_op jit(solution)/shard_map/ppermute | solution.py:254
Sparse Core Ops, SparseCore 0:
  10.1 48.9 all-gather.1

commit v2 on v1

--- a/solution.py
+++ b/solution.py
@@ -60,13 +60,21 @@
     return state / scale, scale
 
 
-def weights_of(gathered, wa, wb, column):
-    for c in range(2 * CHIPS):
-        at, to = c * SHARD, c * LANE
-        wa[to : to + LANE, :LANE] = gathered[at : at + LANE, :]
-        wa[to : to + LANE, LANE:] = gathered[at + LANE : at + 2 * LANE, :]
-        wb[:, to : to + LANE] = gathered[at + G : at + 2 * G, :]
-        column[:, to : to + LANE] = gathered[at + 2 * G : at + 2 * G + 1, :].astype(f32)
+def share_kernel(weight_in, weight_out, router, out):
+    out[:LANE, :] = weight_in[0, :, :LANE]
+    out[LANE:G, :] = weight_in[0, :, LANE:]
+    out[G : 2 * G, :] = weight_out[0]
+    out[2 * G :, :] = jnp.broadcast_to(router[...], (SHARD - 2 * G, LANE))
+
+
+def place(block, first, chip, wa, wb, column):
+    for core in range(2):
+        at = first + core * SHARD
+        to = pl.ds(pl.multiple_of((2 * chip + core) * LANE, LANE), LANE)
+        wa[to, :LANE] = block[at : at + LANE, :]
+        wa[to, LANE:] = block[at + LANE : at + G, :]
+        wb[:, to] = block[at + G : at + 2 * G, :]
+        column[:, to] = block[at + 2 * G : at + 2 * G + 1, :].astype(f32)
 
 
 def forward(rows, wa, wb, column):
@@ -102,13 +110,22 @@
     unpack(wide, upstream, 2 * PEER, PEER)
 
 
-def first_kernel(rows, gathered, out, positive_out, hidden_out, gate_out, wa, wb, column, wide):
-    weights_of(gathered, wa, wb, column)
+def first_kernel(
+    rows, own, pair_1, pair_2, pair_3, far,
+    out, positive_out, kept, gate_out, wa, wb, column, wide
+):
+    chip = lax.div(lax.axis_index("ctx"), 2)
+    place(own, 0, chip, wa, wb, column)
+    for hop, pair in enumerate((pair_1, pair_2, pair_3), 1):
+        place(pair, 0, lax.rem(chip + CHIPS - hop, CHIPS), wa, wb, column)
+        place(pair, 2 * SHARD, lax.rem(chip + hop, CHIPS), wa, wb, column)
+    place(far, 0, lax.rem(chip + CHIPS // 2, CHIPS), wa, wb, column)
     positive, hidden, expert_out, gate = forward(rows[...], wa, wb, column)
     pack((gate * expert_out), wide)
     out[...] = wide[...].astype(bf16)
     positive_out[...] = positive
-    hidden_out[...] = hidden
+    kept[:, :D] = rows[...]
+    kept[:, D:] = hidden
     gate_out[...] = jnp.broadcast_to(gate, (SLOTS, LANE))
 
 
@@ -123,12 +140,11 @@
 
 
 def second_kernel(
-    taken, upstream, gathered, out, rows, expert_grad, pre_grad, hidden_out, wa, wb, column, wide
+    taken, upstream, wa, wb, column, out, kept, grads, wide, dense
 ):
     wide[...] = taken[...].astype(f32)
-    unpack(wide, rows)
-    weights_of(gathered, wa, wb, column)
-    positive, hidden, expert_out, gate = forward(rows[...], wa, wb, column)
+    unpack(wide, dense)
+    positive, hidden, expert_out, gate = forward(dense[...], wa, wb, column)
     upper, grad_expert, grad_pre = backward(upstream[...], wb, positive, gate)
     grad_gate = jnp.sum(upper * expert_out, axis=1, keepdims=True)
     grad_logit = grad_gate * gate * (1.0 - gate)
@@ -137,9 +153,10 @@
     )
     pack(flowing + grad_logit * column[...], wide)
     out[...] = wide[...].astype(bf16)
-    expert_grad[...] = grad_expert
-    pre_grad[...] = grad_pre
-    hidden_out[...] = hidden
+    kept[:, :D] = dense[...]
+    kept[:, D:] = hidden
+    grads[:, :D] = grad_expert
+    grads[:, D:] = grad_pre
 
 
 def return_kernel(cotangent, state, ids, taken, out, wide, dense):
@@ -153,33 +170,35 @@
     out[...] = wide[...].astype(bf16)
 
 
-def weight_kernel(
-    taken, gathered, rows_zero, positive, hidden_zero, gate,
-    rows_one, expert_one, pre_one, hidden_one,
-    mine, other, wide, dense, wb, part
-):
+def over_rows(left, right):
+    return lax.dot_general(left, right, (((0,), (0,)), ((), ())), preferred_element_type=f32)
+
+
+def first_grad_kernel(taken, wb, positive, gate, out, wide, dense):
     wide[...] = taken[...].astype(f32)
     unpack(wide, dense)
-    for c in range(2 * CHIPS):
-        wb[:, c * LANE : (c + 1) * LANE] = gathered[c * SHARD + G : c * SHARD + 2 * G, :]
     _, grad_expert, grad_pre = backward(dense[...], wb, positive[...], gate[:, :1])
-    over_rows = (((0,), (0,)), ((), ()))
-    part[:G, :] = lax.dot_general(
-        grad_pre, rows_zero[...], over_rows, preferred_element_type=f32
-    ) + lax.dot_general(pre_one[...], rows_one[...], over_rows, preferred_element_type=f32)
-    part[G:, :] = lax.dot_general(
-        hidden_zero[...], grad_expert, over_rows, preferred_element_type=f32
-    ) + lax.dot_general(hidden_one[...], expert_one[...], over_rows, preferred_element_type=f32)
+    out[:, :D] = grad_expert
+    out[:, D:] = grad_pre
+
+
+def weight_kernel(grads_zero, kept_zero, grads_one, kept_one, out, rows, grads, parts):
     core = lax.rem(lax.axis_index("ctx"), 2)
+    parts_in = ((grads_zero, kept_zero), (grads_one, kept_one))
+    for at, (grad, kept) in zip((0, 2 * SLOTS), parts_in):
+        to = slice(at, at + 2 * SLOTS)
+        for z in range(CHIPS):
+            own = pl.ds(pl.multiple_of((2 * z + core) * LANE, LANE), LANE)
+            rows[to, z * LANE : (z + 1) * LANE] = kept[:, own]
+            grads[to, z * LANE : (z + 1) * LANE] = grad[:, own]
+        parts[to, :G] = grad[:, D:]
+        parts[to, G:] = kept[:, D:]
+    part_in = over_rows(parts[:, :G], rows[...])
+    part_out = over_rows(parts[:, G:], grads[...])
     for z in range(CHIPS):
-        here = pl.multiple_of((2 * z + core) * LANE, LANE)
-        there = pl.multiple_of((2 * z + 1 - core) * LANE, LANE)
-        mine[z] = part[:, pl.ds(here, LANE)].astype(bf16)
-        other[z] = part[:, pl.ds(there, LANE)].astype(bf16)
-
-
-def pair_kernel(mine, other, out):
-    out[...] = (mine[...].astype(f32) + other[...].astype(f32)).astype(bf16)
+        at = slice(z * LANE, (z + 1) * LANE)
+        out[z, :G, :] = part_in[:, at].astype(bf16)
+        out[z, G:, :] = part_out[:, at].astype(bf16)
 
 
 def total_kernel(parts, grad_in, grad_out):
@@ -190,19 +209,19 @@
     grad_out[0] = total[G:, :]
 
 
-def call(kernel, outs, scratch=(), **params):
+def call(kernel, outs, scratch=(), room=24):
     return pl.pallas_call(
         kernel,
         out_shape=[jax.ShapeDtypeStruct(s, t) for s, t in outs],
         scratch_shapes=[pltpu.VMEM(s, t) for s, t in scratch],
-        compiler_params=pltpu.CompilerParams(vmem_limit_bytes=24 << 20, **params),
+        compiler_params=pltpu.CompilerParams(vmem_limit_bytes=room << 20),
     )
 
 
 PACKED = ((EXPERTS * PEER, LANE), bf16)
 WIDE = ((EXPERTS * PEER, LANE), f32)
 DENSE = ((SLOTS, D), bf16)
-NARROW = ((SLOTS, G), bf16)
+KEPT = ((SLOTS, D + G), bf16)
 WEIGHTS = (((D, G), bf16), ((G, D), bf16), ((1, D), f32))
 
 
@@ -214,44 +233,53 @@
 def on_device(tokens, cotangent, expert_ids, weight_in, weight_out, router):
     chips = lax.axis_size("ctx") // 2
     ids = expert_ids[:, :, 0]
-    shard = jnp.concatenate(
-        [
-            weight_in[0, :, :LANE],
-            weight_in[0, :, LANE:],
-            weight_out[0],
-            jnp.pad(router.reshape(1, LANE), ((0, 15), (0, 0))),
-        ],
-        axis=0,
-    )
-    gathered = lax.all_gather(shard, "ctx", axis=0, tiled=True)
+    cores = [[2 * z, 2 * z + 1] for z in range(chips)]
+
+    def both_cores(value):
+        return lax.all_gather(value, "ctx", axis=0, tiled=True, axis_index_groups=cores)
+
+    around = [(2 * z, 2 * ((z + 1) % chips)) for z in range(chips)]
+    around += [(2 * z + 1, 2 * ((z - 1) % chips) + 1) for z in range(chips)]
+    (share,) = call(share_kernel, [((SHARD, LANE), bf16)], room=60)(
+        weight_in, weight_out, router.reshape(1, LANE)
+    )
+    own = both_cores(share)
+    passing, pairs = own, []
+    for hop in range(chips // 2):
+        if hop > 1:
+            passing, pairs[hop - 2] = lax.optimization_barrier((passing, both_cores(pairs[hop - 2])))
+        passing = lax.ppermute(passing, "ctx", around)
+        pairs.append(passing)
+        if hop == 0:
+            first_hop = passing
+    pairs[2] = both_cores(pairs[2])
     wide_two = ((2 * EXPERTS * PEER, LANE), f32)
-    (leaving,) = call(dispatch_kernel, [((2 * EXPERTS * PEER, LANE), bf16)], [wide_two])(
+    (leaving,) = call(dispatch_kernel, [((2 * EXPERTS * PEER, LANE), bf16)], [wide_two], room=60)(
         tokens, cotangent, ids
     )
+    leaving, _ = lax.optimization_barrier((leaving, first_hop))
     rows_zero, upstream_one = call(arrive_kernel, [DENSE, DENSE], [wide_two])(over_exp(leaving))
-    mixed, positive, hidden_zero, gate = call(
+    mixed, positive, kept_zero, gate, wa, wb, column = call(
         first_kernel,
-        [PACKED, ((SLOTS, G), f32), NARROW, ((SLOTS, LANE), f32)],
-        [*WEIGHTS, WIDE],
-    )(rows_zero, gathered)
+        [PACKED, ((SLOTS, G), f32), KEPT, ((SLOTS, LANE), f32), *WEIGHTS],
+        [WIDE],
+    )(rows_zero, own, *pairs)
     leaving, state_one = call(middle_kernel, [PACKED, ((TOK, D), f32)], [WIDE, DENSE])(
         tokens, ids, over_exp(mixed)
     )
-    leaving, rows_one, expert_one, pre_one, hidden_one = call(
-        second_kernel, [PACKED, DENSE, DENSE, NARROW, NARROW], [*WEIGHTS, WIDE]
-    )(over_exp(leaving), upstream_one, gathered)
+    leaving, kept_one, grads_one = call(second_kernel, [PACKED, KEPT, KEPT], [WIDE, DENSE])(
+        over_exp(leaving), upstream_one, wa, wb, column
+    )
     (leaving,) = call(return_kernel, [PACKED], [WIDE, DENSE])(
         cotangent, state_one, ids, over_exp(leaving)
     )
-    block = ((CHIPS, 2 * G, LANE), bf16)
-    mine, other = call(
-        weight_kernel, [block, block], [WIDE, DENSE, WEIGHTS[1], ((2 * G, D), f32)]
-    )(
-        over_exp(leaving), gathered, rows_zero, positive, hidden_zero, gate,
-        rows_one, expert_one, pre_one, hidden_one,
-    )
-    across = [(2 * z + c, 2 * z + 1 - c) for z in range(chips) for c in range(2)]
-    (pair,) = call(pair_kernel, [block])(mine, lax.ppermute(other, "ctx", across))
+    (grads_zero,) = call(first_grad_kernel, [KEPT], [WIDE, DENSE])(
+        over_exp(leaving), wb, positive, gate
+    )
+    half = ((4 * SLOTS, D // 2), bf16)
+    (pair,) = call(
+        weight_kernel, [((CHIPS, 2 * G, LANE), bf16)], [half, half, ((4 * SLOTS, 2 * G), bf16)]
+    )(both_cores(grads_zero), both_cores(kept_zero), both_cores(grads_one), both_cores(kept_one))
     columns = [[2 * z + c for z in range(chips)] for c in range(2)]
     parts = lax.all_to_all(pair, "ctx", 0, 0, tiled=True, axis_index_groups=columns)
     grad_in, grad_out = call(total_kernel, [((1, LANE, G), f32), ((1, G, LANE), f32)])(parts)

time: 194 us -> 181 us (0.933)
  starting transfers between devices: 6.16 us -> 34.5 us
  between operations: 14.1 us -> 0.82 us
  waiting for transfers between devices: 15.3 us -> 2.39 us
  blocking collectives: 139 us -> 127 us
  local copies, waits for them, and re-layouts: 5.16 us -> 0.72 us
  Pallas kernels: 11.8 us -> 14.6 us
    all_to_all x5 -> x3, blocking collectives: 108 us -> 51.4 us  [over_exp(): return lax.all_to_all(shaped, 'exp', 0, 0, tiled=True).reshape(buffer.shape)]
    all_gather x0 -> x8, blocking collectives: none -> 39.6 us  [both_cores(): lax.all_gather(value, 'ctx', axis=0, tiled=True, axis_index_groups=cores)]
    ppermute x1 -> x4, starting transfers between devices: 6.12 us -> 20.8 us  [on_device(): passing = lax.ppermute(passing, 'ctx', around)]
    all_to_all x0 -> x2, starting transfers between devices: none -> 13.7 us  [over_exp(): return lax.all_to_all(shaped, 'exp', 0, 0, tiled=True).reshape(buffer.shape)]
    all_gather x1 -> x0, waiting for transfers between devices: 13 us -> none  [on_device(): gathered = lax.all_gather(shard, 'ctx', axis=0, tiled=True)]
    all_to_all x1, blocking collectives: 31.6 us -> 35.9 us  [on_device(): lax.all_to_all(pair, 'ctx', 0, 0, tiled=True, axis_index_groups=columns)]
    unnamed x16 -> x20, local copies, waits for them, and re-layouts: 4.38 us -> 0.72 us
    pallas_call x5 -> x6, Pallas kernels: 7.55 us -> 9.58 us  [the longest x1 3.54 us: on_device(): call(dispatch_kernel, [((2 * EXPERTS * PEER, LANE), bf16)], [wide_two], r...]
  transfers between devices with their start and end apart: 2 -> 6, of which waited for: 2 -> 2; matrix products, arithmetic and copies ran while one was open for 0% -> 0% of each run, Pallas kernels for 1% -> 3%
where the time goes in v2:
time: 181 us; the launch traced here: 180 us
  blocking collectives  127 us (70%)
  starting transfers between devices  34.5 us (19%)
  Pallas kernels  14.6 us (8%)
  waiting for transfers between devices  2.39 us (1%)
    all_to_all x3, blocking collectives, over_exp(): return lax.all_to_all(shaped, 'exp', 0, 0, tiled=True).reshape(buffer.shape)  51.4 us
    all_gather x8, blocking collectives, both_cores(): lax.all_gather(value, 'ctx', axis=0, tiled=True, axis_index_groups=cores)  39.6 us
    all_to_all x1, blocking collectives, on_device(): lax.all_to_all(pair, 'ctx', 0, 0, tiled=True, axis_index_groups=columns)  35.9 us
    ppermute x4, starting transfers between devices, on_device(): passing = lax.ppermute(passing, 'ctx', around)  20.8 us
    all_to_all x2, starting transfers between devices, over_exp(): return lax.all_to_all(shaped, 'exp', 0, 0, tiled=True).reshape(buffer.shape)  13.7 us
  transfers between devices with their start and end apart: 6, of which 2 were waited for; matrix products, arithmetic and copies ran while one was open for 0% of the time, Pallas kernels for 3%

profile of v2, /device:TPU:1, one launch (start us, length us, event | category | flops | bytes accessed | tf_op | source)
XLA Modules:
  0.0 179.9 jit_solution(7607034824739412748)
XLA Ops:
  0.6 1.6 shard_map.78
  2.2 8.7 %all_gather.24.own = bf16[1056,128]{1,0:T(8,128)(2,1)S(1)} all-gather(bf16[528,128]{1,0:T(8,128)(2,1)} %shard_map.78), channel_id=1, replica_groups={{0,32},{64,96},{128,160},{192,224},{256,288},{320,352},{384,416},{448,4..., dimensions={0}, use_global_device_ids=true | all-gather | bytes 405504 | tf_op jit(solution)/shard_map/all_gather | solution.py:239
  10.9 5.3 %collective-permute-start = (bf16[1056,128]{1,0:T(8,128)(2,1)S(1)}, bf16[1056,128]{1,0:T(8,128)(2,1)S(1)}, u32[]{:S(2)}, u32[]{:S(2)}) collective-permute-start(bf16[1056,128]{1,0:T(8,128)(2,1)S(1)} %all_gather.24.own), channel_id=1, source_target_pairs={{0,64},{64,128},{128,192},{192,256},{256,320},{320,384},{384,448},... | collective-permute-start | bytes 811016 | tf_op jit(solution)/shard_map/ppermute | solution.py:251
  16.2 3.5 %shard_map.77 = bf16[3072,128]{1,0:T(8,128)(2,1)} custom-call(bf16[128,2048]{1,0:T(8,128)(2,1)} %tokens.3, bf16[128,2048]{1,0:T(8,128)(2,1)} %cotangent.3, s32[2,128]{1,0:T(2,128)} %bitcast.20), custom_call_target="tpu_custom_call" | custom-call | tf_op jit(solution)/shard_map/pallas_call | solution.py:257
  19.7 9.7 %all-to-all-start = ((bf16[32,96,128]{2,1,0:T(8,128)(2,1)}), bf16[32,96,128]{2,1,0:T(8,128)(2,1)S(1)}, u32[]{:S(2)}, u32[]{:S(2)}) async-start(bf16[32,96,128]{2,1,0:T(8,128)(2,1)} %bitcast.23), calls=%async_computation | async-start | bytes 1572864 | tf_op jit(solution)/shard_map/all_to_all | solution.py:230
  29.4 4.9 %collective-permute-start.1 = (bf16[1056,128]{1,0:T(8,128)(2,1)S(1)}, bf16[1056,128]{1,0:T(8,128)(2,1)S(1)}, u32[]{:S(2)}, u32[]{:S(2)}) collective-permute-start(bf16[1056,128]{1,0:T(8,128)(2,1)S(1)} %collective-permute-done), channel_id=1, source_target_pairs={{0,64},{64,128},{128,192},{192,256},{256,320},{320,384},{384,448},... | collective-permute-start | bytes 811016 | tf_op jit(solution)/shard_map/ppermute | solution.py:251
  34.3 2.2 %all_gather.25.pair_1 = bf16[2112,128]{1,0:T(8,128)(2,1)S(1)} all-gather(bf16[1056,128]{1,0:T(8,128)(2,1)S(1)} %collective-permute-done), channel_id=1, replica_groups={{0,32},{64,96},{128,160},{192,224},{256,288},{320,352},{384,416},{448,4..., dimensions={0}, use_global_device_ids=true | all-gather | bytes 811008 | tf_op jit(solution)/shard_map/all_gather | solution.py:239
  36.5 1.2 collective-permute-done.1
  37.7 5.3 %collective-permute-start.2 = (bf16[1056,128]{1,0:T(8,128)(2,1)S(1)}, bf16[1056,128]{1,0:T(8,128)(2,1)S(1)}, u32[]{:S(2)}, u32[]{:S(2)}) collective-permute-start(bf16[1056,128]{1,0:T(8,128)(2,1)S(1)} %collective-permute-done.1), channel_id=1, source_target_pairs={{0,64},{64,128},{128,192},{192,256},{256,320},{320,384},{384,448},... | collective-permute-start | bytes 811016 | tf_op jit(solution)/shard_map/ppermute | solution.py:251
  43.0 2.2 %all_gather.26.pair_2 = bf16[2112,128]{1,0:T(8,128)(2,1)S(1)} all-gather(bf16[1056,128]{1,0:T(8,128)(2,1)S(1)} %collective-permute-done.1), channel_id=1, replica_groups={{0,32},{64,96},{128,160},{192,224},{256,288},{320,352},{384,416},{448,4..., dimensions={0}, use_global_device_ids=true | all-gather | bytes 811008 | tf_op jit(solution)/shard_map/all_gather | solution.py:239
  45.2 1.2 collective-permute-done.2
  46.4 5.3 %collective-permute-start.3 = (bf16[1056,128]{1,0:T(8,128)(2,1)S(1)}, bf16[1056,128]{1,0:T(8,128)(2,1)S(1)}, u32[]{:S(2)}, u32[]{:S(2)}) collective-permute-start(bf16[1056,128]{1,0:T(8,128)(2,1)S(1)} %collective-permute-done.2), channel_id=1, source_target_pairs={{0,64},{64,128},{128,192},{192,256},{256,320},{320,384},{384,448},... | collective-permute-start | bytes 811016 | tf_op jit(solution)/shard_map/ppermute | solution.py:251
  51.7 2.4 %all_gather.27.pair_3 = bf16[2112,128]{1,0:T(8,128)(2,1)S(1)} all-gather(bf16[1056,128]{1,0:T(8,128)(2,1)S(1)} %collective-permute-done.2), channel_id=1, replica_groups={{0,32},{64,96},{128,160},{192,224},{256,288},{320,352},{384,416},{448,4..., dimensions={0}, use_global_device_ids=true | all-gather | bytes 811008 | tf_op jit(solution)/shard_map/all_gather | solution.py:239
  54.1 1.0 shard_map.79
  55.1 1.2 shard_map.80
  56.4 20.9 %all_to_all.30 = bf16[32,48,128]{2,1,0:T(8,128)(2,1)S(1)} all-to-all(bf16[32,48,128]{2,1,0:T(8,128)(2,1)S(1)} %bitcast.17), channel_id=1, replica_groups=mesh['ctx'=16,'exp'=32] {'exp'}, dimensions={0} | all-to-all | bytes 786432 | tf_op jit(solution)/shard_map/all_to_all | solution.py:230
  77.2 0.7 copy-done.9
  77.9 1.2 shard_map.81
  79.1 15.2 %all_to_all.31 = bf16[32,48,128]{2,1,0:T(8,128)(2,1)S(1)} all-to-all(bf16[32,48,128]{2,1,0:T(8,128)(2,1)S(1)} %bitcast.19), channel_id=1, replica_groups=mesh['ctx'=16,'exp'=32] {'exp'}, dimensions={0} | all-to-all | bytes 786432 | tf_op jit(solution)/shard_map/all_to_all | solution.py:230
  94.3 1.9 %shard_map.82 = (bf16[1536,128]{1,0:T(8,128)(2,1)S(1)}, bf16[96,2304]{1,0:T(8,128)(2,1)S(1)}, bf16[96,2304]{1,0:T(8,128)(2,1)S(1)}) custom-call(bf16[1536,128]{1,0:T(8,128)(2,1)S(1)} %bitcast.15, bf16[96,2048]{1,0:T(8,128)(2,1)S(1)} %get-tuple-element.30.upstream, bf16[2048,256]{1,0:T(8,128)(2,1)S(1)} %get-tuple-element.31.wa, ...), custom_call_target="tpu_custom_call" | custom-call | tf_op jit(solution)/shard_map/pallas_call | solution.py:270
  96.2 0.0 copy-start.2
  96.2 15.3 %all_to_all.32 = bf16[32,48,128]{2,1,0:T(8,128)(2,1)S(1)} all-to-all(bf16[32,48,128]{2,1,0:T(8,128)(2,1)S(1)} %bitcast.18), channel_id=1, replica_groups=mesh['ctx'=16,'exp'=32] {'exp'}, dimensions={0} | all-to-all | bytes 786432 | tf_op jit(solution)/shard_map/all_to_all | solution.py:230
  111.5 2.0 %shard_map.83 = bf16[1536,128]{1,0:T(8,128)(2,1)} custom-call(bf16[128,2048]{1,0:T(8,128)(2,1)S(1)} %copy-done.2, f32[128,2048]{1,0:T(8,128)S(1)} %get-tuple-element.28.state, s32[2,128]{1,0:T(2,128)S(1)} %bitcast.22, bf16[1536,128]{1,0:T(8,128)(2,1)S(1)} %bitcast.16), custom_call_target="tpu_custom_call" | custom-call | tf_op jit(solution)/shard_map/pallas_call | solution.py:273
  113.6 4.0 %all-to-all-start.4 = ((bf16[32,48,128]{2,1,0:T(8,128)(2,1)}), bf16[32,48,128]{2,1,0:T(8,128)(2,1)S(1)}, u32[]{:S(2)}, u32[]{:S(2)}) async-start(bf16[32,48,128]{2,1,0:T(8,128)(2,1)} %bitcast.10), calls=%async_computation.4 | async-start | bytes 786432 | tf_op jit(solution)/shard_map/all_to_all | solution.py:230
  117.6 11.5 %all_gather.29.kept_zero = bf16[192,2304]{1,0:T(8,128)(2,1)S(1)} all-gather(bf16[96,2304]{1,0:T(8,128)(2,1)S(1)} %copy-done.4), channel_id=1, replica_groups={{0,32},{64,96},{128,160},{192,224},{256,288},{320,352},{384,416},{448,4..., dimensions={0}, use_global_device_ids=true | all-gather | bytes 1327104 | tf_op jit(solution)/shard_map/all_gather | solution.py:239
  129.1 2.6 %all_gather.30.grads_one = bf16[192,2304]{1,0:T(8,128)(2,1)S(1)} all-gather(bf16[96,2304]{1,0:T(8,128)(2,1)S(1)} %copy-done.8), channel_id=1, replica_groups={{0,32},{64,96},{128,160},{192,224},{256,288},{320,352},{384,416},{448,4..., dimensions={0}, use_global_device_ids=true | all-gather | bytes 1327104 | tf_op jit(solution)/shard_map/all_gather | solution.py:239
  131.7 2.6 %all_gather.31.kept_one = bf16[192,2304]{1,0:T(8,128)(2,1)} all-gather(bf16[96,2304]{1,0:T(8,128)(2,1)S(1)} %copy-done.6), channel_id=1, replica_groups={{0,32},{64,96},{128,160},{192,224},{256,288},{320,352},{384,416},{448,4..., dimensions={0}, use_global_device_ids=true | all-gather | bytes 1327104 | tf_op jit(solution)/shard_map/all_gather | solution.py:239
  134.3 0.6 shard_map.84
  134.8 7.5 %all_gather.28.grads_zero = bf16[192,2304]{1,0:T(8,128)(2,1)S(1)} all-gather(bf16[96,2304]{1,0:T(8,128)(2,1)S(1)} %shard_map.84), channel_id=1, replica_groups={{0,32},{64,96},{128,160},{192,224},{256,288},{320,352},{384,416},{448,4..., dimensions={0}, use_global_device_ids=true | all-gather | bytes 1327104 | tf_op jit(solution)/shard_map/all_gather | solution.py:239
  142.3 0.8 shard_map.85
  143.1 35.9 %all_to_all.33.parts = bf16[8,512,128]{2,1,0:T(8,128)(2,1)S(1)} all-to-all(bf16[8,512,128]{2,1,0:T(8,128)(2,1)S(1)} %shard_map.85), channel_id=1, replica_groups={{0,64,128,192,256,320,384,448},{32,96,160,224,288,352,416,480},{1,65,12..., dimensions={0} | all-to-all | bytes 2097152 | tf_op jit(solution)/shard_map/all_to_all | solution.py:284
  179.0 0.8 shard_map.86
  (22 shorter events, 0.0 us)
Async XLA Ops:
  10.9 8.8 %collective-permute-start = (bf16[1056,128]{1,0:T(8,128)(2,1)S(1)}, bf16[1056,128]{1,0:T(8,128)(2,1)S(1)}, u32[]{:S(2)}, u32[]{:S(2)}) collective-permute-start(bf16[1056,128]{1,0:T(8,128)(2,1)S(1)} %all_gather.24.own), channel_id=1, source_target_pairs={{0,64},{64,128},{128,192},{192,256},{256,320},{320,384},{384,448},... | collective-permute-start | bytes 811016 | tf_op jit(solution)/shard_map/ppermute | solution.py:251
  19.7 34.3 %all-to-all-start = ((bf16[32,96,128]{2,1,0:T(8,128)(2,1)}), bf16[32,96,128]{2,1,0:T(8,128)(2,1)S(1)}, u32[]{:S(2)}, u32[]{:S(2)}) async-start(bf16[32,96,128]{2,1,0:T(8,128)(2,1)} %bitcast.23), calls=%async_computation | async-start | bytes 1572864 | tf_op jit(solution)/shard_map/all_to_all | solution.py:230
  29.4 8.3 %collective-permute-start.1 = (bf16[1056,128]{1,0:T(8,128)(2,1)S(1)}, bf16[1056,128]{1,0:T(8,128)(2,1)S(1)}, u32[]{:S(2)}, u32[]{:S(2)}) collective-permute-start(bf16[1056,128]{1,0:T(8,128)(2,1)S(1)} %collective-permute-done), channel_id=1, source_target_pairs={{0,64},{64,128},{128,192},{192,256},{256,320},{320,384},{384,448},... | collective-permute-start | bytes 811016 | tf_op jit(solution)/shard_map/ppermute | solution.py:251
  37.7 8.7 %collective-permute-start.2 = (bf16[1056,128]{1,0:T(8,128)(2,1)S(1)}, bf16[1056,128]{1,0:T(8,128)(2,1)S(1)}, u32[]{:S(2)}, u32[]{:S(2)}) collective-permute-start(bf16[1056,128]{1,0:T(8,128)(2,1)S(1)} %collective-permute-done.1), channel_id=1, source_target_pairs={{0,64},{64,128},{128,192},{192,256},{256,320},{320,384},{384,448},... | collective-permute-start | bytes 811016 | tf_op jit(solution)/shard_map/ppermute | solution.py:251
  46.4 8.7 %collective-permute-start.3 = (bf16[1056,128]{1,0:T(8,128)(2,1)S(1)}, bf16[1056,128]{1,0:T(8,128)(2,1)S(1)}, u32[]{:S(2)}, u32[]{:S(2)}) collective-permute-start(bf16[1056,128]{1,0:T(8,128)(2,1)S(1)} %collective-permute-done.2), channel_id=1, source_target_pairs={{0,64},{64,128},{128,192},{192,256},{256,320},{320,384},{384,448},... | collective-permute-start | bytes 811016 | tf_op jit(solution)/shard_map/ppermute | solution.py:251
  56.3 22.8 %copy-start.3 = (bf16[96,2304]{1,0:T(8,128)(2,1)}, bf16[96,2304]{1,0:T(8,128)(2,1)S(1)}, u32[]{:S(2)}) copy-start(bf16[96,2304]{1,0:T(8,128)(2,1)S(1)} %get-tuple-element.37) | copy-start | bytes 1327108
  56.3 20.9 %copy-start.1 = (bf16[128,2048]{1,0:T(8,128)(2,1)S(1)}, bf16[128,2048]{1,0:T(8,128)(2,1)}, u32[]{:S(2)}) copy-start(bf16[128,2048]{1,0:T(8,128)(2,1)} %tokens.3) | copy-start | bytes 1572868
  77.2 0.7 copy-start.9
  96.2 17.4 %copy-start.5 = (bf16[96,2304]{1,0:T(8,128)(2,1)}, bf16[96,2304]{1,0:T(8,128)(2,1)S(1)}, u32[]{:S(2)}) copy-start(bf16[96,2304]{1,0:T(8,128)(2,1)S(1)} %get-tuple-element.39) | copy-start | bytes 1327108
  96.2 17.4 %copy-start.7 = (bf16[96,2304]{1,0:T(8,128)(2,1)}, bf16[96,2304]{1,0:T(8,128)(2,1)S(1)}, u32[]{:S(2)}) copy-start(bf16[96,2304]{1,0:T(8,128)(2,1)S(1)} %get-tuple-element.38) | copy-start | bytes 1327108
  96.2 15.3 %copy-start.2 = (bf16[128,2048]{1,0:T(8,128)(2,1)S(1)}, bf16[128,2048]{1,0:T(8,128)(2,1)}, u32[]{:S(2)}) copy-start(bf16[128,2048]{1,0:T(8,128)(2,1)} %cotangent.3) | copy-start | bytes 1572868
  113.6 4.1 %copy-start.4 = (bf16[96,2304]{1,0:T(8,128)(2,1)S(1)}, bf16[96,2304]{1,0:T(8,128)(2,1)}, u32[]{:S(2)}) copy-start(bf16[96,2304]{1,0:T(8,128)(2,1)} %copy-done.3) | copy-start | bytes 1327108
  113.6 20.7 %all-to-all-start.4 = ((bf16[32,48,128]{2,1,0:T(8,128)(2,1)}), bf16[32,48,128]{2,1,0:T(8,128)(2,1)S(1)}, u32[]{:S(2)}, u32[]{:S(2)}) async-start(bf16[32,48,128]{2,1,0:T(8,128)(2,1)} %bitcast.10), calls=%async_computation.4 | async-start | bytes 786432 | tf_op jit(solution)/shard_map/all_to_all | solution.py:230
  117.6 11.5 %copy-start.8 = (bf16[96,2304]{1,0:T(8,128)(2,1)S(1)}, bf16[96,2304]{1,0:T(8,128)(2,1)}, u32[]{:S(2)}) copy-start(bf16[96,2304]{1,0:T(8,128)(2,1)} %copy-done.7) | copy-start | bytes 1327108
  129.1 2.6 %copy-start.6 = (bf16[96,2304]{1,0:T(8,128)(2,1)S(1)}, bf16[96,2304]{1,0:T(8,128)(2,1)}, u32[]{:S(2)}) copy-start(bf16[96,2304]{1,0:T(8,128)(2,1)} %copy-done.5) | copy-start | bytes 1327108
  134.8 7.5 %copy-start = (bf16[192,2304]{1,0:T(8,128)(2,1)S(1)}, bf16[192,2304]{1,0:T(8,128)(2,1)}, u32[]{:S(2)}) copy-start(bf16[192,2304]{1,0:T(8,128)(2,1)} %all_gather.31.kept_one) | copy-start | bytes 2654212

commit v3 on v2

--- a/solution.py
+++ b/solution.py
@@ -67,6 +67,19 @@
     out[2 * G :, :] = jnp.broadcast_to(router[...], (SHARD - 2 * G, LANE))
 
 
+def columns_kernel(own, pair_1, pair_2, column):
+    chip = lax.div(lax.axis_index("ctx"), 2)
+    column[...] = jnp.zeros_like(column)
+    blocks = [(own, 0, chip)]
+    for hop, pair in enumerate((pair_1, pair_2), 1):
+        blocks += [(pair, 0, chip + CHIPS - hop), (pair, 2 * SHARD, chip + hop)]
+    for block, first, where in blocks:
+        for core in range(2):
+            at = first + core * SHARD + 2 * G
+            to = pl.multiple_of((2 * lax.rem(where, CHIPS) + core) * LANE, LANE)
+            column[:, pl.ds(to, LANE)] = block[at : at + 1, :].astype(f32)
+
+
 def place(block, first, chip, wa, wb, column):
     for core in range(2):
         at = first + core * SHARD
@@ -77,6 +90,16 @@
         column[:, to] = block[at + 2 * G : at + 2 * G + 1, :].astype(f32)
 
 
+def split(full, narrow, own, mate, first=0):
+    core = lax.rem(lax.axis_index("ctx"), 2)
+    for z in range(CHIPS):
+        to = slice(first + z * LANE, first + (z + 1) * LANE)
+        own[:, to] = full[:, pl.ds(pl.multiple_of((2 * z + core) * LANE, LANE), LANE)]
+        mate[:, to] = full[:, pl.ds(pl.multiple_of((2 * z + 1 - core) * LANE, LANE), LANE)]
+    own[:, first + D // 2 : first + HALF] = narrow
+    mate[:, first + D // 2 : first + HALF] = narrow
+
+
 def forward(rows, wa, wb, column):
     before = jnp.dot(rows, wa[...], preferred_element_type=f32)
     positive = jnp.maximum(before, 0.0)
@@ -111,10 +134,11 @@
 
 
 def first_kernel(
-    rows, own, pair_1, pair_2, pair_3, far,
-    out, positive_out, kept, gate_out, wa, wb, column, wide
+    rows, own, pair_1, pair_2, pair_3, far, columns,
+    out, positive_out, own_out, mate_out, gate_out, wa, wb, column, wide
 ):
     chip = lax.div(lax.axis_index("ctx"), 2)
+    column[...] = columns[...]
     place(own, 0, chip, wa, wb, column)
     for hop, pair in enumerate((pair_1, pair_2, pair_3), 1):
         place(pair, 0, lax.rem(chip + CHIPS - hop, CHIPS), wa, wb, column)
@@ -124,23 +148,27 @@
     pack((gate * expert_out), wide)
     out[...] = wide[...].astype(bf16)
     positive_out[...] = positive
-    kept[:, :D] = rows[...]
-    kept[:, D:] = hidden
+    split(rows, hidden, own_out, mate_out)
     gate_out[...] = jnp.broadcast_to(gate, (SLOTS, LANE))
 
 
-def middle_kernel(tokens, ids, mixed, out, state_out, wide, dense):
+def choose_kernel(ids, first, second):
+    first[...] = choose(ids[0:1, :])
+    second[...] = choose(ids[1:2, :])
+
+
+def middle_kernel(tokens, pick_zero, pick_one, mixed, out, state_out, wide, dense):
     wide[...] = mixed[...].astype(f32)
     unpack(wide, dense)
-    state = tokens[...].astype(f32) + to_tokens(choose(ids[0:1, :]), dense[...])
+    state = tokens[...].astype(f32) + to_tokens(pick_zero[...], dense[...])
     state_out[...] = state
     unit, _ = normalize(state)
-    pack(to_slots(choose(ids[1:2, :]), unit.astype(bf16)), wide)
+    pack(to_slots(pick_one[...], unit.astype(bf16)), wide)
     out[...] = wide[...].astype(bf16)
 
 
 def second_kernel(
-    taken, upstream, wa, wb, column, out, kept, grads, wide, dense
+    taken, upstream, wa, wb, column, out, own, mate, wide, dense, expert
 ):
     wide[...] = taken[...].astype(f32)
     unpack(wide, dense)
@@ -153,20 +181,19 @@
     )
     pack(flowing + grad_logit * column[...], wide)
     out[...] = wide[...].astype(bf16)
-    kept[:, :D] = dense[...]
-    kept[:, D:] = hidden
-    grads[:, :D] = grad_expert
-    grads[:, D:] = grad_pre
-
-
-def return_kernel(cotangent, state, ids, taken, out, wide, dense):
+    expert[...] = grad_expert
+    split(dense, hidden, own, mate)
+    split(expert, grad_pre, own, mate, HALF)
+
+
+def return_kernel(cotangent, state, pick_zero, pick_one, taken, out, wide, dense):
     wide[...] = taken[...].astype(f32)
     unpack(wide, dense)
     unit, scale = normalize(state[...])
-    grad = to_tokens(choose(ids[1:2, :]), dense[...])
+    grad = to_tokens(pick_one[...], dense[...])
     inner = jnp.mean(grad * unit, axis=-1, keepdims=True)
     upstream = cotangent[...].astype(f32) + (grad - unit * inner) / scale
-    pack(to_slots(choose(ids[0:1, :]), upstream.astype(bf16)), wide)
+    pack(to_slots(pick_zero[...], upstream.astype(bf16)), wide)
     out[...] = wide[...].astype(bf16)
 
 
@@ -174,27 +201,26 @@
     return lax.dot_general(left, right, (((0,), (0,)), ((), ())), preferred_element_type=f32)
 
 
-def first_grad_kernel(taken, wb, positive, gate, out, wide, dense):
+def first_grad_kernel(taken, wb, positive, gate, own, mate, wide, dense):
     wide[...] = taken[...].astype(f32)
     unpack(wide, dense)
     _, grad_expert, grad_pre = backward(dense[...], wb, positive[...], gate[:, :1])
-    out[:, :D] = grad_expert
-    out[:, D:] = grad_pre
-
-
-def weight_kernel(grads_zero, kept_zero, grads_one, kept_one, out, rows, grads, parts):
-    core = lax.rem(lax.axis_index("ctx"), 2)
-    parts_in = ((grads_zero, kept_zero), (grads_one, kept_one))
-    for at, (grad, kept) in zip((0, 2 * SLOTS), parts_in):
-        to = slice(at, at + 2 * SLOTS)
-        for z in range(CHIPS):
-            own = pl.ds(pl.multiple_of((2 * z + core) * LANE, LANE), LANE)
-            rows[to, z * LANE : (z + 1) * LANE] = kept[:, own]
-            grads[to, z * LANE : (z + 1) * LANE] = grad[:, own]
-        parts[to, :G] = grad[:, D:]
-        parts[to, G:] = kept[:, D:]
-    part_in = over_rows(parts[:, :G], rows[...])
-    part_out = over_rows(parts[:, G:], grads[...])
+    dense[...] = grad_expert
+    split(dense, grad_pre, own, mate)
+
+
+def weight_kernel(
+    grads_own, grads_both, kept_own, kept_mate, one_own, one_mate, out, rows, hidden, grads, pre
+):
+    mate = pl.multiple_of((1 - lax.rem(lax.axis_index("ctx"), 2)) * SLOTS, SLOTS)
+    kept = (kept_own[...], kept_mate[...], one_own[:, :HALF], one_mate[:, :HALF])
+    grad = (grads_own[...], grads_both[pl.ds(mate, SLOTS), :], one_own[:, HALF:], one_mate[:, HALF:])
+    for i in range(4):
+        to = slice(i * SLOTS, (i + 1) * SLOTS)
+        rows[to, :], hidden[to, :] = kept[i][:, : D // 2], kept[i][:, D // 2 :]
+        grads[to, :], pre[to, :] = grad[i][:, : D // 2], grad[i][:, D // 2 :]
+    part_in = over_rows(pre[...], rows[...])
+    part_out = over_rows(hidden[...], grads[...])
     for z in range(CHIPS):
         at = slice(z * LANE, (z + 1) * LANE)
         out[z, :G, :] = part_in[:, at].astype(bf16)
@@ -209,19 +235,24 @@
     grad_out[0] = total[G:, :]
 
 
-def call(kernel, outs, scratch=(), room=24):
+def call(kernel, outs, scratch=(), room=24, cost=0):
     return pl.pallas_call(
         kernel,
         out_shape=[jax.ShapeDtypeStruct(s, t) for s, t in outs],
         scratch_shapes=[pltpu.VMEM(s, t) for s, t in scratch],
         compiler_params=pltpu.CompilerParams(vmem_limit_bytes=room << 20),
+        cost_estimate=pl.CostEstimate(flops=cost, bytes_accessed=0, transcendentals=0)
+        if cost
+        else None,
     )
 
 
 PACKED = ((EXPERTS * PEER, LANE), bf16)
 WIDE = ((EXPERTS * PEER, LANE), f32)
 DENSE = ((SLOTS, D), bf16)
-KEPT = ((SLOTS, D + G), bf16)
+PICK = ((SLOTS, TOK), bf16)
+HALF = D // 2 + G
+KEPT = ((SLOTS, HALF), bf16)
 WEIGHTS = (((D, G), bf16), ((G, D), bf16), ((1, D), f32))
 
 
@@ -244,42 +275,48 @@
         weight_in, weight_out, router.reshape(1, LANE)
     )
     own = both_cores(share)
-    passing, pairs = own, []
-    for hop in range(chips // 2):
-        if hop > 1:
-            passing, pairs[hop - 2] = lax.optimization_barrier((passing, both_cores(pairs[hop - 2])))
-        passing = lax.ppermute(passing, "ctx", around)
-        pairs.append(passing)
-        if hop == 0:
-            first_hop = passing
-    pairs[2] = both_cores(pairs[2])
     wide_two = ((2 * EXPERTS * PEER, LANE), f32)
     (leaving,) = call(dispatch_kernel, [((2 * EXPERTS * PEER, LANE), bf16)], [wide_two], room=60)(
         tokens, cotangent, ids
     )
-    leaving, _ = lax.optimization_barrier((leaving, first_hop))
+    passing = lax.ppermute(own, "ctx", around)
+    leaving, passing = lax.optimization_barrier((leaving, passing))
+    pairs = [passing]
+    passing = lax.ppermute(passing, "ctx", around)
+    pairs.append(passing)
+    passing = lax.ppermute(passing, "ctx", around)
+    pairs = [both_cores(pair) for pair in pairs]
+    picks = call(choose_kernel, [PICK, PICK])(ids)
+    passing, *rest = lax.optimization_barrier((passing, *pairs, *picks))
+    pairs, picks = rest[:2], rest[2:]
+    pairs += [both_cores(passing), lax.ppermute(passing, "ctx", around)]
+    (columns,) = call(columns_kernel, [WEIGHTS[2]], cost=10 * 1150000000)(own, *pairs[:2])
     rows_zero, upstream_one = call(arrive_kernel, [DENSE, DENSE], [wide_two])(over_exp(leaving))
-    mixed, positive, kept_zero, gate, wa, wb, column = call(
+    mixed, positive, kept_own, kept_mate, gate, wa, wb, column = call(
         first_kernel,
-        [PACKED, ((SLOTS, G), f32), KEPT, ((SLOTS, LANE), f32), *WEIGHTS],
+        [PACKED, ((SLOTS, G), f32), KEPT, KEPT, ((SLOTS, LANE), f32), *WEIGHTS],
         [WIDE],
-    )(rows_zero, own, *pairs)
+    )(rows_zero, own, *pairs, columns)
+    across = [(2 * z + c, 2 * z + 1 - c) for z in range(chips) for c in range(2)]
+    kept_mate = lax.ppermute(kept_mate, "ctx", across)
     leaving, state_one = call(middle_kernel, [PACKED, ((TOK, D), f32)], [WIDE, DENSE])(
-        tokens, ids, over_exp(mixed)
-    )
-    leaving, kept_one, grads_one = call(second_kernel, [PACKED, KEPT, KEPT], [WIDE, DENSE])(
-        over_exp(leaving), upstream_one, wa, wb, column
-    )
+        tokens, *picks, over_exp(mixed)
+    )
+    double = ((SLOTS, 2 * HALF), bf16)
+    leaving, one_own, one_mate = call(
+        second_kernel, [PACKED, double, double], [WIDE, DENSE, DENSE]
+    )(over_exp(leaving), upstream_one, wa, wb, column)
+    one_mate = lax.ppermute(one_mate, "ctx", across)
     (leaving,) = call(return_kernel, [PACKED], [WIDE, DENSE])(
-        cotangent, state_one, ids, over_exp(leaving)
-    )
-    (grads_zero,) = call(first_grad_kernel, [KEPT], [WIDE, DENSE])(
+        cotangent, state_one, *picks, over_exp(leaving)
+    )
+    grads_own, grads_mate = call(first_grad_kernel, [KEPT, KEPT], [WIDE, DENSE])(
         over_exp(leaving), wb, positive, gate
     )
-    half = ((4 * SLOTS, D // 2), bf16)
+    half, narrow = ((4 * SLOTS, D // 2), bf16), ((4 * SLOTS, G), bf16)
     (pair,) = call(
-        weight_kernel, [((CHIPS, 2 * G, LANE), bf16)], [half, half, ((4 * SLOTS, 2 * G), bf16)]
-    )(both_cores(grads_zero), both_cores(kept_zero), both_cores(grads_one), both_cores(kept_one))
+        weight_kernel, [((CHIPS, 2 * G, LANE), bf16)], [half, narrow, half, narrow]
+    )(grads_own, both_cores(grads_mate), kept_own, kept_mate, one_own, one_mate)
     columns = [[2 * z + c for z in range(chips)] for c in range(2)]
     parts = lax.all_to_all(pair, "ctx", 0, 0, tiled=True, axis_index_groups=columns)
     grad_in, grad_out = call(total_kernel, [((1, LANE, G), f32), ((1, G, LANE), f32)])(parts)

time: 181 us -> 178 us (0.983)
  blocking collectives: 127 us -> 108 us
  waiting for transfers between devices: 2.39 us -> 15.9 us
  starting transfers between devices: 34.5 us -> 36.6 us
    all_gather x8 -> x5, blocking collectives: 39.6 us -> 21.5 us  [both_cores(): lax.all_gather(value, 'ctx', axis=0, tiled=True, axis_index_groups=cores)]
    all_to_all x2, waiting for transfers between devices: 0.01 us -> 14.6 us  [over_exp(): return lax.all_to_all(shaped, 'exp', 0, 0, tiled=True).reshape(buffer.shape)]
    ppermute x0 -> x4, starting transfers between devices: none -> 14.3 us  [the longest x1 5.28 us: on_device(): passing = lax.ppermute(own, 'ctx', around)]
    ppermute x4 -> x2, starting transfers between devices: 20.8 us -> 6.75 us  [on_device(): passing = lax.ppermute(passing, 'ctx', around)]
    all_to_all x1, blocking collectives: 35.9 us -> 31.6 us  [on_device(): lax.all_to_all(pair, 'ctx', 0, 0, tiled=True, axis_index_groups=columns)]
    all_to_all x3, blocking collectives: 51.4 us -> 55.2 us  [over_exp(): return lax.all_to_all(shaped, 'exp', 0, 0, tiled=True).reshape(buffer.shape)]
    all_to_all x2, starting transfers between devices: 13.7 us -> 15.6 us  [over_exp(): return lax.all_to_all(shaped, 'exp', 0, 0, tiled=True).reshape(buffer.shape)]
    pallas_call x4 -> x6, Pallas kernels: 4.49 us -> 5.33 us  [the longest x1 2.38 us: on_device(): call(second_kernel, [PACKED, double, double], [WIDE, DENSE, DENSE])]
  transfers between devices with their start and end apart: 6 -> 8, of which waited for: 2 -> 3; matrix products, arithmetic and copies ran while one was open for 0% -> 0% of each run, Pallas kernels for 3% -> 3%
where the time goes in v3:
time: 178 us; the launch traced here: 177 us
  blocking collectives  108 us (61%)
  starting transfers between devices  36.6 us (21%)
  waiting for transfers between devices  15.9 us (9%)
  Pallas kernels  15.3 us (9%)
    all_to_all x3, blocking collectives, over_exp(): return lax.all_to_all(shaped, 'exp', 0, 0, tiled=True).reshape(buffer.shape)  55.2 us
    all_to_all x1, blocking collectives, on_device(): lax.all_to_all(pair, 'ctx', 0, 0, tiled=True, axis_index_groups=columns)  31.6 us
    all_gather x5, blocking collectives, both_cores(): lax.all_gather(value, 'ctx', axis=0, tiled=True, axis_index_groups=cores)  21.5 us
    all_to_all x2, starting transfers between devices, over_exp(): return lax.all_to_all(shaped, 'exp', 0, 0, tiled=True).reshape(buffer.shape)  15.6 us
    all_to_all x2, waiting for transfers between devices, over_exp(): return lax.all_to_all(shaped, 'exp', 0, 0, tiled=True).reshape(buffer.shape)  14.6 us
    ppermute x2, starting transfers between devices, on_device(): passing = lax.ppermute(passing, 'ctx', around)  6.75 us
    ppermute x1, starting transfers between devices, on_device(): passing = lax.ppermute(own, 'ctx', around)  5.28 us
    ppermute x1, starting transfers between devices, on_device(): one_mate = lax.ppermute(one_mate, 'ctx', across)  4.05 us
  transfers between devices with their start and end apart: 8, of which 3 were waited for; matrix products, arithmetic and copies ran while one was open for 0% of the time, Pallas kernels for 3%

profile of v3, /device:TPU:1, one launch (start us, length us, event | category | flops | bytes accessed | tf_op | source)
XLA Modules:
  0.0 177.1 jit_solution(2095870366909025608)
XLA Ops:
  0.6 1.6 shard_map.78
  2.2 8.7 %all_gather.15.own = bf16[1056,128]{1,0:T(8,128)(2,1)S(1)} all-gather(bf16[528,128]{1,0:T(8,128)(2,1)} %shard_map.78), channel_id=1, replica_groups={{0,32},{64,96},{128,160},{192,224},{256,288},{320,352},{384,416},{448,4..., dimensions={0}, use_global_device_ids=true | all-gather | bytes 405504 | tf_op jit(solution)/shard_map/all_gather | solution.py:270
  10.9 5.3 %collective-permute-start = (bf16[1056,128]{1,0:T(8,128)(2,1)S(1)}, bf16[1056,128]{1,0:T(8,128)(2,1)S(1)}, u32[]{:S(2)}, u32[]{:S(2)}) collective-permute-start(bf16[1056,128]{1,0:T(8,128)(2,1)S(1)} %all_gather.15.own), channel_id=1, source_target_pairs={{0,64},{64,128},{128,192},{192,256},{256,320},{320,384},{384,448},... | collective-permute-start | bytes 811016 | tf_op jit(solution)/shard_map/ppermute | solution.py:282
  16.2 3.6 %shard_map.77 = bf16[3072,128]{1,0:T(8,128)(2,1)} custom-call(bf16[128,2048]{1,0:T(8,128)(2,1)} %tokens.3, bf16[128,2048]{1,0:T(8,128)(2,1)} %cotangent.3, s32[2,128]{1,0:T(2,128)} %bitcast.20), custom_call_target="tpu_custom_call" | custom-call | tf_op jit(solution)/shard_map/pallas_call | solution.py:279
  19.8 4.8 %collective-permute-start.1 = (bf16[1056,128]{1,0:T(8,128)(2,1)S(1)}, bf16[1056,128]{1,0:T(8,128)(2,1)S(1)}, u32[]{:S(2)}, u32[]{:S(2)}) collective-permute-start(bf16[1056,128]{1,0:T(8,128)(2,1)S(1)} %collective-permute-done), channel_id=1, source_target_pairs={{0,64},{64,128},{128,192},{192,256},{256,320},{320,384},{384,448},... | collective-permute-start | bytes 811016 | tf_op jit(solution)/shard_map/ppermute | solution.py:285
  24.6 0.0 copy-start.10
  24.6 9.7 %all-to-all-start = ((bf16[32,96,128]{2,1,0:T(8,128)(2,1)}), bf16[32,96,128]{2,1,0:T(8,128)(2,1)S(1)}, u32[]{:S(2)}, u32[]{:S(2)}) async-start(bf16[32,96,128]{2,1,0:T(8,128)(2,1)} %bitcast.22), calls=%async_computation | async-start | bytes 1572864 | tf_op jit(solution)/shard_map/all_to_all | solution.py:261
  34.3 0.2 shard_map.79
  34.5 1.9 %collective-permute-start.2 = (bf16[1056,128]{1,0:T(8,128)(2,1)S(1)}, bf16[1056,128]{1,0:T(8,128)(2,1)}, u32[]{:S(2)}, u32[]{:S(2)}) collective-permute-start(bf16[1056,128]{1,0:T(8,128)(2,1)S(1)} %collective-permute-done.1), channel_id=1, source_target_pairs={{0,64},{64,128},{128,192},{192,256},{256,320},{320,384},{384,448},... | collective-permute-start | bytes 811016 | tf_op jit(solution)/shard_map/ppermute | solution.py:287
  36.5 2.2 %all_gather.16.pair_1 = bf16[2112,128]{1,0:T(8,128)(2,1)S(1)} all-gather(bf16[1056,128]{1,0:T(8,128)(2,1)S(1)} %collective-permute-done), channel_id=1, replica_groups={{0,32},{64,96},{128,160},{192,224},{256,288},{320,352},{384,416},{448,4..., dimensions={0}, use_global_device_ids=true | all-gather | bytes 811008 | tf_op jit(solution)/shard_map/all_gather | solution.py:270
  38.7 2.2 %all_gather.17.pair_2 = bf16[2112,128]{1,0:T(8,128)(2,1)S(1)} all-gather(bf16[1056,128]{1,0:T(8,128)(2,1)S(1)} %collective-permute-done.1), channel_id=1, replica_groups={{0,32},{64,96},{128,160},{192,224},{256,288},{320,352},{384,416},{448,4..., dimensions={0}, use_global_device_ids=true | all-gather | bytes 811008 | tf_op jit(solution)/shard_map/all_gather | solution.py:270
  40.8 1.3 collective-permute-done.2
  42.1 3.0 %collective-permute-start.3 = (bf16[1056,128]{1,0:T(8,128)(2,1)}, bf16[1056,128]{1,0:T(8,128)(2,1)S(1)}, u32[]{:S(2)}, u32[]{:S(2)}) collective-permute-start(bf16[1056,128]{1,0:T(8,128)(2,1)} %collective-permute-done.2), channel_id=1, source_target_pairs={{0,64},{64,128},{128,192},{192,256},{256,320},{320,384},{384,448},... | collective-permute-start | bytes 811016 | tf_op jit(solution)/shard_map/ppermute | solution.py:292
  45.2 2.4 %all_gather.18.pair_3 = bf16[2112,128]{1,0:T(8,128)(2,1)S(1)} all-gather(bf16[1056,128]{1,0:T(8,128)(2,1)} %collective-permute-done.2), channel_id=1, replica_groups={{0,32},{64,96},{128,160},{192,224},{256,288},{320,352},{384,416},{448,4..., dimensions={0}, use_global_device_ids=true | all-gather | bytes 811008 | tf_op jit(solution)/shard_map/all_gather | solution.py:270
  47.6 8.6 %all-to-all-done = bf16[32,96,128]{2,1,0:T(8,128)(2,1)S(1)} async-done(((bf16[32,96,128]{2,1,0:T(8,128)(2,1)}), bf16[32,96,128]{2,1,0:T(8,128)(2,1)S(1)}, u32[]{:S(2)}, u32[]{:S(2)}) %all-to-all-start) | async-done | bytes 786464 | tf_op jit(solution)/shard_map/all_to_all | solution.py:261
  56.2 1.0 shard_map.80
  57.2 1.3 shard_map.82
  58.6 19.9 %all_to_all.30 = bf16[32,48,128]{2,1,0:T(8,128)(2,1)S(1)} all-to-all(bf16[32,48,128]{2,1,0:T(8,128)(2,1)S(1)} %bitcast.17), channel_id=1, replica_groups=mesh['ctx'=16,'exp'=32] {'exp'}, dimensions={0} | all-to-all | bytes 786432 | tf_op jit(solution)/shard_map/all_to_all | solution.py:261
  78.5 1.1 shard_map.83
  79.6 17.2 %all_to_all.31 = bf16[32,48,128]{2,1,0:T(8,128)(2,1)S(1)} all-to-all(bf16[32,48,128]{2,1,0:T(8,128)(2,1)S(1)} %bitcast.19), channel_id=1, replica_groups=mesh['ctx'=16,'exp'=32] {'exp'}, dimensions={0} | all-to-all | bytes 786432 | tf_op jit(solution)/shard_map/all_to_all | solution.py:261
  96.8 2.4 %shard_map.84 = (bf16[1536,128]{1,0:T(8,128)(2,1)S(1)}, bf16[96,2560]{1,0:T(8,128)(2,1)S(1)}, bf16[96,2560]{1,0:T(8,128)(2,1)}) custom-call(bf16[1536,128]{1,0:T(8,128)(2,1)S(1)} %bitcast.16, bf16[96,2048]{1,0:T(8,128)(2,1)S(1)} %get-tuple-element.41.upstream, bf16[2048,256]{1,0:T(8,128)(2,1)S(1)} %get-tuple-element.42.wa, ...), custom_call_target="tpu_custom_call" | custom-call | tf_op jit(solution)/shard_map/pallas_call | solution.py:306
  99.2 18.1 %all_to_all.32 = bf16[32,48,128]{2,1,0:T(8,128)(2,1)S(1)} all-to-all(bf16[32,48,128]{2,1,0:T(8,128)(2,1)S(1)} %bitcast.18), channel_id=1, replica_groups=mesh['ctx'=16,'exp'=32] {'exp'}, dimensions={0} | all-to-all | bytes 786432 | tf_op jit(solution)/shard_map/all_to_all | solution.py:261
  117.3 1.9 %shard_map.85 = bf16[1536,128]{1,0:T(8,128)(2,1)} custom-call(bf16[128,2048]{1,0:T(8,128)(2,1)S(1)} %copy-done.1, f32[128,2048]{1,0:T(8,128)S(1)} %get-tuple-element.39.state, bf16[96,128]{1,0:T(8,128)(2,1)S(1)} %copy-done.3, bf16[96,128]{1,0:T(8,128)(2,1)S(1)} %copy-done.5, bf16[1536,128]{1,0:T(8,128)(2,1)S(1)} %bitcast.13), custom_call_target="tpu_custom_call" | custom-call | tf_op jit(solution)/shard_map/pallas_call | solution.py:310
  119.2 5.9 %all-to-all-start.4 = ((bf16[32,48,128]{2,1,0:T(8,128)(2,1)}), bf16[32,48,128]{2,1,0:T(8,128)(2,1)S(1)}, u32[]{:S(2)}, u32[]{:S(2)}) async-start(bf16[32,48,128]{2,1,0:T(8,128)(2,1)} %bitcast.10), calls=%async_computation.4 | async-start | bytes 786432 | tf_op jit(solution)/shard_map/all_to_all | solution.py:261
  125.2 4.1 %collective-permute-start.5 = (bf16[96,2560]{1,0:T(8,128)(2,1)}, bf16[96,2560]{1,0:T(8,128)(2,1)S(1)}, u32[]{:S(2)}, u32[]{:S(2)}) collective-permute-start(bf16[96,2560]{1,0:T(8,128)(2,1)} %get-tuple-element.53), channel_id=1, source_target_pairs={{0,32},{32,0},{64,96},{96,64},{128,160},{160,128},{192,224},{224,1... | collective-permute-start | bytes 1474568 | tf_op jit(solution)/shard_map/ppermute | solution.py:309
  129.2 1.9 %collective-permute-start.4 = (bf16[96,1280]{1,0:T(8,128)(2,1)S(1)}, bf16[96,1280]{1,0:T(8,128)(2,1)S(1)}, u32[]{:S(2)}, u32[]{:S(2)}) collective-permute-start(bf16[96,1280]{1,0:T(8,128)(2,1)S(1)} %copy-done.12), channel_id=1, source_target_pairs={{0,32},{32,0},{64,96},{96,64},{128,160},{160,128},{192,224},{224,1... | collective-permute-start | bytes 737288 | tf_op jit(solution)/shard_map/ppermute | solution.py:301
  131.2 6.0 %all-to-all-done.4 = bf16[32,48,128]{2,1,0:T(8,128)(2,1)S(1)} async-done(((bf16[32,48,128]{2,1,0:T(8,128)(2,1)}), bf16[32,48,128]{2,1,0:T(8,128)(2,1)S(1)}, u32[]{:S(2)}, u32[]{:S(2)}) %all-to-all-start.4) | async-done | bytes 393248 | tf_op jit(solution)/shard_map/all_to_all | solution.py:261
  137.2 0.7 shard_map.86
  137.9 6.0 %all_gather.19.grads_both = bf16[192,1280]{1,0:T(8,128)(2,1)S(1)} all-gather(bf16[96,1280]{1,0:T(8,128)(2,1)S(1)} %get-tuple-element.49), channel_id=1, replica_groups={{0,32},{64,96},{128,160},{192,224},{256,288},{320,352},{384,416},{448,4..., dimensions={0}, use_global_device_ids=true | all-gather | bytes 737280 | tf_op jit(solution)/shard_map/all_gather | solution.py:270
  143.9 0.7 shard_map.87
  144.7 31.6 %all_to_all.33.parts = bf16[8,512,128]{2,1,0:T(8,128)(2,1)S(1)} all-to-all(bf16[8,512,128]{2,1,0:T(8,128)(2,1)S(1)} %shard_map.87), channel_id=1, replica_groups={{0,64,128,192,256,320,384,448},{32,96,160,224,288,352,416,480},{1,65,12..., dimensions={0} | all-to-all | bytes 2097152 | tf_op jit(solution)/shard_map/all_to_all | solution.py:321
  176.3 0.8 shard_map.88
  (31 shorter events, 0.1 us)
Async XLA Ops:
  10.9 8.9 %collective-permute-start = (bf16[1056,128]{1,0:T(8,128)(2,1)S(1)}, bf16[1056,128]{1,0:T(8,128)(2,1)S(1)}, u32[]{:S(2)}, u32[]{:S(2)}) collective-permute-start(bf16[1056,128]{1,0:T(8,128)(2,1)S(1)} %all_gather.15.own), channel_id=1, source_target_pairs={{0,64},{64,128},{128,192},{192,256},{256,320},{320,384},{384,448},... | collective-permute-start | bytes 811016 | tf_op jit(solution)/shard_map/ppermute | solution.py:282
  19.8 14.7 %collective-permute-start.1 = (bf16[1056,128]{1,0:T(8,128)(2,1)S(1)}, bf16[1056,128]{1,0:T(8,128)(2,1)S(1)}, u32[]{:S(2)}, u32[]{:S(2)}) collective-permute-start(bf16[1056,128]{1,0:T(8,128)(2,1)S(1)} %collective-permute-done), channel_id=1, source_target_pairs={{0,64},{64,128},{128,192},{192,256},{256,320},{320,384},{384,448},... | collective-permute-start | bytes 811016 | tf_op jit(solution)/shard_map/ppermute | solution.py:285
  24.6 9.7 %copy-start.10 = (s32[2,128,1]{1,2,0:T(1,128)S(1)}, s32[2,128,1]{1,2,0:T(1,128)}, u32[]{:S(2)}) copy-start(s32[2,128,1]{1,2,0:T(1,128)} %param.8) | copy-start | bytes 3076
  24.6 31.6 %all-to-all-start = ((bf16[32,96,128]{2,1,0:T(8,128)(2,1)}), bf16[32,96,128]{2,1,0:T(8,128)(2,1)S(1)}, u32[]{:S(2)}, u32[]{:S(2)}) async-start(bf16[32,96,128]{2,1,0:T(8,128)(2,1)} %bitcast.22), calls=%async_computation | async-start | bytes 1572864 | tf_op jit(solution)/shard_map/all_to_all | solution.py:261
  34.5 4.2 %copy-start.2 = (bf16[96,128]{1,0:T(8,128)(2,1)}, bf16[96,128]{1,0:T(8,128)(2,1)S(1)}, u32[]{:S(2)}) copy-start(bf16[96,128]{1,0:T(8,128)(2,1)S(1)} %get-tuple-element.31.pick_zero) | copy-start | bytes 73732
  34.5 4.1 %copy-start.4 = (bf16[96,128]{1,0:T(8,128)(2,1)}, bf16[96,128]{1,0:T(8,128)(2,1)S(1)}, u32[]{:S(2)}) copy-start(bf16[96,128]{1,0:T(8,128)(2,1)S(1)} %get-tuple-element.32.pick_one) | copy-start | bytes 73732
  34.5 7.6 %collective-permute-start.2 = (bf16[1056,128]{1,0:T(8,128)(2,1)S(1)}, bf16[1056,128]{1,0:T(8,128)(2,1)}, u32[]{:S(2)}, u32[]{:S(2)}) collective-permute-start(bf16[1056,128]{1,0:T(8,128)(2,1)S(1)} %collective-permute-done.1), channel_id=1, source_target_pairs={{0,64},{64,128},{128,192},{192,256},{256,320},{320,384},{384,448},... | collective-permute-start | bytes 811016 | tf_op jit(solution)/shard_map/ppermute | solution.py:287
  42.1 15.1 %collective-permute-start.3 = (bf16[1056,128]{1,0:T(8,128)(2,1)}, bf16[1056,128]{1,0:T(8,128)(2,1)S(1)}, u32[]{:S(2)}, u32[]{:S(2)}) collective-permute-start(bf16[1056,128]{1,0:T(8,128)(2,1)} %collective-permute-done.2), channel_id=1, source_target_pairs={{0,64},{64,128},{128,192},{192,256},{256,320},{320,384},{384,448},... | collective-permute-start | bytes 811016 | tf_op jit(solution)/shard_map/ppermute | solution.py:292
  45.2 2.4 %copy-start.8 = (f32[1,2048]{1,0:T(1,128)}, f32[1,2048]{1,0:T(1,128)S(1)}, u32[]{:S(2)}) copy-start(f32[1,2048]{1,0:T(1,128)S(1)} %shard_map.81.columns) | copy-start | bytes 24580
  56.2 1.0 copy-start.9
  58.5 20.0 %copy-start.6 = (f32[96,128]{1,0:T(8,128)}, f32[96,128]{1,0:T(8,128)S(1)}, u32[]{:S(2)}) copy-start(f32[96,128]{1,0:T(8,128)S(1)} %get-tuple-element.47.gate) | copy-start | bytes 147460
  58.6 20.0 %copy-start.11 = (bf16[96,1280]{1,0:T(8,128)(2,1)}, bf16[96,1280]{1,0:T(8,128)(2,1)S(1)}, u32[]{:S(2)}) copy-start(bf16[96,1280]{1,0:T(8,128)(2,1)S(1)} %get-tuple-element.51) | copy-start | bytes 737284
  58.6 20.0 %copy-start = (bf16[128,2048]{1,0:T(8,128)(2,1)S(1)}, bf16[128,2048]{1,0:T(8,128)(2,1)}, u32[]{:S(2)}) copy-start(bf16[128,2048]{1,0:T(8,128)(2,1)} %tokens.3) | copy-start | bytes 1572868
  58.6 19.9 %copy-start.3 = (bf16[96,128]{1,0:T(8,128)(2,1)S(1)}, bf16[96,128]{1,0:T(8,128)(2,1)}, u32[]{:S(2)}) copy-start(bf16[96,128]{1,0:T(8,128)(2,1)} %copy-done.2) | copy-start | bytes 73732
  58.6 19.9 %copy-start.5 = (bf16[96,128]{1,0:T(8,128)(2,1)S(1)}, bf16[96,128]{1,0:T(8,128)(2,1)}, u32[]{:S(2)}) copy-start(bf16[96,128]{1,0:T(8,128)(2,1)} %copy-done.4) | copy-start | bytes 73732
  99.2 18.1 %copy-start.1 = (bf16[128,2048]{1,0:T(8,128)(2,1)S(1)}, bf16[128,2048]{1,0:T(8,128)(2,1)}, u32[]{:S(2)}) copy-start(bf16[128,2048]{1,0:T(8,128)(2,1)} %cotangent.3) | copy-start | bytes 1572868
  119.2 10.0 %copy-start.12 = (bf16[96,1280]{1,0:T(8,128)(2,1)S(1)}, bf16[96,1280]{1,0:T(8,128)(2,1)}, u32[]{:S(2)}) copy-start(bf16[96,1280]{1,0:T(8,128)(2,1)} %copy-done.11) | copy-start | bytes 737284
  119.2 17.9 %copy-start.7 = (f32[96,128]{1,0:T(8,128)S(1)}, f32[96,128]{1,0:T(8,128)}, u32[]{:S(2)}) copy-start(f32[96,128]{1,0:T(8,128)} %copy-done.6) | copy-start | bytes 147460
  119.2 17.9 %all-to-all-start.4 = ((bf16[32,48,128]{2,1,0:T(8,128)(2,1)}), bf16[32,48,128]{2,1,0:T(8,128)(2,1)S(1)}, u32[]{:S(2)}, u32[]{:S(2)}) async-start(bf16[32,48,128]{2,1,0:T(8,128)(2,1)} %bitcast.10), calls=%async_computation.4 | async-start | bytes 786432 | tf_op jit(solution)/shard_map/all_to_all | solution.py:261
  125.2 18.8 %collective-permute-start.5 = (bf16[96,2560]{1,0:T(8,128)(2,1)}, bf16[96,2560]{1,0:T(8,128)(2,1)S(1)}, u32[]{:S(2)}, u32[]{:S(2)}) collective-permute-start(bf16[96,2560]{1,0:T(8,128)(2,1)} %get-tuple-element.53), channel_id=1, source_target_pairs={{0,32},{32,0},{64,96},{96,64},{128,160},{160,128},{192,224},{224,1... | collective-permute-start | bytes 1474568 | tf_op jit(solution)/shard_map/ppermute | solution.py:309
  129.2 14.7 %collective-permute-start.4 = (bf16[96,1280]{1,0:T(8,128)(2,1)S(1)}, bf16[96,1280]{1,0:T(8,128)(2,1)S(1)}, u32[]{:S(2)}, u32[]{:S(2)}) collective-permute-start(bf16[96,1280]{1,0:T(8,128)(2,1)S(1)} %copy-done.12), channel_id=1, source_target_pairs={{0,32},{32,0},{64,96},{96,64},{128,160},{160,128},{192,224},{224,1... | collective-permute-start | bytes 737288 | tf_op jit(solution)/shard_map/ppermute | solution.py:301

commit v4 on v3

--- a/solution.py
+++ b/solution.py
@@ -90,14 +90,24 @@
         column[:, to] = block[at + 2 * G : at + 2 * G + 1, :].astype(f32)
 
 
+def own_chunks(core):
+    chip = lax.div(lax.axis_index("ctx"), 2)
+    way = 1 - 2 * core
+
+    def chunk(hops, parity):
+        return 2 * lax.rem(chip + hops * way + CHIPS, CHIPS) + parity
+
+    pairs = [chunk(hops, parity) for hops in (1, 3, 2) for parity in range(2)]
+    return pairs[:4] + [chunk(4, core)] + pairs[4:] + [chunk(0, core)]
+
+
 def split(full, narrow, own, mate, first=0):
     core = lax.rem(lax.axis_index("ctx"), 2)
-    for z in range(CHIPS):
-        to = slice(first + z * LANE, first + (z + 1) * LANE)
-        own[:, to] = full[:, pl.ds(pl.multiple_of((2 * z + core) * LANE, LANE), LANE)]
-        mate[:, to] = full[:, pl.ds(pl.multiple_of((2 * z + 1 - core) * LANE, LANE), LANE)]
-    own[:, first + D // 2 : first + HALF] = narrow
-    mate[:, first + D // 2 : first + HALF] = narrow
+    for half, chunks in ((own, own_chunks(core)), (mate, own_chunks(1 - core))):
+        for i, chunk in enumerate(chunks):
+            at = pl.ds(pl.multiple_of(chunk * LANE, LANE), LANE)
+            half[:, first + i * LANE : first + (i + 1) * LANE] = full[:, at]
+        half[:, first + D // 2 : first + HALF] = narrow
 
 
 def forward(rows, wa, wb, column):
@@ -210,7 +220,8 @@
 
 
 def weight_kernel(
-    grads_own, grads_both, kept_own, kept_mate, one_own, one_mate, out, rows, hidden, grads, pre
+    grads_own, grads_both, kept_own, kept_mate, one_own, one_mate,
+    near, far, next_chip, own_chip, rows, hidden, grads, pre
 ):
     mate = pl.multiple_of((1 - lax.rem(lax.axis_index("ctx"), 2)) * SLOTS, SLOTS)
     kept = (kept_own[...], kept_mate[...], one_own[:, :HALF], one_mate[:, :HALF])
@@ -221,16 +232,27 @@
         grads[to, :], pre[to, :] = grad[i][:, : D // 2], grad[i][:, D // 2 :]
     part_in = over_rows(pre[...], rows[...])
     part_out = over_rows(hidden[...], grads[...])
-    for z in range(CHIPS):
-        at = slice(z * LANE, (z + 1) * LANE)
-        out[z, :G, :] = part_in[:, at].astype(bf16)
-        out[z, G:, :] = part_out[:, at].astype(bf16)
-
-
-def total_kernel(parts, grad_in, grad_out):
-    total = parts[0].astype(f32)
-    for z in range(1, CHIPS):
-        total = total + parts[z].astype(f32)
+    targets = [(near, i) for i in range(4)] + [(far, 0), (next_chip, 0), (next_chip, 1), (own_chip, 0)]
+    for i, (out, to) in enumerate(targets):
+        at = slice(i * LANE, (i + 1) * LANE)
+        out[to, :G, :] = part_in[:, at].astype(out.dtype)
+        out[to, G:, :] = part_out[:, at].astype(out.dtype)
+
+
+def relay_kernel(near, far, next_chip, same, cross, give):
+    core = lax.rem(lax.axis_index("ctx"), 2)
+    same[...] = (
+        next_chip[core] + near[2 + core].astype(f32) + far[0].astype(f32)
+    ).astype(bf16)
+    cross[...] = (next_chip[1 - core] + near[3 - core].astype(f32)).astype(bf16)
+    give[...] = near[1 - core]
+
+
+def total_kernel(own_chip, near, gives, same, cross, grad_in, grad_out):
+    core = lax.rem(lax.axis_index("ctx"), 2)
+    mate = pl.multiple_of((1 - core) * 2 * G, 2 * G)
+    total = own_chip[0] + near[core].astype(f32) + gives[pl.ds(mate, 2 * G), :].astype(f32)
+    total = total + same[...].astype(f32) + cross[...].astype(f32)
     grad_in[0] = total[:G, :].T
     grad_out[0] = total[G:, :]
 
@@ -279,18 +301,16 @@
     (leaving,) = call(dispatch_kernel, [((2 * EXPERTS * PEER, LANE), bf16)], [wide_two], room=60)(
         tokens, cotangent, ids
     )
-    passing = lax.ppermute(own, "ctx", around)
-    leaving, passing = lax.optimization_barrier((leaving, passing))
-    pairs = [passing]
-    passing = lax.ppermute(passing, "ctx", around)
-    pairs.append(passing)
-    passing = lax.ppermute(passing, "ctx", around)
-    pairs = [both_cores(pair) for pair in pairs]
+    two_on = [
+        (2 * z + c, 2 * ((z + 2 - 4 * c) % chips) + c) for z in range(chips) for c in range(2)
+    ]
+    one, two = lax.ppermute(own, "ctx", around), lax.ppermute(own, "ctx", two_on)
+    _, two = lax.optimization_barrier((leaving, two))
+    three, four = lax.ppermute(two, "ctx", around), lax.ppermute(two, "ctx", two_on)
+    pairs = [both_cores(one), both_cores(two), both_cores(three), four]
     picks = call(choose_kernel, [PICK, PICK])(ids)
-    passing, *rest = lax.optimization_barrier((passing, *pairs, *picks))
-    pairs, picks = rest[:2], rest[2:]
-    pairs += [both_cores(passing), lax.ppermute(passing, "ctx", around)]
     (columns,) = call(columns_kernel, [WEIGHTS[2]], cost=10 * 1150000000)(own, *pairs[:2])
+    columns, picks = lax.optimization_barrier((columns, picks))
     rows_zero, upstream_one = call(arrive_kernel, [DENSE, DENSE], [wide_two])(over_exp(leaving))
     mixed, positive, kept_own, kept_mate, gate, wa, wb, column = call(
         first_kernel,
@@ -314,12 +334,19 @@
         over_exp(leaving), wb, positive, gate
     )
     half, narrow = ((4 * SLOTS, D // 2), bf16), ((4 * SLOTS, G), bf16)
-    (pair,) = call(
-        weight_kernel, [((CHIPS, 2 * G, LANE), bf16)], [half, narrow, half, narrow]
+    chunk = (2 * G, LANE)
+    near, far, next_chip, own_chip = call(
+        weight_kernel,
+        [((4, *chunk), bf16), ((1, *chunk), bf16), ((2, *chunk), f32), ((1, *chunk), f32)],
+        [half, narrow, half, narrow],
     )(grads_own, both_cores(grads_mate), kept_own, kept_mate, one_own, one_mate)
-    columns = [[2 * z + c for z in range(chips)] for c in range(2)]
-    parts = lax.all_to_all(pair, "ctx", 0, 0, tiled=True, axis_index_groups=columns)
-    grad_in, grad_out = call(total_kernel, [((1, LANE, G), f32), ((1, G, LANE), f32)])(parts)
+    near, far = lax.ppermute(near, "ctx", around), lax.ppermute(far, "ctx", two_on)
+    same, cross, give = call(relay_kernel, [(chunk, bf16)] * 3)(near, far, next_chip)
+    same = lax.ppermute(same, "ctx", two_on)
+    cross = lax.ppermute(cross, "ctx", [(a, b + 1 - 2 * (b % 2)) for a, b in two_on])
+    grad_in, grad_out = call(total_kernel, [((1, LANE, G), f32), ((1, G, LANE), f32)])(
+        own_chip, near, both_cores(give), same, cross
+    )
     return (grad_in, grad_out)
 
 

time: 178 us -> 170 us (0.955)
  blocking collectives: 108 us -> 83.9 us
  starting transfers between devices: 36.6 us -> 47 us
  waiting for transfers between devices: 15.9 us -> 20.5 us
    all_to_all x1 -> x0, blocking collectives: 31.6 us -> none  [on_device(): lax.all_to_all(pair, 'ctx', 0, 0, tiled=True, axis_index_groups=columns)]
    ppermute x4 -> x8, starting transfers between devices: 15 us -> 25.3 us  [the longest x1 5.99 us: on_device(): lax.ppermute(cross, 'ctx', [(a, b + 1 - 2 * (b % 2)) for a, b in two_on])]
    ppermute x4 -> x8, waiting for transfers between devices: 1.3 us -> 10.4 us  [the longest x1 7.89 us: on_device(): lax.ppermute(far, 'ctx', two_on)]
    all_gather x5 -> x6, blocking collectives: 21.5 us -> 28.9 us  [both_cores(): lax.all_gather(value, 'ctx', axis=0, tiled=True, axis_index_groups=cores)]
    all_to_all x2, waiting for transfers between devices: 14.6 us -> 10.1 us  [over_exp(): return lax.all_to_all(shaped, 'exp', 0, 0, tiled=True).reshape(buffer.shape)]
  transfers between devices with their start and end apart: 8 -> 12, of which waited for: 3 -> 5; matrix products, arithmetic and copies ran while one was open for 0% -> 0% of each run, Pallas kernels for 3% -> 3%
where the time goes in v4:
time: 170 us; the launch traced here: 168 us
  blocking collectives  83.9 us (49%)
  starting transfers between devices  47 us (28%)
  waiting for transfers between devices  20.5 us (12%)
  Pallas kernels  15.7 us (9%)
    all_to_all x3, blocking collectives, over_exp(): return lax.all_to_all(shaped, 'exp', 0, 0, tiled=True).reshape(buffer.shape)  55 us
    all_gather x6, blocking collectives, both_cores(): lax.all_gather(value, 'ctx', axis=0, tiled=True, axis_index_groups=cores)  28.9 us
    all_to_all x2, starting transfers between devices, over_exp(): return lax.all_to_all(shaped, 'exp', 0, 0, tiled=True).reshape(buffer.shape)  15.7 us
    all_to_all x2, waiting for transfers between devices, over_exp(): return lax.all_to_all(shaped, 'exp', 0, 0, tiled=True).reshape(buffer.shape)  10.1 us
    ppermute x1, waiting for transfers between devices, on_device(): lax.ppermute(far, 'ctx', two_on)  7.89 us
    ppermute x1, starting transfers between devices, on_device(): lax.ppermute(cross, 'ctx', [(a, b + 1 - 2 * (b % 2)) for a, b in two_on])  5.99 us
    ppermute x1, starting transfers between devices, on_device(): lax.ppermute(own, 'ctx', two_on)  5.27 us
    ppermute x1, starting transfers between devices, on_device(): one_mate = lax.ppermute(one_mate, 'ctx', across)  4.05 us
  transfers between devices with their start and end apart: 12, of which 5 were waited for; matrix products, arithmetic and copies ran while one was open for 0% of the time, Pallas kernels for 3%

profile of v4, /device:TPU:1, one launch (start us, length us, event | category | flops | bytes accessed | tf_op | source)
XLA Modules:
  0.0 168.1 jit_solution(8225699041737469286)
XLA Ops:
  0.6 1.5 shard_map.77
  2.2 8.7 %all_gather.18.own = bf16[1056,128]{1,0:T(8,128)(2,1)S(1)} all-gather(bf16[528,128]{1,0:T(8,128)(2,1)} %shard_map.77), channel_id=1, replica_groups={{0,32},{64,96},{128,160},{192,224},{256,288},{320,352},{384,416},{448,4..., dimensions={0}, use_global_device_ids=true | all-gather | bytes 405504 | tf_op jit(solution)/shard_map/all_gather | solution.py:292
  10.9 5.3 %collective-permute-start.1 = (bf16[1056,128]{1,0:T(8,128)(2,1)S(1)}, bf16[1056,128]{1,0:T(8,128)(2,1)S(1)}, u32[]{:S(2)}, u32[]{:S(2)}) collective-permute-start(bf16[1056,128]{1,0:T(8,128)(2,1)S(1)} %all_gather.18.own), channel_id=1, source_target_pairs={{0,128},{32,416},{64,192},{96,480},{128,256},{160,32},{192,320},{2... | collective-permute-start | bytes 811016 | tf_op jit(solution)/shard_map/ppermute | solution.py:307
  16.2 2.2 %collective-permute-start = (bf16[1056,128]{1,0:T(8,128)(2,1)S(1)}, bf16[1056,128]{1,0:T(8,128)(2,1)S(1)}, u32[]{:S(2)}, u32[]{:S(2)}) collective-permute-start(bf16[1056,128]{1,0:T(8,128)(2,1)S(1)} %all_gather.18.own), channel_id=1, source_target_pairs={{0,64},{64,128},{128,192},{192,256},{256,320},{320,384},{384,448},... | collective-permute-start | bytes 811016 | tf_op jit(solution)/shard_map/ppermute | solution.py:307
  18.4 3.6 %shard_map.78 = bf16[3072,128]{1,0:T(8,128)(2,1)} custom-call(bf16[128,2048]{1,0:T(8,128)(2,1)} %tokens.3, bf16[128,2048]{1,0:T(8,128)(2,1)} %cotangent.3, s32[2,128]{1,0:T(2,128)} %bitcast.20), custom_call_target="tpu_custom_call" | custom-call | tf_op jit(solution)/shard_map/pallas_call | solution.py:301
  21.9 9.8 %all-to-all-start = ((bf16[32,96,128]{2,1,0:T(8,128)(2,1)}), bf16[32,96,128]{2,1,0:T(8,128)(2,1)S(1)}, u32[]{:S(2)}, u32[]{:S(2)}) async-start(bf16[32,96,128]{2,1,0:T(8,128)(2,1)} %bitcast.22), calls=%async_computation | async-start | bytes 1572864 | tf_op jit(solution)/shard_map/all_to_all | solution.py:283
  32.0 1.9 %collective-permute-start.3 = (bf16[1056,128]{1,0:T(8,128)(2,1)S(1)}, bf16[1056,128]{1,0:T(8,128)(2,1)S(1)}, u32[]{:S(2)}, u32[]{:S(2)}) collective-permute-start(bf16[1056,128]{1,0:T(8,128)(2,1)S(1)} %collective-permute-done.1), channel_id=1, source_target_pairs={{0,128},{32,416},{64,192},{96,480},{128,256},{160,32},{192,320},{2... | collective-permute-start | bytes 811016 | tf_op jit(solution)/shard_map/ppermute | solution.py:309
  33.9 2.2 %collective-permute-start.2 = (bf16[1056,128]{1,0:T(8,128)(2,1)S(1)}, bf16[1056,128]{1,0:T(8,128)(2,1)S(1)}, u32[]{:S(2)}, u32[]{:S(2)}) collective-permute-start(bf16[1056,128]{1,0:T(8,128)(2,1)S(1)} %collective-permute-done.1), channel_id=1, source_target_pairs={{0,64},{64,128},{128,192},{192,256},{256,320},{320,384},{384,448},... | collective-permute-start | bytes 811016 | tf_op jit(solution)/shard_map/ppermute | solution.py:309
  36.1 5.7 %all_gather.20.pair_2 = bf16[2112,128]{1,0:T(8,128)(2,1)S(1)} all-gather(bf16[1056,128]{1,0:T(8,128)(2,1)S(1)} %collective-permute-done.1), channel_id=1, replica_groups={{0,32},{64,96},{128,160},{192,224},{256,288},{320,352},{384,416},{448,4..., dimensions={0}, use_global_device_ids=true | all-gather | bytes 811008 | tf_op jit(solution)/shard_map/all_gather | solution.py:292
  41.8 2.2 %all_gather.19.pair_1 = bf16[2112,128]{1,0:T(8,128)(2,1)S(1)} all-gather(bf16[1056,128]{1,0:T(8,128)(2,1)S(1)} %collective-permute-done), channel_id=1, replica_groups={{0,32},{64,96},{128,160},{192,224},{256,288},{320,352},{384,416},{448,4..., dimensions={0}, use_global_device_ids=true | all-gather | bytes 811008 | tf_op jit(solution)/shard_map/all_gather | solution.py:292
  44.0 1.3 collective-permute-done.2
  45.2 4.3 %all_gather.21.pair_3 = bf16[2112,128]{1,0:T(8,128)(2,1)S(1)} all-gather(bf16[1056,128]{1,0:T(8,128)(2,1)S(1)} %collective-permute-done.2), channel_id=1, replica_groups={{0,32},{64,96},{128,160},{192,224},{256,288},{320,352},{384,416},{448,4..., dimensions={0}, use_global_device_ids=true | all-gather | bytes 811008 | tf_op jit(solution)/shard_map/all_gather | solution.py:292
  49.5 4.1 %all-to-all-done = bf16[32,96,128]{2,1,0:T(8,128)(2,1)S(1)} async-done(((bf16[32,96,128]{2,1,0:T(8,128)(2,1)}), bf16[32,96,128]{2,1,0:T(8,128)(2,1)S(1)}, u32[]{:S(2)}, u32[]{:S(2)}) %all-to-all-start) | async-done | bytes 786464 | tf_op jit(solution)/shard_map/all_to_all | solution.py:283
  54.6 1.3 shard_map.82
  56.0 19.2 %all_to_all.25 = bf16[32,48,128]{2,1,0:T(8,128)(2,1)S(1)} all-to-all(bf16[32,48,128]{2,1,0:T(8,128)(2,1)S(1)} %bitcast.17), channel_id=1, replica_groups=mesh['ctx'=16,'exp'=32] {'exp'}, dimensions={0} | all-to-all | bytes 786432 | tf_op jit(solution)/shard_map/all_to_all | solution.py:283
  75.2 1.1 shard_map.83
  76.3 17.6 %all_to_all.26 = bf16[32,48,128]{2,1,0:T(8,128)(2,1)S(1)} all-to-all(bf16[32,48,128]{2,1,0:T(8,128)(2,1)S(1)} %bitcast.19), channel_id=1, replica_groups=mesh['ctx'=16,'exp'=32] {'exp'}, dimensions={0} | all-to-all | bytes 786432 | tf_op jit(solution)/shard_map/all_to_all | solution.py:283
  93.9 2.7 %shard_map.84 = (bf16[1536,128]{1,0:T(8,128)(2,1)S(1)}, bf16[96,2560]{1,0:T(8,128)(2,1)S(1)}, bf16[96,2560]{1,0:T(8,128)(2,1)}) custom-call(bf16[1536,128]{1,0:T(8,128)(2,1)S(1)} %bitcast.16, bf16[96,2048]{1,0:T(8,128)(2,1)S(1)} %get-tuple-element.42.upstream, bf16[2048,256]{1,0:T(8,128)(2,1)S(1)} %get-tuple-element.43.wa, ...), custom_call_target="tpu_custom_call" | custom-call | tf_op jit(solution)/shard_map/pallas_call | solution.py:326
  96.6 18.2 %all_to_all.27 = bf16[32,48,128]{2,1,0:T(8,128)(2,1)S(1)} all-to-all(bf16[32,48,128]{2,1,0:T(8,128)(2,1)S(1)} %bitcast.18), channel_id=1, replica_groups=mesh['ctx'=16,'exp'=32] {'exp'}, dimensions={0} | all-to-all | bytes 786432 | tf_op jit(solution)/shard_map/all_to_all | solution.py:283
  114.8 1.9 %shard_map.85 = bf16[1536,128]{1,0:T(8,128)(2,1)} custom-call(bf16[128,2048]{1,0:T(8,128)(2,1)S(1)} %copy-done.1, f32[128,2048]{1,0:T(8,128)S(1)} %get-tuple-element.40.state, bf16[96,128]{1,0:T(8,128)(2,1)S(1)} %copy-done.3, bf16[96,128]{1,0:T(8,128)(2,1)S(1)} %copy-done.5, bf16[1536,128]{1,0:T(8,128)(2,1)S(1)} %bitcast.13), custom_call_target="tpu_custom_call" | custom-call | tf_op jit(solution)/shard_map/pallas_call | solution.py:330
  116.7 5.9 %all-to-all-start.4 = ((bf16[32,48,128]{2,1,0:T(8,128)(2,1)}), bf16[32,48,128]{2,1,0:T(8,128)(2,1)S(1)}, u32[]{:S(2)}, u32[]{:S(2)}) async-start(bf16[32,48,128]{2,1,0:T(8,128)(2,1)} %bitcast.10), calls=%async_computation.4 | async-start | bytes 786432 | tf_op jit(solution)/shard_map/all_to_all | solution.py:283
  122.7 4.1 %collective-permute-start.5 = (bf16[96,2560]{1,0:T(8,128)(2,1)}, bf16[96,2560]{1,0:T(8,128)(2,1)S(1)}, u32[]{:S(2)}, u32[]{:S(2)}) collective-permute-start(bf16[96,2560]{1,0:T(8,128)(2,1)} %get-tuple-element.54), channel_id=1, source_target_pairs={{0,32},{32,0},{64,96},{96,64},{128,160},{160,128},{192,224},{224,1... | collective-permute-start | bytes 1474568 | tf_op jit(solution)/shard_map/ppermute | solution.py:329
  126.8 1.9 %collective-permute-start.4 = (bf16[96,1280]{1,0:T(8,128)(2,1)S(1)}, bf16[96,1280]{1,0:T(8,128)(2,1)S(1)}, u32[]{:S(2)}, u32[]{:S(2)}) collective-permute-start(bf16[96,1280]{1,0:T(8,128)(2,1)S(1)} %copy-done.12), channel_id=1, source_target_pairs={{0,32},{32,0},{64,96},{96,64},{128,160},{160,128},{192,224},{224,1... | collective-permute-start | bytes 737288 | tf_op jit(solution)/shard_map/ppermute | solution.py:321
  128.7 6.0 %all-to-all-done.4 = bf16[32,48,128]{2,1,0:T(8,128)(2,1)S(1)} async-done(((bf16[32,48,128]{2,1,0:T(8,128)(2,1)}), bf16[32,48,128]{2,1,0:T(8,128)(2,1)S(1)}, u32[]{:S(2)}, u32[]{:S(2)}) %all-to-all-start.4) | async-done | bytes 393248 | tf_op jit(solution)/shard_map/all_to_all | solution.py:283
  135.6 6.0 %all_gather.22.grads_both = bf16[192,1280]{1,0:T(8,128)(2,1)S(1)} all-gather(bf16[96,1280]{1,0:T(8,128)(2,1)S(1)} %get-tuple-element.50), channel_id=1, replica_groups={{0,32},{64,96},{128,160},{192,224},{256,288},{320,352},{384,416},{448,4..., dimensions={0}, use_global_device_ids=true | all-gather | bytes 737280 | tf_op jit(solution)/shard_map/all_gather | solution.py:292
  142.3 1.9 %collective-permute-start.6 = (bf16[4,512,128]{2,1,0:T(8,128)(2,1)S(1)}, bf16[4,512,128]{2,1,0:T(8,128)(2,1)S(1)}, u32[]{:S(2)}, u32[]{:S(2)}) collective-permute-start(bf16[4,512,128]{2,1,0:T(8,128)(2,1)S(1)} %get-tuple-element.56), channel_id=1, source_target_pairs={{0,64},{64,128},{128,192},{192,256},{256,320},{320,384},{384,448},... | collective-permute-start | bytes 1572872 | tf_op jit(solution)/shard_map/ppermute | solution.py:343
  144.3 3.4 %collective-permute-start.7 = (bf16[1,512,128]{2,1,0:T(8,128)(2,1)S(1)}, bf16[1,512,128]{2,1,0:T(8,128)(2,1)S(1)}, u32[]{:S(2)}, u32[]{:S(2)}) collective-permute-start(bf16[1,512,128]{2,1,0:T(8,128)(2,1)S(1)} %get-tuple-element.57), channel_id=1, source_target_pairs={{0,128},{32,416},{64,192},{96,480},{128,256},{160,32},{192,320},{2... | collective-permute-start | bytes 393224 | tf_op jit(solution)/shard_map/ppermute | solution.py:343
  147.7 7.9 %collective-permute-done.7.far = bf16[1,512,128]{2,1,0:T(8,128)(2,1)S(1)} collective-permute-done((bf16[1,512,128]{2,1,0:T(8,128)(2,1)S(1)}, bf16[1,512,128]{2,1,0:T(8,128)(2,1)S(1)}, u32[]{:S(2)}, u32[]{:S(2)}) %collective-permute-start.7) | collective-permute-done | bytes 131104 | tf_op jit(solution)/shard_map/ppermute | solution.py:343
  155.6 2.4 %collective-permute-start.8 = (bf16[512,128]{1,0:T(8,128)(2,1)S(1)}, bf16[512,128]{1,0:T(8,128)(2,1)S(1)}, u32[]{:S(2)}, u32[]{:S(2)}) collective-permute-start(bf16[512,128]{1,0:T(8,128)(2,1)S(1)} %get-tuple-element.60), channel_id=1, source_target_pairs={{0,128},{32,416},{64,192},{96,480},{128,256},{160,32},{192,320},{2... | collective-permute-start | bytes 393224 | tf_op jit(solution)/shard_map/ppermute | solution.py:345
  158.1 6.0 %collective-permute-start.9 = (bf16[512,128]{1,0:T(8,128)(2,1)S(1)}, bf16[512,128]{1,0:T(8,128)(2,1)S(1)}, u32[]{:S(2)}, u32[]{:S(2)}) collective-permute-start(bf16[512,128]{1,0:T(8,128)(2,1)S(1)} %get-tuple-element.61), channel_id=1, source_target_pairs={{0,160},{32,384},{64,224},{96,448},{128,288},{160,0},{192,352},{22... | collective-permute-start | bytes 393224 | tf_op jit(solution)/shard_map/ppermute | solution.py:346
  164.0 2.0 %all_gather.23.gives = bf16[1024,128]{1,0:T(8,128)(2,1)S(1)} all-gather(bf16[512,128]{1,0:T(8,128)(2,1)S(1)} %get-tuple-element.59), channel_id=1, replica_groups={{0,32},{64,96},{128,160},{192,224},{256,288},{320,352},{384,416},{448,4..., dimensions={0}, use_global_device_ids=true | all-gather | bytes 393216 | tf_op jit(solution)/shard_map/all_gather | solution.py:292
  166.0 1.2 collective-permute-done.9.cross
  (40 shorter events, 3.7 us)
Async XLA Ops:
  10.9 21.1 %collective-permute-start.1 = (bf16[1056,128]{1,0:T(8,128)(2,1)S(1)}, bf16[1056,128]{1,0:T(8,128)(2,1)S(1)}, u32[]{:S(2)}, u32[]{:S(2)}) collective-permute-start(bf16[1056,128]{1,0:T(8,128)(2,1)S(1)} %all_gather.18.own), channel_id=1, source_target_pairs={{0,128},{32,416},{64,192},{96,480},{128,256},{160,32},{192,320},{2... | collective-permute-start | bytes 811016 | tf_op jit(solution)/shard_map/ppermute | solution.py:307
  16.2 25.6 %collective-permute-start = (bf16[1056,128]{1,0:T(8,128)(2,1)S(1)}, bf16[1056,128]{1,0:T(8,128)(2,1)S(1)}, u32[]{:S(2)}, u32[]{:S(2)}) collective-permute-start(bf16[1056,128]{1,0:T(8,128)(2,1)S(1)} %all_gather.18.own), channel_id=1, source_target_pairs={{0,64},{64,128},{128,192},{192,256},{256,320},{320,384},{384,448},... | collective-permute-start | bytes 811016 | tf_op jit(solution)/shard_map/ppermute | solution.py:307
  21.9 9.8 %copy-start.10 = (s32[2,128,1]{1,2,0:T(1,128)S(1)}, s32[2,128,1]{1,2,0:T(1,128)}, u32[]{:S(2)}) copy-start(s32[2,128,1]{1,2,0:T(1,128)} %param.8) | copy-start | bytes 3076
  21.9 31.7 %all-to-all-start = ((bf16[32,96,128]{2,1,0:T(8,128)(2,1)}), bf16[32,96,128]{2,1,0:T(8,128)(2,1)S(1)}, u32[]{:S(2)}, u32[]{:S(2)}) async-start(bf16[32,96,128]{2,1,0:T(8,128)(2,1)} %bitcast.22), calls=%async_computation | async-start | bytes 1572864 | tf_op jit(solution)/shard_map/all_to_all | solution.py:283
  31.9 9.8 %copy-start.2 = (bf16[96,128]{1,0:T(8,128)(2,1)}, bf16[96,128]{1,0:T(8,128)(2,1)S(1)}, u32[]{:S(2)}) copy-start(bf16[96,128]{1,0:T(8,128)(2,1)S(1)} %get-tuple-element.35.pick_zero) | copy-start | bytes 73732
  31.9 9.8 %copy-start.4 = (bf16[96,128]{1,0:T(8,128)(2,1)}, bf16[96,128]{1,0:T(8,128)(2,1)S(1)}, u32[]{:S(2)}) copy-start(bf16[96,128]{1,0:T(8,128)(2,1)S(1)} %get-tuple-element.36.pick_one) | copy-start | bytes 73732
  32.0 22.7 %collective-permute-start.3 = (bf16[1056,128]{1,0:T(8,128)(2,1)S(1)}, bf16[1056,128]{1,0:T(8,128)(2,1)S(1)}, u32[]{:S(2)}, u32[]{:S(2)}) collective-permute-start(bf16[1056,128]{1,0:T(8,128)(2,1)S(1)} %collective-permute-done.1), channel_id=1, source_target_pairs={{0,128},{32,416},{64,192},{96,480},{128,256},{160,32},{192,320},{2... | collective-permute-start | bytes 811016 | tf_op jit(solution)/shard_map/ppermute | solution.py:309
  33.9 11.4 %collective-permute-start.2 = (bf16[1056,128]{1,0:T(8,128)(2,1)S(1)}, bf16[1056,128]{1,0:T(8,128)(2,1)S(1)}, u32[]{:S(2)}, u32[]{:S(2)}) collective-permute-start(bf16[1056,128]{1,0:T(8,128)(2,1)S(1)} %collective-permute-done.1), channel_id=1, source_target_pairs={{0,64},{64,128},{128,192},{192,256},{256,320},{320,384},{384,448},... | collective-permute-start | bytes 811016 | tf_op jit(solution)/shard_map/ppermute | solution.py:309
  44.0 5.6 %copy-start.8 = (f32[1,2048]{1,0:T(1,128)}, f32[1,2048]{1,0:T(1,128)S(1)}, u32[]{:S(2)}) copy-start(f32[1,2048]{1,0:T(1,128)S(1)} %shard_map.79.columns) | copy-start | bytes 24580
  53.6 1.0 copy-start.9
  55.9 19.3 %copy-start.6 = (f32[96,128]{1,0:T(8,128)}, f32[96,128]{1,0:T(8,128)S(1)}, u32[]{:S(2)}) copy-start(f32[96,128]{1,0:T(8,128)S(1)} %get-tuple-element.48.gate) | copy-start | bytes 147460
  56.0 19.3 %copy-start.11 = (bf16[96,1280]{1,0:T(8,128)(2,1)}, bf16[96,1280]{1,0:T(8,128)(2,1)S(1)}, u32[]{:S(2)}) copy-start(bf16[96,1280]{1,0:T(8,128)(2,1)S(1)} %get-tuple-element.52) | copy-start | bytes 737284
  56.0 19.2 %copy-start = (bf16[128,2048]{1,0:T(8,128)(2,1)S(1)}, bf16[128,2048]{1,0:T(8,128)(2,1)}, u32[]{:S(2)}) copy-start(bf16[128,2048]{1,0:T(8,128)(2,1)} %tokens.3) | copy-start | bytes 1572868
  56.0 19.2 %copy-start.3 = (bf16[96,128]{1,0:T(8,128)(2,1)S(1)}, bf16[96,128]{1,0:T(8,128)(2,1)}, u32[]{:S(2)}) copy-start(bf16[96,128]{1,0:T(8,128)(2,1)} %copy-done.2) | copy-start | bytes 73732
  56.0 19.2 %copy-start.5 = (bf16[96,128]{1,0:T(8,128)(2,1)S(1)}, bf16[96,128]{1,0:T(8,128)(2,1)}, u32[]{:S(2)}) copy-start(bf16[96,128]{1,0:T(8,128)(2,1)} %copy-done.4) | copy-start | bytes 73732
  96.6 18.2 %copy-start.1 = (bf16[128,2048]{1,0:T(8,128)(2,1)S(1)}, bf16[128,2048]{1,0:T(8,128)(2,1)}, u32[]{:S(2)}) copy-start(bf16[128,2048]{1,0:T(8,128)(2,1)} %cotangent.3) | copy-start | bytes 1572868
  116.7 10.0 %copy-start.12 = (bf16[96,1280]{1,0:T(8,128)(2,1)S(1)}, bf16[96,1280]{1,0:T(8,128)(2,1)}, u32[]{:S(2)}) copy-start(bf16[96,1280]{1,0:T(8,128)(2,1)} %copy-done.11) | copy-start | bytes 737284
  116.7 17.9 %copy-start.7 = (f32[96,128]{1,0:T(8,128)S(1)}, f32[96,128]{1,0:T(8,128)}, u32[]{:S(2)}) copy-start(f32[96,128]{1,0:T(8,128)} %copy-done.6) | copy-start | bytes 147460
  116.7 17.9 %all-to-all-start.4 = ((bf16[32,48,128]{2,1,0:T(8,128)(2,1)}), bf16[32,48,128]{2,1,0:T(8,128)(2,1)S(1)}, u32[]{:S(2)}, u32[]{:S(2)}) async-start(bf16[32,48,128]{2,1,0:T(8,128)(2,1)} %bitcast.10), calls=%async_computation.4 | async-start | bytes 786432 | tf_op jit(solution)/shard_map/all_to_all | solution.py:283
  122.7 18.9 %collective-permute-start.5 = (bf16[96,2560]{1,0:T(8,128)(2,1)}, bf16[96,2560]{1,0:T(8,128)(2,1)S(1)}, u32[]{:S(2)}, u32[]{:S(2)}) collective-permute-start(bf16[96,2560]{1,0:T(8,128)(2,1)} %get-tuple-element.54), channel_id=1, source_target_pairs={{0,32},{32,0},{64,96},{96,64},{128,160},{160,128},{192,224},{224,1... | collective-permute-start | bytes 1474568 | tf_op jit(solution)/shard_map/ppermute | solution.py:329
  126.8 14.8 %collective-permute-start.4 = (bf16[96,1280]{1,0:T(8,128)(2,1)S(1)}, bf16[96,1280]{1,0:T(8,128)(2,1)S(1)}, u32[]{:S(2)}, u32[]{:S(2)}) collective-permute-start(bf16[96,1280]{1,0:T(8,128)(2,1)S(1)} %copy-done.12), channel_id=1, source_target_pairs={{0,32},{32,0},{64,96},{96,64},{128,160},{160,128},{192,224},{224,1... | collective-permute-start | bytes 737288 | tf_op jit(solution)/shard_map/ppermute | solution.py:321
  142.3 13.2 %collective-permute-start.6 = (bf16[4,512,128]{2,1,0:T(8,128)(2,1)S(1)}, bf16[4,512,128]{2,1,0:T(8,128)(2,1)S(1)}, u32[]{:S(2)}, u32[]{:S(2)}) collective-permute-start(bf16[4,512,128]{2,1,0:T(8,128)(2,1)S(1)} %get-tuple-element.56), channel_id=1, source_target_pairs={{0,64},{64,128},{128,192},{192,256},{256,320},{320,384},{384,448},... | collective-permute-start | bytes 1572872 | tf_op jit(solution)/shard_map/ppermute | solution.py:343
  144.3 11.3 %collective-permute-start.7 = (bf16[1,512,128]{2,1,0:T(8,128)(2,1)S(1)}, bf16[1,512,128]{2,1,0:T(8,128)(2,1)S(1)}, u32[]{:S(2)}, u32[]{:S(2)}) collective-permute-start(bf16[1,512,128]{2,1,0:T(8,128)(2,1)S(1)} %get-tuple-element.57), channel_id=1, source_target_pairs={{0,128},{32,416},{64,192},{96,480},{128,256},{160,32},{192,320},{2... | collective-permute-start | bytes 393224 | tf_op jit(solution)/shard_map/ppermute | solution.py:343
  155.6 10.4 %collective-permute-start.8 = (bf16[512,128]{1,0:T(8,128)(2,1)S(1)}, bf16[512,128]{1,0:T(8,128)(2,1)S(1)}, u32[]{:S(2)}, u32[]{:S(2)}) collective-permute-start(bf16[512,128]{1,0:T(8,128)(2,1)S(1)} %get-tuple-element.60), channel_id=1, source_target_pairs={{0,128},{32,416},{64,192},{96,480},{128,256},{160,32},{192,320},{2... | collective-permute-start | bytes 393224 | tf_op jit(solution)/shard_map/ppermute | solution.py:345
  158.1 9.2 %collective-permute-start.9 = (bf16[512,128]{1,0:T(8,128)(2,1)S(1)}, bf16[512,128]{1,0:T(8,128)(2,1)S(1)}, u32[]{:S(2)}, u32[]{:S(2)}) collective-permute-start(bf16[512,128]{1,0:T(8,128)(2,1)S(1)} %get-tuple-element.61), channel_id=1, source_target_pairs={{0,160},{32,384},{64,224},{96,448},{128,288},{160,0},{192,352},{22... | collective-permute-start | bytes 393224 | tf_op jit(solution)/shard_map/ppermute | solution.py:346

commit v5 on v4

--- a/solution.py
+++ b/solution.py
@@ -130,11 +130,29 @@
     return upper, grad_expert, grad_pre
 
 
-def dispatch_kernel(tokens, cotangent, ids, out, wide):
-    unit, _ = normalize(tokens[...].astype(f32))
-    pack(to_slots(choose(ids[0:1, :]), unit.astype(bf16)), wide, 2 * PEER, 0)
-    pack(to_slots(choose(ids[1:2, :]), cotangent[...]), wide, 2 * PEER, PEER)
-    out[...] = wide[...].astype(bf16)
+def dispatch_kernel(tokens, cotangent, ids, out, first, second, wide, packed, sems):
+    loads = []
+    for i, (source, target) in enumerate(((tokens, first), (cotangent, second))):
+        for j in range(4):
+            rows = pl.ds(j * TOK // 4, TOK // 4)
+            copy = pltpu.make_async_copy(source.at[rows, :], target.at[rows, :], sems.at[4 * i + j])
+            copy.start()
+            loads.append(copy)
+    picks = choose(ids[0:1, :]), choose(ids[1:2, :])
+    stores = []
+    for i in range(2):
+        for copy in loads[4 * i : 4 * i + 4]:
+            copy.wait()
+        rows = second[...] if i else normalize(first[...].astype(f32))[0].astype(bf16)
+        pack(to_slots(picks[i], rows), wide.at[i])
+        packed[i] = wide[i].reshape(EXPERTS, PEER, LANE).astype(bf16)
+        copy = pltpu.make_async_copy(
+            packed.at[i], out.at[:, pl.ds(i * PEER, PEER), :], sems.at[8 + i]
+        )
+        copy.start()
+        stores.append(copy)
+    for copy in stores:
+        copy.wait()
 
 
 def arrive_kernel(taken, rows, upstream, wide):
@@ -178,11 +196,11 @@
 
 
 def second_kernel(
-    taken, upstream, wa, wb, column, out, own, mate, wide, dense, expert
+    taken, upstream, wa, wb, column, out, rows, hidden_out, expert, pre, wide
 ):
     wide[...] = taken[...].astype(f32)
-    unpack(wide, dense)
-    positive, hidden, expert_out, gate = forward(dense[...], wa, wb, column)
+    unpack(wide, rows)
+    positive, hidden, expert_out, gate = forward(rows[...], wa, wb, column)
     upper, grad_expert, grad_pre = backward(upstream[...], wb, positive, gate)
     grad_gate = jnp.sum(upper * expert_out, axis=1, keepdims=True)
     grad_logit = grad_gate * gate * (1.0 - gate)
@@ -191,9 +209,14 @@
     )
     pack(flowing + grad_logit * column[...], wide)
     out[...] = wide[...].astype(bf16)
+    hidden_out[...] = hidden
     expert[...] = grad_expert
-    split(dense, hidden, own, mate)
-    split(expert, grad_pre, own, mate, HALF)
+    pre[...] = grad_pre
+
+
+def split_kernel(rows, hidden, expert, pre, own, mate):
+    split(rows, hidden[...], own, mate)
+    split(expert, pre[...], own, mate, HALF)
 
 
 def return_kernel(cotangent, state, pick_zero, pick_one, taken, out, wide, dense):
@@ -298,18 +321,32 @@
     )
     own = both_cores(share)
     wide_two = ((2 * EXPERTS * PEER, LANE), f32)
-    (leaving,) = call(dispatch_kernel, [((2 * EXPERTS * PEER, LANE), bf16)], [wide_two], room=60)(
-        tokens, cotangent, ids
-    )
+    far_away = pl.BlockSpec(memory_space=pl.ANY)
+    leaving = pl.pallas_call(
+        dispatch_kernel,
+        out_shape=jax.ShapeDtypeStruct((EXPERTS, 2 * PEER, LANE), bf16),
+        in_specs=[far_away, far_away, pl.BlockSpec(memory_space=pltpu.VMEM)],
+        out_specs=far_away,
+        scratch_shapes=[
+            pltpu.VMEM((TOK, D), bf16),
+            pltpu.VMEM((TOK, D), bf16),
+            pltpu.VMEM((2, EXPERTS * PEER, LANE), f32),
+            pltpu.VMEM((2, EXPERTS, PEER, LANE), bf16),
+            pltpu.SemaphoreType.DMA((10,)),
+        ],
+        compiler_params=pltpu.CompilerParams(vmem_limit_bytes=60 << 20),
+    )(tokens, cotangent, ids).reshape(2 * EXPERTS * PEER, LANE)
     two_on = [
         (2 * z + c, 2 * ((z + 2 - 4 * c) % chips) + c) for z in range(chips) for c in range(2)
     ]
-    one, two = lax.ppermute(own, "ctx", around), lax.ppermute(own, "ctx", two_on)
+    two = lax.ppermute(own, "ctx", two_on)
+    later, two = lax.optimization_barrier((own, two))
     _, two = lax.optimization_barrier((leaving, two))
+    one = lax.ppermute(later, "ctx", around)
     three, four = lax.ppermute(two, "ctx", around), lax.ppermute(two, "ctx", two_on)
     pairs = [both_cores(one), both_cores(two), both_cores(three), four]
     picks = call(choose_kernel, [PICK, PICK])(ids)
-    (columns,) = call(columns_kernel, [WEIGHTS[2]], cost=10 * 1150000000)(own, *pairs[:2])
+    (columns,) = call(columns_kernel, [WEIGHTS[2]], cost=8 * 1150000000)(own, *pairs[:2])
     columns, picks = lax.optimization_barrier((columns, picks))
     rows_zero, upstream_one = call(arrive_kernel, [DENSE, DENSE], [wide_two])(over_exp(leaving))
     mixed, positive, kept_own, kept_mate, gate, wa, wb, column = call(
@@ -323,9 +360,11 @@
         tokens, *picks, over_exp(mixed)
     )
     double = ((SLOTS, 2 * HALF), bf16)
-    leaving, one_own, one_mate = call(
-        second_kernel, [PACKED, double, double], [WIDE, DENSE, DENSE]
-    )(over_exp(leaving), upstream_one, wa, wb, column)
+    slim = ((SLOTS, G), bf16)
+    leaving, *second = call(second_kernel, [PACKED, DENSE, slim, DENSE, slim], [WIDE])(
+        over_exp(leaving), upstream_one, wa, wb, column
+    )
+    one_own, one_mate = call(split_kernel, [double, double])(*second)
     one_mate = lax.ppermute(one_mate, "ctx", across)
     (leaving,) = call(return_kernel, [PACKED], [WIDE, DENSE])(
         cotangent, state_one, *picks, over_exp(leaving)

time: 170 us -> 168 us (0.988)
  waiting for transfers between devices: 20.5 us -> 15.9 us
  blocking collectives: 83.9 us -> 87 us
    all_to_all x2, waiting for transfers between devices: 10.1 us -> 5.26 us  [over_exp(): return lax.all_to_all(shaped, 'exp', 0, 0, tiled=True).reshape(buffer.shape)]
    all_to_all x3, blocking collectives: 55 us -> 58.9 us  [over_exp(): return lax.all_to_all(shaped, 'exp', 0, 0, tiled=True).reshape(buffer.shape)]
    pallas_call x3 -> x4, Pallas kernels: 6.26 us -> 6.48 us  [the longest x1 3.63 us: on_device(): pl.pallas_call(dispatch_kernel, out_shape=jax.ShapeDtypeStruct((EXPERTS,...]
  transfers between devices with their start and end apart: 12 -> 12, of which waited for: 5 -> 5; matrix products, arithmetic and copies ran while one was open for 0% -> 0% of each run, Pallas kernels for 3% -> 4%
where the time goes in v5:
time: 168 us; the launch traced here: 167 us
  blocking collectives  87 us (52%)
  starting transfers between devices  47.4 us (28%)
  Pallas kernels  15.9 us (9%)
  waiting for transfers between devices  15.9 us (9%)
    all_to_all x3, blocking collectives, over_exp(): return lax.all_to_all(shaped, 'exp', 0, 0, tiled=True).reshape(buffer.shape)  58.9 us
    all_gather x6, blocking collectives, both_cores(): lax.all_gather(value, 'ctx', axis=0, tiled=True, axis_index_groups=cores)  28.1 us
    all_to_all x2, starting transfers between devices, over_exp(): return lax.all_to_all(shaped, 'exp', 0, 0, tiled=True).reshape(buffer.shape)  15.5 us
    ppermute x1, waiting for transfers between devices, on_device(): lax.ppermute(far, 'ctx', two_on)  7.24 us
    ppermute x1, starting transfers between devices, on_device(): lax.ppermute(cross, 'ctx', [(a, b + 1 - 2 * (b % 2)) for a, b in two_on])  5.43 us
    ppermute x1, starting transfers between devices, on_device(): two = lax.ppermute(own, 'ctx', two_on)  5.27 us
    all_to_all x2, waiting for transfers between devices, over_exp(): return lax.all_to_all(shaped, 'exp', 0, 0, tiled=True).reshape(buffer.shape)  5.26 us
    ppermute x1, starting transfers between devices, on_device(): lax.ppermute(far, 'ctx', two_on)  4.39 us
  transfers between devices with their start and end apart: 12, of which 5 were waited for; matrix products, arithmetic and copies ran while one was open for 0% of the time, Pallas kernels for 4%

profile of v5, /device:TPU:1, one launch (start us, length us, event | category | flops | bytes accessed | tf_op | source)
XLA Modules:
  0.0 167.3 jit_solution(16869519125966351944)
XLA Ops:
  0.6 1.5 shard_map.77
  2.2 8.7 %all_gather.18.own = bf16[1056,128]{1,0:T(8,128)(2,1)S(1)} all-gather(bf16[528,128]{1,0:T(8,128)(2,1)} %shard_map.77), channel_id=1, replica_groups={{0,32},{64,96},{128,160},{192,224},{256,288},{320,352},{384,416},{448,4..., dimensions={0}, use_global_device_ids=true | all-gather | bytes 405504 | tf_op jit(solution)/shard_map/all_gather | solution.py:315
  10.9 5.3 %collective-permute-start = (bf16[1056,128]{1,0:T(8,128)(2,1)S(1)}, bf16[1056,128]{1,0:T(8,128)(2,1)S(1)}, u32[]{:S(2)}, u32[]{:S(2)}) collective-permute-start(bf16[1056,128]{1,0:T(8,128)(2,1)S(1)} %all_gather.18.own), channel_id=1, source_target_pairs={{0,128},{32,416},{64,192},{96,480},{128,256},{160,32},{192,320},{2... | collective-permute-start | bytes 811016 | tf_op jit(solution)/shard_map/ppermute | solution.py:342
  16.2 3.6 %shard_map.80 = bf16[32,96,128]{2,1,0:T(8,128)(2,1)} custom-call(bf16[128,2048]{1,0:T(8,128)(2,1)} %tokens.3, bf16[128,2048]{1,0:T(8,128)(2,1)} %cotangent.3, s32[2,128]{1,0:T(2,128)} %bitcast.19), custom_call_target="tpu_custom_call" | custom-call | tf_op jit(solution)/shard_map/pallas_call | solution.py:325
  19.8 9.7 %all-to-all-start = ((bf16[32,96,128]{2,1,0:T(8,128)(2,1)}), bf16[32,96,128]{2,1,0:T(8,128)(2,1)S(1)}, u32[]{:S(2)}, u32[]{:S(2)}) async-start(bf16[32,96,128]{2,1,0:T(8,128)(2,1)} %shard_map.80), calls=%async_computation | async-start | bytes 1572864 | tf_op jit(solution)/shard_map/all_to_all | solution.py:306
  29.5 2.2 %collective-permute-start.1 = (bf16[1056,128]{1,0:T(8,128)(2,1)S(1)}, bf16[1056,128]{1,0:T(8,128)(2,1)S(1)}, u32[]{:S(2)}, u32[]{:S(2)}) collective-permute-start(bf16[1056,128]{1,0:T(8,128)(2,1)S(1)} %all_gather.18.own), channel_id=1, source_target_pairs={{0,64},{64,128},{128,192},{192,256},{256,320},{320,384},{384,448},... | collective-permute-start | bytes 811016 | tf_op jit(solution)/shard_map/ppermute | solution.py:345
  31.9 1.9 %collective-permute-start.3 = (bf16[1056,128]{1,0:T(8,128)(2,1)S(1)}, bf16[1056,128]{1,0:T(8,128)(2,1)S(1)}, u32[]{:S(2)}, u32[]{:S(2)}) collective-permute-start(bf16[1056,128]{1,0:T(8,128)(2,1)S(1)} %collective-permute-done), channel_id=1, source_target_pairs={{0,128},{32,416},{64,192},{96,480},{128,256},{160,32},{192,320},{2... | collective-permute-start | bytes 811016 | tf_op jit(solution)/shard_map/ppermute | solution.py:346
  33.9 2.2 %collective-permute-start.2 = (bf16[1056,128]{1,0:T(8,128)(2,1)S(1)}, bf16[1056,128]{1,0:T(8,128)(2,1)S(1)}, u32[]{:S(2)}, u32[]{:S(2)}) collective-permute-start(bf16[1056,128]{1,0:T(8,128)(2,1)S(1)} %collective-permute-done), channel_id=1, source_target_pairs={{0,64},{64,128},{128,192},{192,256},{256,320},{320,384},{384,448},... | collective-permute-start | bytes 811016 | tf_op jit(solution)/shard_map/ppermute | solution.py:346
  36.1 5.6 %all_gather.20.pair_2 = bf16[2112,128]{1,0:T(8,128)(2,1)S(1)} all-gather(bf16[1056,128]{1,0:T(8,128)(2,1)S(1)} %collective-permute-done), channel_id=1, replica_groups={{0,32},{64,96},{128,160},{192,224},{256,288},{320,352},{384,416},{448,4..., dimensions={0}, use_global_device_ids=true | all-gather | bytes 811008 | tf_op jit(solution)/shard_map/all_gather | solution.py:315
  41.7 2.2 %all_gather.19.pair_1 = bf16[2112,128]{1,0:T(8,128)(2,1)S(1)} all-gather(bf16[1056,128]{1,0:T(8,128)(2,1)S(1)} %collective-permute-done.1), channel_id=1, replica_groups={{0,32},{64,96},{128,160},{192,224},{256,288},{320,352},{384,416},{448,4..., dimensions={0}, use_global_device_ids=true | all-gather | bytes 811008 | tf_op jit(solution)/shard_map/all_gather | solution.py:315
  43.9 1.8 %collective-permute-done.2 = bf16[1056,128]{1,0:T(8,128)(2,1)S(1)} collective-permute-done((bf16[1056,128]{1,0:T(8,128)(2,1)S(1)}, bf16[1056,128]{1,0:T(8,128)(2,1)S(1)}, u32[]{:S(2)}, u32[]{:S(2)}) %collective-permute-start.2) | collective-permute-done | bytes 270368 | tf_op jit(solution)/shard_map/ppermute | solution.py:346
  45.7 3.6 %all_gather.21.pair_3 = bf16[2112,128]{1,0:T(8,128)(2,1)S(1)} all-gather(bf16[1056,128]{1,0:T(8,128)(2,1)S(1)} %collective-permute-done.2), channel_id=1, replica_groups={{0,32},{64,96},{128,160},{192,224},{256,288},{320,352},{384,416},{448,4..., dimensions={0}, use_global_device_ids=true | all-gather | bytes 811008 | tf_op jit(solution)/shard_map/all_gather | solution.py:315
  49.6 1.0 shard_map.81
  50.6 1.3 shard_map.82
  51.9 23.0 %all_to_all.25 = bf16[32,48,128]{2,1,0:T(8,128)(2,1)S(1)} all-to-all(bf16[32,48,128]{2,1,0:T(8,128)(2,1)S(1)} %bitcast.16), channel_id=1, replica_groups=mesh['ctx'=16,'exp'=32] {'exp'}, dimensions={0} | all-to-all | bytes 786432 | tf_op jit(solution)/shard_map/all_to_all | solution.py:306
  75.0 1.1 shard_map.83
  76.1 17.6 %all_to_all.26 = bf16[32,48,128]{2,1,0:T(8,128)(2,1)S(1)} all-to-all(bf16[32,48,128]{2,1,0:T(8,128)(2,1)S(1)} %bitcast.18), channel_id=1, replica_groups=mesh['ctx'=16,'exp'=32] {'exp'}, dimensions={0} | all-to-all | bytes 786432 | tf_op jit(solution)/shard_map/all_to_all | solution.py:306
  93.7 1.8 %shard_map.84 = (bf16[1536,128]{1,0:T(8,128)(2,1)S(1)}, bf16[96,2048]{1,0:T(8,128)(2,1)S(1)}, bf16[96,256]{1,0:T(8,128)(2,1)S(1)}, bf16[96,2048]{1,0:T(8,128)(2,1)S(1)}, bf16[96,256]{1,0:T(8,128)(2,1)S(1)}) custom-call(bf16[1536,128]{1,0:T(8,128)(2,1)S(1)} %bitcast.15, bf16[96,2048]{1,0:T(8,128)(2,1)S(1)} %get-tuple-element.48.upstream, ...), custom_call_target="tpu_custom_call" | custom-call | tf_op jit(solution)/shard_map/pallas_call | solution.py:364
  95.6 18.2 %all_to_all.27 = bf16[32,48,128]{2,1,0:T(8,128)(2,1)S(1)} all-to-all(bf16[32,48,128]{2,1,0:T(8,128)(2,1)S(1)} %bitcast.17), channel_id=1, replica_groups=mesh['ctx'=16,'exp'=32] {'exp'}, dimensions={0} | all-to-all | bytes 786432 | tf_op jit(solution)/shard_map/all_to_all | solution.py:306
  113.8 1.9 %shard_map.85 = bf16[1536,128]{1,0:T(8,128)(2,1)} custom-call(bf16[128,2048]{1,0:T(8,128)(2,1)S(1)} %copy-done.1, f32[128,2048]{1,0:T(8,128)S(1)} %get-tuple-element.46.state, bf16[96,128]{1,0:T(8,128)(2,1)S(1)} %copy-done.3, bf16[96,128]{1,0:T(8,128)(2,1)S(1)} %copy-done.5, bf16[1536,128]{1,0:T(8,128)(2,1)S(1)} %bitcast.12), custom_call_target="tpu_custom_call" | custom-call | tf_op jit(solution)/shard_map/pallas_call | solution.py:369
  115.7 5.8 %all-to-all-start.4 = ((bf16[32,48,128]{2,1,0:T(8,128)(2,1)}), bf16[32,48,128]{2,1,0:T(8,128)(2,1)S(1)}, u32[]{:S(2)}, u32[]{:S(2)}) async-start(bf16[32,48,128]{2,1,0:T(8,128)(2,1)} %bitcast.9), calls=%async_computation.4 | async-start | bytes 786432 | tf_op jit(solution)/shard_map/all_to_all | solution.py:306
  122.5 4.0 %collective-permute-start.5 = (bf16[96,2560]{1,0:T(8,128)(2,1)}, bf16[96,2560]{1,0:T(8,128)(2,1)S(1)}, u32[]{:S(2)}, u32[]{:S(2)}) collective-permute-start(bf16[96,2560]{1,0:T(8,128)(2,1)} %get-tuple-element.64), channel_id=1, source_target_pairs={{0,32},{32,0},{64,96},{96,64},{128,160},{160,128},{192,224},{224,1... | collective-permute-start | bytes 1474568 | tf_op jit(solution)/shard_map/ppermute | solution.py:368
  126.6 1.9 %collective-permute-start.4 = (bf16[96,1280]{1,0:T(8,128)(2,1)S(1)}, bf16[96,1280]{1,0:T(8,128)(2,1)S(1)}, u32[]{:S(2)}, u32[]{:S(2)}) collective-permute-start(bf16[96,1280]{1,0:T(8,128)(2,1)S(1)} %copy-done.12), channel_id=1, source_target_pairs={{0,32},{32,0},{64,96},{96,64},{128,160},{160,128},{192,224},{224,1... | collective-permute-start | bytes 737288 | tf_op jit(solution)/shard_map/ppermute | solution.py:358
  128.5 5.0 %all-to-all-done.4 = bf16[32,48,128]{2,1,0:T(8,128)(2,1)S(1)} async-done(((bf16[32,48,128]{2,1,0:T(8,128)(2,1)}), bf16[32,48,128]{2,1,0:T(8,128)(2,1)S(1)}, u32[]{:S(2)}, u32[]{:S(2)}) %all-to-all-start.4) | async-done | bytes 393248 | tf_op jit(solution)/shard_map/all_to_all | solution.py:306
  134.4 6.0 %all_gather.22.grads_both = bf16[192,1280]{1,0:T(8,128)(2,1)S(1)} all-gather(bf16[96,1280]{1,0:T(8,128)(2,1)S(1)} %get-tuple-element.56), channel_id=1, replica_groups={{0,32},{64,96},{128,160},{192,224},{256,288},{320,352},{384,416},{448,4..., dimensions={0}, use_global_device_ids=true | all-gather | bytes 737280 | tf_op jit(solution)/shard_map/all_gather | solution.py:315
  141.2 1.9 %collective-permute-start.6 = (bf16[4,512,128]{2,1,0:T(8,128)(2,1)S(1)}, bf16[4,512,128]{2,1,0:T(8,128)(2,1)S(1)}, u32[]{:S(2)}, u32[]{:S(2)}) collective-permute-start(bf16[4,512,128]{2,1,0:T(8,128)(2,1)S(1)} %get-tuple-element.66), channel_id=1, source_target_pairs={{0,64},{64,128},{128,192},{192,256},{256,320},{320,384},{384,448},... | collective-permute-start | bytes 1572872 | tf_op jit(solution)/shard_map/ppermute | solution.py:382
  143.1 4.4 %collective-permute-start.7 = (bf16[1,512,128]{2,1,0:T(8,128)(2,1)S(1)}, bf16[1,512,128]{2,1,0:T(8,128)(2,1)S(1)}, u32[]{:S(2)}, u32[]{:S(2)}) collective-permute-start(bf16[1,512,128]{2,1,0:T(8,128)(2,1)S(1)} %get-tuple-element.67), channel_id=1, source_target_pairs={{0,128},{32,416},{64,192},{96,480},{128,256},{160,32},{192,320},{2... | collective-permute-start | bytes 393224 | tf_op jit(solution)/shard_map/ppermute | solution.py:382
  147.5 7.2 %collective-permute-done.7.far = bf16[1,512,128]{2,1,0:T(8,128)(2,1)S(1)} collective-permute-done((bf16[1,512,128]{2,1,0:T(8,128)(2,1)S(1)}, bf16[1,512,128]{2,1,0:T(8,128)(2,1)S(1)}, u32[]{:S(2)}, u32[]{:S(2)}) %collective-permute-start.7) | collective-permute-done | bytes 131104 | tf_op jit(solution)/shard_map/ppermute | solution.py:382
  154.8 2.6 %collective-permute-start.8 = (bf16[512,128]{1,0:T(8,128)(2,1)S(1)}, bf16[512,128]{1,0:T(8,128)(2,1)S(1)}, u32[]{:S(2)}, u32[]{:S(2)}) collective-permute-start(bf16[512,128]{1,0:T(8,128)(2,1)S(1)} %get-tuple-element.70), channel_id=1, source_target_pairs={{0,128},{32,416},{64,192},{96,480},{128,256},{160,32},{192,320},{2... | collective-permute-start | bytes 393224 | tf_op jit(solution)/shard_map/ppermute | solution.py:384
  157.5 5.4 %collective-permute-start.9 = (bf16[512,128]{1,0:T(8,128)(2,1)S(1)}, bf16[512,128]{1,0:T(8,128)(2,1)S(1)}, u32[]{:S(2)}, u32[]{:S(2)}) collective-permute-start(bf16[512,128]{1,0:T(8,128)(2,1)S(1)} %get-tuple-element.71), channel_id=1, source_target_pairs={{0,160},{32,384},{64,224},{96,448},{128,288},{160,0},{192,352},{22... | collective-permute-start | bytes 393224 | tf_op jit(solution)/shard_map/ppermute | solution.py:385
  162.9 2.0 %all_gather.23.gives = bf16[1024,128]{1,0:T(8,128)(2,1)S(1)} all-gather(bf16[512,128]{1,0:T(8,128)(2,1)S(1)} %get-tuple-element.69), channel_id=1, replica_groups={{0,32},{64,96},{128,160},{192,224},{256,288},{320,352},{384,416},{448,4..., dimensions={0}, use_global_device_ids=true | all-gather | bytes 393216 | tf_op jit(solution)/shard_map/all_gather | solution.py:315
  164.9 1.6 collective-permute-done.9.cross
  (41 shorter events, 4.0 us)
Async XLA Ops:
  10.9 18.6 %collective-permute-start = (bf16[1056,128]{1,0:T(8,128)(2,1)S(1)}, bf16[1056,128]{1,0:T(8,128)(2,1)S(1)}, u32[]{:S(2)}, u32[]{:S(2)}) collective-permute-start(bf16[1056,128]{1,0:T(8,128)(2,1)S(1)} %all_gather.18.own), channel_id=1, source_target_pairs={{0,128},{32,416},{64,192},{96,480},{128,256},{160,32},{192,320},{2... | collective-permute-start | bytes 811016 | tf_op jit(solution)/shard_map/ppermute | solution.py:342
  19.8 11.9 %copy-start.10 = (s32[2,128,1]{1,2,0:T(1,128)S(1)}, s32[2,128,1]{1,2,0:T(1,128)}, u32[]{:S(2)}) copy-start(s32[2,128,1]{1,2,0:T(1,128)} %param.8) | copy-start | bytes 3076
  19.8 29.7 %all-to-all-start = ((bf16[32,96,128]{2,1,0:T(8,128)(2,1)}), bf16[32,96,128]{2,1,0:T(8,128)(2,1)S(1)}, u32[]{:S(2)}, u32[]{:S(2)}) async-start(bf16[32,96,128]{2,1,0:T(8,128)(2,1)} %shard_map.80), calls=%async_computation | async-start | bytes 1572864 | tf_op jit(solution)/shard_map/all_to_all | solution.py:306
  29.5 12.2 %collective-permute-start.1 = (bf16[1056,128]{1,0:T(8,128)(2,1)S(1)}, bf16[1056,128]{1,0:T(8,128)(2,1)S(1)}, u32[]{:S(2)}, u32[]{:S(2)}) collective-permute-start(bf16[1056,128]{1,0:T(8,128)(2,1)S(1)} %all_gather.18.own), channel_id=1, source_target_pairs={{0,64},{64,128},{128,192},{192,256},{256,320},{320,384},{384,448},... | collective-permute-start | bytes 811016 | tf_op jit(solution)/shard_map/ppermute | solution.py:345
  31.9 9.8 %copy-start.2 = (bf16[96,128]{1,0:T(8,128)(2,1)}, bf16[96,128]{1,0:T(8,128)(2,1)S(1)}, u32[]{:S(2)}) copy-start(bf16[96,128]{1,0:T(8,128)(2,1)S(1)} %get-tuple-element.41.pick_zero) | copy-start | bytes 73732
  31.9 9.8 %copy-start.4 = (bf16[96,128]{1,0:T(8,128)(2,1)}, bf16[96,128]{1,0:T(8,128)(2,1)S(1)}, u32[]{:S(2)}) copy-start(bf16[96,128]{1,0:T(8,128)(2,1)S(1)} %get-tuple-element.42.pick_one) | copy-start | bytes 73732
  31.9 18.6 %collective-permute-start.3 = (bf16[1056,128]{1,0:T(8,128)(2,1)S(1)}, bf16[1056,128]{1,0:T(8,128)(2,1)S(1)}, u32[]{:S(2)}, u32[]{:S(2)}) collective-permute-start(bf16[1056,128]{1,0:T(8,128)(2,1)S(1)} %collective-permute-done), channel_id=1, source_target_pairs={{0,128},{32,416},{64,192},{96,480},{128,256},{160,32},{192,320},{2... | collective-permute-start | bytes 811016 | tf_op jit(solution)/shard_map/ppermute | solution.py:346
  33.9 11.8 %collective-permute-start.2 = (bf16[1056,128]{1,0:T(8,128)(2,1)S(1)}, bf16[1056,128]{1,0:T(8,128)(2,1)S(1)}, u32[]{:S(2)}, u32[]{:S(2)}) collective-permute-start(bf16[1056,128]{1,0:T(8,128)(2,1)S(1)} %collective-permute-done), channel_id=1, source_target_pairs={{0,64},{64,128},{128,192},{192,256},{256,320},{320,384},{384,448},... | collective-permute-start | bytes 811016 | tf_op jit(solution)/shard_map/ppermute | solution.py:346
  43.9 5.4 %copy-start.8 = (f32[1,2048]{1,0:T(1,128)}, f32[1,2048]{1,0:T(1,128)S(1)}, u32[]{:S(2)}) copy-start(f32[1,2048]{1,0:T(1,128)S(1)} %shard_map.78.columns) | copy-start | bytes 24580
  49.6 1.0 copy-start.9
  51.9 23.1 %copy-start.6 = (f32[96,128]{1,0:T(8,128)}, f32[96,128]{1,0:T(8,128)S(1)}, u32[]{:S(2)}) copy-start(f32[96,128]{1,0:T(8,128)S(1)} %get-tuple-element.54.gate) | copy-start | bytes 147460
  51.9 23.1 %copy-start.11 = (bf16[96,1280]{1,0:T(8,128)(2,1)}, bf16[96,1280]{1,0:T(8,128)(2,1)S(1)}, u32[]{:S(2)}) copy-start(bf16[96,1280]{1,0:T(8,128)(2,1)S(1)} %get-tuple-element.58) | copy-start | bytes 737284
  51.9 23.1 %copy-start = (bf16[128,2048]{1,0:T(8,128)(2,1)S(1)}, bf16[128,2048]{1,0:T(8,128)(2,1)}, u32[]{:S(2)}) copy-start(bf16[128,2048]{1,0:T(8,128)(2,1)} %tokens.3) | copy-start | bytes 1572868
  51.9 23.1 %copy-start.3 = (bf16[96,128]{1,0:T(8,128)(2,1)S(1)}, bf16[96,128]{1,0:T(8,128)(2,1)}, u32[]{:S(2)}) copy-start(bf16[96,128]{1,0:T(8,128)(2,1)} %copy-done.2) | copy-start | bytes 73732
  51.9 23.1 %copy-start.5 = (bf16[96,128]{1,0:T(8,128)(2,1)S(1)}, bf16[96,128]{1,0:T(8,128)(2,1)}, u32[]{:S(2)}) copy-start(bf16[96,128]{1,0:T(8,128)(2,1)} %copy-done.4) | copy-start | bytes 73732
  95.6 18.2 %copy-start.1 = (bf16[128,2048]{1,0:T(8,128)(2,1)S(1)}, bf16[128,2048]{1,0:T(8,128)(2,1)}, u32[]{:S(2)}) copy-start(bf16[128,2048]{1,0:T(8,128)(2,1)} %cotangent.3) | copy-start | bytes 1572868
  115.7 17.8 %all-to-all-start.4 = ((bf16[32,48,128]{2,1,0:T(8,128)(2,1)}), bf16[32,48,128]{2,1,0:T(8,128)(2,1)S(1)}, u32[]{:S(2)}, u32[]{:S(2)}) async-start(bf16[32,48,128]{2,1,0:T(8,128)(2,1)} %bitcast.9), calls=%async_computation.4 | async-start | bytes 786432 | tf_op jit(solution)/shard_map/all_to_all | solution.py:306
  121.5 5.1 %copy-start.12 = (bf16[96,1280]{1,0:T(8,128)(2,1)S(1)}, bf16[96,1280]{1,0:T(8,128)(2,1)}, u32[]{:S(2)}) copy-start(bf16[96,1280]{1,0:T(8,128)(2,1)} %copy-done.11) | copy-start | bytes 737284
  121.5 12.0 %copy-start.7 = (f32[96,128]{1,0:T(8,128)S(1)}, f32[96,128]{1,0:T(8,128)}, u32[]{:S(2)}) copy-start(f32[96,128]{1,0:T(8,128)} %copy-done.6) | copy-start | bytes 147460
  122.5 17.9 %collective-permute-start.5 = (bf16[96,2560]{1,0:T(8,128)(2,1)}, bf16[96,2560]{1,0:T(8,128)(2,1)S(1)}, u32[]{:S(2)}, u32[]{:S(2)}) collective-permute-start(bf16[96,2560]{1,0:T(8,128)(2,1)} %get-tuple-element.64), channel_id=1, source_target_pairs={{0,32},{32,0},{64,96},{96,64},{128,160},{160,128},{192,224},{224,1... | collective-permute-start | bytes 1474568 | tf_op jit(solution)/shard_map/ppermute | solution.py:368
  126.6 13.8 %collective-permute-start.4 = (bf16[96,1280]{1,0:T(8,128)(2,1)S(1)}, bf16[96,1280]{1,0:T(8,128)(2,1)S(1)}, u32[]{:S(2)}, u32[]{:S(2)}) collective-permute-start(bf16[96,1280]{1,0:T(8,128)(2,1)S(1)} %copy-done.12), channel_id=1, source_target_pairs={{0,32},{32,0},{64,96},{96,64},{128,160},{160,128},{192,224},{224,1... | collective-permute-start | bytes 737288 | tf_op jit(solution)/shard_map/ppermute | solution.py:358
  141.2 13.6 %collective-permute-start.6 = (bf16[4,512,128]{2,1,0:T(8,128)(2,1)S(1)}, bf16[4,512,128]{2,1,0:T(8,128)(2,1)S(1)}, u32[]{:S(2)}, u32[]{:S(2)}) collective-permute-start(bf16[4,512,128]{2,1,0:T(8,128)(2,1)S(1)} %get-tuple-element.66), channel_id=1, source_target_pairs={{0,64},{64,128},{128,192},{192,256},{256,320},{320,384},{384,448},... | collective-permute-start | bytes 1572872 | tf_op jit(solution)/shard_map/ppermute | solution.py:382
  143.1 11.6 %collective-permute-start.7 = (bf16[1,512,128]{2,1,0:T(8,128)(2,1)S(1)}, bf16[1,512,128]{2,1,0:T(8,128)(2,1)S(1)}, u32[]{:S(2)}, u32[]{:S(2)}) collective-permute-start(bf16[1,512,128]{2,1,0:T(8,128)(2,1)S(1)} %get-tuple-element.67), channel_id=1, source_target_pairs={{0,128},{32,416},{64,192},{96,480},{128,256},{160,32},{192,320},{2... | collective-permute-start | bytes 393224 | tf_op jit(solution)/shard_map/ppermute | solution.py:382
  154.8 10.1 %collective-permute-start.8 = (bf16[512,128]{1,0:T(8,128)(2,1)S(1)}, bf16[512,128]{1,0:T(8,128)(2,1)S(1)}, u32[]{:S(2)}, u32[]{:S(2)}) collective-permute-start(bf16[512,128]{1,0:T(8,128)(2,1)S(1)} %get-tuple-element.70), channel_id=1, source_target_pairs={{0,128},{32,416},{64,192},{96,480},{128,256},{160,32},{192,320},{2... | collective-permute-start | bytes 393224 | tf_op jit(solution)/shard_map/ppermute | solution.py:384
  157.5 9.1 %collective-permute-start.9 = (bf16[512,128]{1,0:T(8,128)(2,1)S(1)}, bf16[512,128]{1,0:T(8,128)(2,1)S(1)}, u32[]{:S(2)}, u32[]{:S(2)}) collective-permute-start(bf16[512,128]{1,0:T(8,128)(2,1)S(1)} %get-tuple-element.71), channel_id=1, source_target_pairs={{0,160},{32,384},{64,224},{96,448},{128,288},{160,0},{192,352},{22... | collective-permute-start | bytes 393224 | tf_op jit(solution)/shard_map/ppermute | solution.py:385

commit v6 on v5

--- a/solution.py
+++ b/solution.py
@@ -27,7 +27,7 @@
     earlier = jnp.where(iota((TOK, TOK), 0) < iota((TOK, TOK), 1), 1.0, 0.0).astype(bf16)
     before = jnp.dot(jnp.where(hit, 1.0, 0.0).astype(bf16), earlier, preferred_element_type=f32)
     position = jnp.sum(jnp.where(hit, before, 0.0), axis=0, keepdims=True).astype(jnp.int32)
-    slot = jnp.where(position < CAP, position * EXPERTS + ids, -1)
+    slot = jnp.where(position < CAP, ids * CAP + position, -1)
     return jnp.where(iota((SLOTS, TOK), 0) == slot, 1.0, 0.0).astype(bf16)
 
 
@@ -39,25 +39,17 @@
     return lax.dot_general(pick, rows, (((0,), (0,)), ((), ())), preferred_element_type=f32)
 
 
-def pack(rows, wide, stride=PEER, first=0):
-    for r in range(CAP):
-        for k in range(CHUNKS):
-            wide[pl.ds(first + r * CHUNKS + k, EXPERTS, stride=stride), :] = rows[
-                r * EXPERTS : (r + 1) * EXPERTS, k * LANE : (k + 1) * LANE
-            ]
-
-
-def unpack(wide, dense, stride=PEER, first=0):
-    for r in range(CAP):
-        for k in range(CHUNKS):
-            dense[r * EXPERTS : (r + 1) * EXPERTS, k * LANE : (k + 1) * LANE] = wide[
-                pl.ds(first + r * CHUNKS + k, EXPERTS, stride=stride), :
-            ].astype(dense.dtype)
+def pack(rows):
+    return rows.astype(bf16).reshape(SLOTS, CHUNKS, LANE).reshape(SLOTS * CHUNKS, LANE)
+
+
+def unpack(blocks):
+    return blocks.reshape(SLOTS, CHUNKS, LANE).reshape(SLOTS, D)
 
 
 def normalize(state):
-    scale = jnp.sqrt(jnp.mean(state * state, axis=-1, keepdims=True) + epsilon)
-    return state / scale, scale
+    inverse = 1.0 / jnp.sqrt(jnp.mean(state * state, axis=-1, keepdims=True) + epsilon)
+    return state * inverse, inverse
 
 
 def share_kernel(weight_in, weight_out, router, out):
@@ -65,19 +57,6 @@
     out[LANE:G, :] = weight_in[0, :, LANE:]
     out[G : 2 * G, :] = weight_out[0]
     out[2 * G :, :] = jnp.broadcast_to(router[...], (SHARD - 2 * G, LANE))
-
-
-def columns_kernel(own, pair_1, pair_2, column):
-    chip = lax.div(lax.axis_index("ctx"), 2)
-    column[...] = jnp.zeros_like(column)
-    blocks = [(own, 0, chip)]
-    for hop, pair in enumerate((pair_1, pair_2), 1):
-        blocks += [(pair, 0, chip + CHIPS - hop), (pair, 2 * SHARD, chip + hop)]
-    for block, first, where in blocks:
-        for core in range(2):
-            at = first + core * SHARD + 2 * G
-            to = pl.multiple_of((2 * lax.rem(where, CHIPS) + core) * LANE, LANE)
-            column[:, pl.ds(to, LANE)] = block[at : at + 1, :].astype(f32)
 
 
 def place(block, first, chip, wa, wb, column):
@@ -130,7 +109,7 @@
     return upper, grad_expert, grad_pre
 
 
-def dispatch_kernel(tokens, cotangent, ids, out, first, second, wide, packed, sems):
+def dispatch_kernel(tokens, cotangent, ids, out, first, second, packed, sems):
     loads = []
     for i, (source, target) in enumerate(((tokens, first), (cotangent, second))):
         for j in range(4):
@@ -144,8 +123,7 @@
         for copy in loads[4 * i : 4 * i + 4]:
             copy.wait()
         rows = second[...] if i else normalize(first[...].astype(f32))[0].astype(bf16)
-        pack(to_slots(picks[i], rows), wide.at[i])
-        packed[i] = wide[i].reshape(EXPERTS, PEER, LANE).astype(bf16)
+        packed[i] = pack(to_slots(picks[i], rows)).reshape(EXPERTS, PEER, LANE)
         copy = pltpu.make_async_copy(
             packed.at[i], out.at[:, pl.ds(i * PEER, PEER), :], sems.at[8 + i]
         )
@@ -155,26 +133,24 @@
         copy.wait()
 
 
-def arrive_kernel(taken, rows, upstream, wide):
-    wide[...] = taken[...].astype(f32)
-    unpack(wide, rows, 2 * PEER, 0)
-    unpack(wide, upstream, 2 * PEER, PEER)
+def arrive_kernel(taken, rows, upstream):
+    blocks = taken[...].reshape(EXPERTS, 2 * PEER, LANE)
+    rows[...] = unpack(blocks[:, :PEER, :].reshape(EXPERTS * PEER, LANE))
+    upstream[...] = unpack(blocks[:, PEER:, :].reshape(EXPERTS * PEER, LANE))
 
 
 def first_kernel(
-    rows, own, pair_1, pair_2, pair_3, far, columns,
-    out, positive_out, own_out, mate_out, gate_out, wa, wb, column, wide
+    rows, own, pair_1, pair_2, pair_3, far,
+    out, positive_out, own_out, mate_out, gate_out, wa, wb, column
 ):
     chip = lax.div(lax.axis_index("ctx"), 2)
-    column[...] = columns[...]
     place(own, 0, chip, wa, wb, column)
     for hop, pair in enumerate((pair_1, pair_2, pair_3), 1):
         place(pair, 0, lax.rem(chip + CHIPS - hop, CHIPS), wa, wb, column)
         place(pair, 2 * SHARD, lax.rem(chip + hop, CHIPS), wa, wb, column)
     place(far, 0, lax.rem(chip + CHIPS // 2, CHIPS), wa, wb, column)
     positive, hidden, expert_out, gate = forward(rows[...], wa, wb, column)
-    pack((gate * expert_out), wide)
-    out[...] = wide[...].astype(bf16)
+    out[...] = pack(gate * expert_out)
     positive_out[...] = positive
     split(rows, hidden, own_out, mate_out)
     gate_out[...] = jnp.broadcast_to(gate, (SLOTS, LANE))
@@ -185,21 +161,18 @@
     second[...] = choose(ids[1:2, :])
 
 
-def middle_kernel(tokens, pick_zero, pick_one, mixed, out, state_out, wide, dense):
-    wide[...] = mixed[...].astype(f32)
-    unpack(wide, dense)
-    state = tokens[...].astype(f32) + to_tokens(pick_zero[...], dense[...])
-    state_out[...] = state
-    unit, _ = normalize(state)
-    pack(to_slots(pick_one[...], unit.astype(bf16)), wide)
-    out[...] = wide[...].astype(bf16)
+def middle_kernel(tokens, pick_zero, pick_one, mixed, out, unit_out, inverse_out):
+    state = tokens[...].astype(f32) + to_tokens(pick_zero[...], unpack(mixed[...]))
+    unit, inverse = normalize(state)
+    unit_out[...] = unit
+    inverse_out[...] = jnp.broadcast_to(inverse, (TOK, LANE))
+    out[...] = pack(to_slots(pick_one[...], unit.astype(bf16)))
 
 
 def second_kernel(
-    taken, upstream, wa, wb, column, out, rows, hidden_out, expert, pre, wide
+    taken, upstream, wa, wb, column, out, rows, hidden_out, expert, pre
 ):
-    wide[...] = taken[...].astype(f32)
-    unpack(wide, rows)
+    rows[...] = unpack(taken[...])
     positive, hidden, expert_out, gate = forward(rows[...], wa, wb, column)
     upper, grad_expert, grad_pre = backward(upstream[...], wb, positive, gate)
     grad_gate = jnp.sum(upper * expert_out, axis=1, keepdims=True)
@@ -207,8 +180,7 @@
     flowing = lax.dot_general(
         grad_pre, wa[...], (((1,), (1,)), ((), ())), preferred_element_type=f32
     )
-    pack(flowing + grad_logit * column[...], wide)
-    out[...] = wide[...].astype(bf16)
+    out[...] = pack(flowing + grad_logit * column[...])
     hidden_out[...] = hidden
     expert[...] = grad_expert
     pre[...] = grad_pre
@@ -219,25 +191,22 @@
     split(expert, pre[...], own, mate, HALF)
 
 
-def return_kernel(cotangent, state, pick_zero, pick_one, taken, out, wide, dense):
-    wide[...] = taken[...].astype(f32)
-    unpack(wide, dense)
-    unit, scale = normalize(state[...])
-    grad = to_tokens(pick_one[...], dense[...])
+def return_kernel(
+    cotangent, unit_in, inverse, pick_zero, pick_one, taken, out
+):
+    unit = unit_in[...]
+    grad = to_tokens(pick_one[...], unpack(taken[...]))
     inner = jnp.mean(grad * unit, axis=-1, keepdims=True)
-    upstream = cotangent[...].astype(f32) + (grad - unit * inner) / scale
-    pack(to_slots(pick_zero[...], upstream.astype(bf16)), wide)
-    out[...] = wide[...].astype(bf16)
+    upstream = cotangent[...].astype(f32) + (grad - unit * inner) * inverse[:, :1]
+    out[...] = pack(to_slots(pick_zero[...], upstream.astype(bf16)))
 
 
 def over_rows(left, right):
     return lax.dot_general(left, right, (((0,), (0,)), ((), ())), preferred_element_type=f32)
 
 
-def first_grad_kernel(taken, wb, positive, gate, own, mate, wide, dense):
-    wide[...] = taken[...].astype(f32)
-    unpack(wide, dense)
-    _, grad_expert, grad_pre = backward(dense[...], wb, positive[...], gate[:, :1])
+def first_grad_kernel(taken, wb, positive, gate, own, mate, dense):
+    _, grad_expert, grad_pre = backward(unpack(taken[...]), wb, positive[...], gate[:, :1])
     dense[...] = grad_expert
     split(dense, grad_pre, own, mate)
 
@@ -293,7 +262,6 @@
 
 
 PACKED = ((EXPERTS * PEER, LANE), bf16)
-WIDE = ((EXPERTS * PEER, LANE), f32)
 DENSE = ((SLOTS, D), bf16)
 PICK = ((SLOTS, TOK), bf16)
 HALF = D // 2 + G
@@ -320,7 +288,6 @@
         weight_in, weight_out, router.reshape(1, LANE)
     )
     own = both_cores(share)
-    wide_two = ((2 * EXPERTS * PEER, LANE), f32)
     far_away = pl.BlockSpec(memory_space=pl.ANY)
     leaving = pl.pallas_call(
         dispatch_kernel,
@@ -330,7 +297,6 @@
         scratch_shapes=[
             pltpu.VMEM((TOK, D), bf16),
             pltpu.VMEM((TOK, D), bf16),
-            pltpu.VMEM((2, EXPERTS * PEER, LANE), f32),
             pltpu.VMEM((2, EXPERTS, PEER, LANE), bf16),
             pltpu.SemaphoreType.DMA((10,)),
         ],
@@ -344,32 +310,34 @@
     _, two = lax.optimization_barrier((leaving, two))
     one = lax.ppermute(later, "ctx", around)
     three, four = lax.ppermute(two, "ctx", around), lax.ppermute(two, "ctx", two_on)
-    pairs = [both_cores(one), both_cores(two), both_cores(three), four]
-    picks = call(choose_kernel, [PICK, PICK])(ids)
-    (columns,) = call(columns_kernel, [WEIGHTS[2]], cost=8 * 1150000000)(own, *pairs[:2])
-    columns, picks = lax.optimization_barrier((columns, picks))
-    rows_zero, upstream_one = call(arrive_kernel, [DENSE, DENSE], [wide_two])(over_exp(leaving))
+    pairs = [both_cores(one), both_cores(two)]
+    ids, *pairs = lax.optimization_barrier((ids, *pairs))
+    picks = call(choose_kernel, [PICK, PICK], cost=8 * 1150000000)(ids)
+    three, *picks = lax.optimization_barrier((three, *picks))
+    pairs += [both_cores(three), four]
+    rows_zero, upstream_one = call(arrive_kernel, [DENSE, DENSE])(over_exp(leaving))
     mixed, positive, kept_own, kept_mate, gate, wa, wb, column = call(
         first_kernel,
         [PACKED, ((SLOTS, G), f32), KEPT, KEPT, ((SLOTS, LANE), f32), *WEIGHTS],
-        [WIDE],
-    )(rows_zero, own, *pairs, columns)
+    )(rows_zero, own, *pairs)
     across = [(2 * z + c, 2 * z + 1 - c) for z in range(chips) for c in range(2)]
     kept_mate = lax.ppermute(kept_mate, "ctx", across)
-    leaving, state_one = call(middle_kernel, [PACKED, ((TOK, D), f32)], [WIDE, DENSE])(
+    leaving, *unit_one = call(
+        middle_kernel, [PACKED, ((TOK, D), f32), ((TOK, LANE), f32)]
+    )(
         tokens, *picks, over_exp(mixed)
     )
     double = ((SLOTS, 2 * HALF), bf16)
     slim = ((SLOTS, G), bf16)
-    leaving, *second = call(second_kernel, [PACKED, DENSE, slim, DENSE, slim], [WIDE])(
+    leaving, *second = call(second_kernel, [PACKED, DENSE, slim, DENSE, slim])(
         over_exp(leaving), upstream_one, wa, wb, column
     )
     one_own, one_mate = call(split_kernel, [double, double])(*second)
     one_mate = lax.ppermute(one_mate, "ctx", across)
-    (leaving,) = call(return_kernel, [PACKED], [WIDE, DENSE])(
-        cotangent, state_one, *picks, over_exp(leaving)
-    )
-    grads_own, grads_mate = call(first_grad_kernel, [KEPT, KEPT], [WIDE, DENSE])(
+    (leaving,) = call(return_kernel, [PACKED])(
+        cotangent, *unit_one, *picks, over_exp(leaving)
+    )
+    grads_own, grads_mate = call(first_grad_kernel, [KEPT, KEPT], [DENSE])(
         over_exp(leaving), wb, positive, gate
     )
     half, narrow = ((4 * SLOTS, D // 2), bf16), ((4 * SLOTS, G), bf16)

time: 168 us -> 166 us (0.988)
  Pallas kernels: 15.9 us -> 13.8 us
    pallas_call x7 -> x6, Pallas kernels: 6.88 us -> 4.99 us  [the longest x1 1.68 us: on_device(): call(second_kernel, [PACKED, DENSE, slim, DENSE, slim])]
  transfers between devices with their start and end apart: 12 -> 12, of which waited for: 5 -> 5; matrix products, arithmetic and copies ran while one was open for 0% -> 0% of each run, Pallas kernels for 4% -> 3%
where the time goes in v6:
time: 166 us; the launch traced here: 165 us
  blocking collectives  86.7 us (52%)
  starting transfers between devices  47.6 us (29%)
  waiting for transfers between devices  15.4 us (9%)
  Pallas kernels  13.8 us (8%)
    all_to_all x3, blocking collectives, over_exp(): return lax.all_to_all(shaped, 'exp', 0, 0, tiled=True).reshape(buffer.shape)  58.7 us
    all_gather x6, blocking collectives, both_cores(): lax.all_gather(value, 'ctx', axis=0, tiled=True, axis_index_groups=cores)  28.1 us
    all_to_all x2, starting transfers between devices, over_exp(): return lax.all_to_all(shaped, 'exp', 0, 0, tiled=True).reshape(buffer.shape)  15.5 us
    ppermute x1, waiting for transfers between devices, on_device(): lax.ppermute(far, 'ctx', two_on)  7.12 us
    all_to_all x2, waiting for transfers between devices, over_exp(): return lax.all_to_all(shaped, 'exp', 0, 0, tiled=True).reshape(buffer.shape)  5.45 us
    ppermute x1, starting transfers between devices, on_device(): lax.ppermute(cross, 'ctx', [(a, b + 1 - 2 * (b % 2)) for a, b in two_on])  5.43 us
    ppermute x1, starting transfers between devices, on_device(): two = lax.ppermute(own, 'ctx', two_on)  5.27 us
    ppermute x1, starting transfers between devices, on_device(): lax.ppermute(far, 'ctx', two_on)  4.54 us
  transfers between devices with their start and end apart: 12, of which 5 were waited for; matrix products, arithmetic and copies ran while one was open for 0% of the time, Pallas kernels for 3%

profile of v6, /device:TPU:1, one launch (start us, length us, event | category | flops | bytes accessed | tf_op | source)
XLA Modules:
  0.0 165.1 jit_solution(10802928993244834336)
XLA Ops:
  0.6 1.5 shard_map.77
  2.2 8.7 %all_gather.18.own = bf16[1056,128]{1,0:T(8,128)(2,1)S(1)} all-gather(bf16[528,128]{1,0:T(8,128)(2,1)} %shard_map.77), channel_id=1, replica_groups={{0,32},{64,96},{128,160},{192,224},{256,288},{320,352},{384,416},{448,4..., dimensions={0}, use_global_device_ids=true | all-gather | bytes 405504 | tf_op jit(solution)/shard_map/all_gather | solution.py:283
  10.9 5.3 %collective-permute-start = (bf16[1056,128]{1,0:T(8,128)(2,1)S(1)}, bf16[1056,128]{1,0:T(8,128)(2,1)S(1)}, u32[]{:S(2)}, u32[]{:S(2)}) collective-permute-start(bf16[1056,128]{1,0:T(8,128)(2,1)S(1)} %all_gather.18.own), channel_id=1, source_target_pairs={{0,128},{32,416},{64,192},{96,480},{128,256},{160,32},{192,320},{2... | collective-permute-start | bytes 811016 | tf_op jit(solution)/shard_map/ppermute | solution.py:308
  16.2 3.4 %shard_map.79 = bf16[32,96,128]{2,1,0:T(8,128)(2,1)} custom-call(bf16[128,2048]{1,0:T(8,128)(2,1)} %tokens.3, bf16[128,2048]{1,0:T(8,128)(2,1)} %cotangent.3, s32[2,128]{1,0:T(2,128)} %bitcast.19), custom_call_target="tpu_custom_call" | custom-call | tf_op jit(solution)/shard_map/pallas_call | solution.py:292
  19.6 9.7 %all-to-all-start = ((bf16[32,96,128]{2,1,0:T(8,128)(2,1)}), bf16[32,96,128]{2,1,0:T(8,128)(2,1)S(1)}, u32[]{:S(2)}, u32[]{:S(2)}) async-start(bf16[32,96,128]{2,1,0:T(8,128)(2,1)} %shard_map.79), calls=%async_computation | async-start | bytes 1572864 | tf_op jit(solution)/shard_map/all_to_all | solution.py:274
  29.3 2.2 %collective-permute-start.2 = (bf16[1056,128]{1,0:T(8,128)(2,1)S(1)}, bf16[1056,128]{1,0:T(8,128)(2,1)S(1)}, u32[]{:S(2)}, u32[]{:S(2)}) collective-permute-start(bf16[1056,128]{1,0:T(8,128)(2,1)S(1)} %all_gather.18.own), channel_id=1, source_target_pairs={{0,64},{64,128},{128,192},{192,256},{256,320},{320,384},{384,448},... | collective-permute-start | bytes 811016 | tf_op jit(solution)/shard_map/ppermute | solution.py:311
  31.5 1.9 %collective-permute-start.3 = (bf16[1056,128]{1,0:T(8,128)(2,1)S(1)}, bf16[1056,128]{1,0:T(8,128)(2,1)S(1)}, u32[]{:S(2)}, u32[]{:S(2)}) collective-permute-start(bf16[1056,128]{1,0:T(8,128)(2,1)S(1)} %collective-permute-done), channel_id=1, source_target_pairs={{0,128},{32,416},{64,192},{96,480},{128,256},{160,32},{192,320},{2... | collective-permute-start | bytes 811016 | tf_op jit(solution)/shard_map/ppermute | solution.py:312
  33.5 2.2 %collective-permute-start.1 = (bf16[1056,128]{1,0:T(8,128)(2,1)S(1)}, bf16[1056,128]{1,0:T(8,128)(2,1)S(1)}, u32[]{:S(2)}, u32[]{:S(2)}) collective-permute-start(bf16[1056,128]{1,0:T(8,128)(2,1)S(1)} %collective-permute-done), channel_id=1, source_target_pairs={{0,64},{64,128},{128,192},{192,256},{256,320},{320,384},{384,448},... | collective-permute-start | bytes 811016 | tf_op jit(solution)/shard_map/ppermute | solution.py:312
  35.6 5.6 %all_gather.20.pair_2 = bf16[2112,128]{1,0:T(8,128)(2,1)S(1)} all-gather(bf16[1056,128]{1,0:T(8,128)(2,1)S(1)} %collective-permute-done), channel_id=1, replica_groups={{0,32},{64,96},{128,160},{192,224},{256,288},{320,352},{384,416},{448,4..., dimensions={0}, use_global_device_ids=true | all-gather | bytes 811008 | tf_op jit(solution)/shard_map/all_gather | solution.py:283
  41.3 2.3 %all_gather.19.pair_1 = bf16[2112,128]{1,0:T(8,128)(2,1)S(1)} all-gather(bf16[1056,128]{1,0:T(8,128)(2,1)S(1)} %collective-permute-done.2), channel_id=1, replica_groups={{0,32},{64,96},{128,160},{192,224},{256,288},{320,352},{384,416},{448,4..., dimensions={0}, use_global_device_ids=true | all-gather | bytes 811008 | tf_op jit(solution)/shard_map/all_gather | solution.py:283
  44.4 1.1 collective-permute-done.1
  45.5 3.4 %all_gather.21.pair_3 = bf16[2112,128]{1,0:T(8,128)(2,1)S(1)} all-gather(bf16[1056,128]{1,0:T(8,128)(2,1)S(1)} %collective-permute-done.1), channel_id=1, replica_groups={{0,32},{64,96},{128,160},{192,224},{256,288},{320,352},{384,416},{448,4..., dimensions={0}, use_global_device_ids=true | all-gather | bytes 811008 | tf_op jit(solution)/shard_map/all_gather | solution.py:283
  49.5 1.2 shard_map.81
  50.8 22.8 %all_to_all.25 = bf16[32,48,128]{2,1,0:T(8,128)(2,1)S(1)} all-to-all(bf16[32,48,128]{2,1,0:T(8,128)(2,1)S(1)} %bitcast.16), channel_id=1, replica_groups=mesh['ctx'=16,'exp'=32] {'exp'}, dimensions={0} | all-to-all | bytes 786432 | tf_op jit(solution)/shard_map/all_to_all | solution.py:274
  74.4 17.6 %all_to_all.26 = bf16[32,48,128]{2,1,0:T(8,128)(2,1)S(1)} all-to-all(bf16[32,48,128]{2,1,0:T(8,128)(2,1)S(1)} %bitcast.18), channel_id=1, replica_groups=mesh['ctx'=16,'exp'=32] {'exp'}, dimensions={0} | all-to-all | bytes 786432 | tf_op jit(solution)/shard_map/all_to_all | solution.py:274
  92.0 1.7 %shard_map.83 = (bf16[1536,128]{1,0:T(8,128)(2,1)S(1)}, bf16[96,2048]{1,0:T(8,128)(2,1)S(1)}, bf16[96,256]{1,0:T(8,128)(2,1)S(1)}, bf16[96,2048]{1,0:T(8,128)(2,1)S(1)}, bf16[96,256]{1,0:T(8,128)(2,1)S(1)}) custom-call(bf16[1536,128]{1,0:T(8,128)(2,1)S(1)} %bitcast.15, bf16[96,2048]{1,0:T(8,128)(2,1)S(1)} %get-tuple-element.56.upstream, ...), custom_call_target="tpu_custom_call" | custom-call | tf_op jit(solution)/shard_map/pallas_call | solution.py:332
  93.7 18.2 %all_to_all.27 = bf16[32,48,128]{2,1,0:T(8,128)(2,1)S(1)} all-to-all(bf16[32,48,128]{2,1,0:T(8,128)(2,1)S(1)} %bitcast.17), channel_id=1, replica_groups=mesh['ctx'=16,'exp'=32] {'exp'}, dimensions={0} | all-to-all | bytes 786432 | tf_op jit(solution)/shard_map/all_to_all | solution.py:274
  112.0 1.6 shard_map.84
  113.5 5.8 %all-to-all-start.4 = ((bf16[32,48,128]{2,1,0:T(8,128)(2,1)}), bf16[32,48,128]{2,1,0:T(8,128)(2,1)S(1)}, u32[]{:S(2)}, u32[]{:S(2)}) async-start(bf16[32,48,128]{2,1,0:T(8,128)(2,1)} %bitcast.9), calls=%async_computation.4 | async-start | bytes 786432 | tf_op jit(solution)/shard_map/all_to_all | solution.py:274
  119.3 1.0 shard_map.86
  120.4 4.0 %collective-permute-start.5 = (bf16[96,2560]{1,0:T(8,128)(2,1)}, bf16[96,2560]{1,0:T(8,128)(2,1)S(1)}, u32[]{:S(2)}, u32[]{:S(2)}) collective-permute-start(bf16[96,2560]{1,0:T(8,128)(2,1)} %get-tuple-element.72), channel_id=1, source_target_pairs={{0,32},{32,0},{64,96},{96,64},{128,160},{160,128},{192,224},{224,1... | collective-permute-start | bytes 1474568 | tf_op jit(solution)/shard_map/ppermute | solution.py:336
  124.4 1.9 %collective-permute-start.4 = (bf16[96,1280]{1,0:T(8,128)(2,1)S(1)}, bf16[96,1280]{1,0:T(8,128)(2,1)S(1)}, u32[]{:S(2)}, u32[]{:S(2)}) collective-permute-start(bf16[96,1280]{1,0:T(8,128)(2,1)S(1)} %copy-done.10), channel_id=1, source_target_pairs={{0,32},{32,0},{64,96},{96,64},{128,160},{160,128},{192,224},{224,1... | collective-permute-start | bytes 737288 | tf_op jit(solution)/shard_map/ppermute | solution.py:324
  126.3 5.0 %all-to-all-done.4 = bf16[32,48,128]{2,1,0:T(8,128)(2,1)S(1)} async-done(((bf16[32,48,128]{2,1,0:T(8,128)(2,1)}), bf16[32,48,128]{2,1,0:T(8,128)(2,1)S(1)}, u32[]{:S(2)}, u32[]{:S(2)}) %all-to-all-start.4) | async-done | bytes 393248 | tf_op jit(solution)/shard_map/all_to_all | solution.py:274
  132.0 6.0 %all_gather.22.grads_both = bf16[192,1280]{1,0:T(8,128)(2,1)S(1)} all-gather(bf16[96,1280]{1,0:T(8,128)(2,1)S(1)} %get-tuple-element.64), channel_id=1, replica_groups={{0,32},{64,96},{128,160},{192,224},{256,288},{320,352},{384,416},{448,4..., dimensions={0}, use_global_device_ids=true | all-gather | bytes 737280 | tf_op jit(solution)/shard_map/all_gather | solution.py:283
  138.8 2.0 %collective-permute-start.6 = (bf16[4,512,128]{2,1,0:T(8,128)(2,1)S(1)}, bf16[4,512,128]{2,1,0:T(8,128)(2,1)S(1)}, u32[]{:S(2)}, u32[]{:S(2)}) collective-permute-start(bf16[4,512,128]{2,1,0:T(8,128)(2,1)S(1)} %get-tuple-element.74), channel_id=1, source_target_pairs={{0,64},{64,128},{128,192},{192,256},{256,320},{320,384},{384,448},... | collective-permute-start | bytes 1572872 | tf_op jit(solution)/shard_map/ppermute | solution.py:350
  140.8 4.5 %collective-permute-start.7 = (bf16[1,512,128]{2,1,0:T(8,128)(2,1)S(1)}, bf16[1,512,128]{2,1,0:T(8,128)(2,1)S(1)}, u32[]{:S(2)}, u32[]{:S(2)}) collective-permute-start(bf16[1,512,128]{2,1,0:T(8,128)(2,1)S(1)} %get-tuple-element.75), channel_id=1, source_target_pairs={{0,128},{32,416},{64,192},{96,480},{128,256},{160,32},{192,320},{2... | collective-permute-start | bytes 393224 | tf_op jit(solution)/shard_map/ppermute | solution.py:350
  145.3 7.1 %collective-permute-done.7.far = bf16[1,512,128]{2,1,0:T(8,128)(2,1)S(1)} collective-permute-done((bf16[1,512,128]{2,1,0:T(8,128)(2,1)S(1)}, bf16[1,512,128]{2,1,0:T(8,128)(2,1)S(1)}, u32[]{:S(2)}, u32[]{:S(2)}) %collective-permute-start.7) | collective-permute-done | bytes 131104 | tf_op jit(solution)/shard_map/ppermute | solution.py:350
  152.5 2.6 %collective-permute-start.8 = (bf16[512,128]{1,0:T(8,128)(2,1)S(1)}, bf16[512,128]{1,0:T(8,128)(2,1)S(1)}, u32[]{:S(2)}, u32[]{:S(2)}) collective-permute-start(bf16[512,128]{1,0:T(8,128)(2,1)S(1)} %get-tuple-element.78), channel_id=1, source_target_pairs={{0,128},{32,416},{64,192},{96,480},{128,256},{160,32},{192,320},{2... | collective-permute-start | bytes 393224 | tf_op jit(solution)/shard_map/ppermute | solution.py:352
  155.1 5.4 %collective-permute-start.9 = (bf16[512,128]{1,0:T(8,128)(2,1)S(1)}, bf16[512,128]{1,0:T(8,128)(2,1)S(1)}, u32[]{:S(2)}, u32[]{:S(2)}) collective-permute-start(bf16[512,128]{1,0:T(8,128)(2,1)S(1)} %get-tuple-element.79), channel_id=1, source_target_pairs={{0,160},{32,384},{64,224},{96,448},{128,288},{160,0},{192,352},{22... | collective-permute-start | bytes 393224 | tf_op jit(solution)/shard_map/ppermute | solution.py:353
  160.6 2.0 %all_gather.23.gives = bf16[1024,128]{1,0:T(8,128)(2,1)S(1)} all-gather(bf16[512,128]{1,0:T(8,128)(2,1)S(1)} %get-tuple-element.77), channel_id=1, replica_groups={{0,32},{64,96},{128,160},{192,224},{256,288},{320,352},{384,416},{448,4..., dimensions={0}, use_global_device_ids=true | all-gather | bytes 393216 | tf_op jit(solution)/shard_map/all_gather | solution.py:283
  162.6 1.7 %collective-permute-done.9.cross = bf16[512,128]{1,0:T(8,128)(2,1)S(1)} collective-permute-done((bf16[512,128]{1,0:T(8,128)(2,1)S(1)}, bf16[512,128]{1,0:T(8,128)(2,1)S(1)}, u32[]{:S(2)}, u32[]{:S(2)}) %collective-permute-start.9) | collective-permute-done | bytes 131104 | tf_op jit(solution)/shard_map/ppermute | solution.py:353
  164.3 0.8 shard_map.89
  (36 shorter events, 3.7 us)
Async XLA Ops:
  10.9 18.4 %collective-permute-start = (bf16[1056,128]{1,0:T(8,128)(2,1)S(1)}, bf16[1056,128]{1,0:T(8,128)(2,1)S(1)}, u32[]{:S(2)}, u32[]{:S(2)}) collective-permute-start(bf16[1056,128]{1,0:T(8,128)(2,1)S(1)} %all_gather.18.own), channel_id=1, source_target_pairs={{0,128},{32,416},{64,192},{96,480},{128,256},{160,32},{192,320},{2... | collective-permute-start | bytes 811016 | tf_op jit(solution)/shard_map/ppermute | solution.py:308
  19.6 29.7 %all-to-all-start = ((bf16[32,96,128]{2,1,0:T(8,128)(2,1)}), bf16[32,96,128]{2,1,0:T(8,128)(2,1)S(1)}, u32[]{:S(2)}, u32[]{:S(2)}) async-start(bf16[32,96,128]{2,1,0:T(8,128)(2,1)} %shard_map.79), calls=%async_computation | async-start | bytes 1572864 | tf_op jit(solution)/shard_map/all_to_all | solution.py:274
  29.3 12.0 %collective-permute-start.2 = (bf16[1056,128]{1,0:T(8,128)(2,1)S(1)}, bf16[1056,128]{1,0:T(8,128)(2,1)S(1)}, u32[]{:S(2)}, u32[]{:S(2)}) collective-permute-start(bf16[1056,128]{1,0:T(8,128)(2,1)S(1)} %all_gather.18.own), channel_id=1, source_target_pairs={{0,64},{64,128},{128,192},{192,256},{256,320},{320,384},{384,448},... | collective-permute-start | bytes 811016 | tf_op jit(solution)/shard_map/ppermute | solution.py:311
  31.5 18.0 %collective-permute-start.3 = (bf16[1056,128]{1,0:T(8,128)(2,1)S(1)}, bf16[1056,128]{1,0:T(8,128)(2,1)S(1)}, u32[]{:S(2)}, u32[]{:S(2)}) collective-permute-start(bf16[1056,128]{1,0:T(8,128)(2,1)S(1)} %collective-permute-done), channel_id=1, source_target_pairs={{0,128},{32,416},{64,192},{96,480},{128,256},{160,32},{192,320},{2... | collective-permute-start | bytes 811016 | tf_op jit(solution)/shard_map/ppermute | solution.py:312
  33.5 12.0 %collective-permute-start.1 = (bf16[1056,128]{1,0:T(8,128)(2,1)S(1)}, bf16[1056,128]{1,0:T(8,128)(2,1)S(1)}, u32[]{:S(2)}, u32[]{:S(2)}) collective-permute-start(bf16[1056,128]{1,0:T(8,128)(2,1)S(1)} %collective-permute-done), channel_id=1, source_target_pairs={{0,64},{64,128},{128,192},{192,256},{256,320},{320,384},{384,448},... | collective-permute-start | bytes 811016 | tf_op jit(solution)/shard_map/ppermute | solution.py:312
  41.3 2.3 %copy-start.8 = (s32[2,128,1]{1,2,0:T(1,128)S(1)}, s32[2,128,1]{1,2,0:T(1,128)}, u32[]{:S(2)}) copy-start(s32[2,128,1]{1,2,0:T(1,128)} %param.8) | copy-start | bytes 3076
  43.8 0.6 copy-start.2
  44.4 4.5 %copy-start.4 = (bf16[96,128]{1,0:T(8,128)(2,1)}, bf16[96,128]{1,0:T(8,128)(2,1)S(1)}, u32[]{:S(2)}) copy-start(bf16[96,128]{1,0:T(8,128)(2,1)S(1)} %get-tuple-element.47.pick_one) | copy-start | bytes 73732
  50.8 22.9 %copy-start.6 = (f32[96,128]{1,0:T(8,128)}, f32[96,128]{1,0:T(8,128)S(1)}, u32[]{:S(2)}) copy-start(f32[96,128]{1,0:T(8,128)S(1)} %get-tuple-element.62.gate) | copy-start | bytes 147460
  50.8 22.9 %copy-start.9 = (bf16[96,1280]{1,0:T(8,128)(2,1)}, bf16[96,1280]{1,0:T(8,128)(2,1)S(1)}, u32[]{:S(2)}) copy-start(bf16[96,1280]{1,0:T(8,128)(2,1)S(1)} %get-tuple-element.66) | copy-start | bytes 737284
  50.8 22.9 %copy-start.1 = (bf16[128,2048]{1,0:T(8,128)(2,1)S(1)}, bf16[128,2048]{1,0:T(8,128)(2,1)}, u32[]{:S(2)}) copy-start(bf16[128,2048]{1,0:T(8,128)(2,1)} %tokens.3) | copy-start | bytes 1572868
  50.8 22.9 %copy-start.3 = (bf16[96,128]{1,0:T(8,128)(2,1)S(1)}, bf16[96,128]{1,0:T(8,128)(2,1)}, u32[]{:S(2)}) copy-start(bf16[96,128]{1,0:T(8,128)(2,1)} %copy-done.2) | copy-start | bytes 73732
  50.8 22.9 %copy-start.5 = (bf16[96,128]{1,0:T(8,128)(2,1)S(1)}, bf16[96,128]{1,0:T(8,128)(2,1)}, u32[]{:S(2)}) copy-start(bf16[96,128]{1,0:T(8,128)(2,1)} %copy-done.4) | copy-start | bytes 73732
  93.7 18.2 %copy-start = (bf16[128,2048]{1,0:T(8,128)(2,1)S(1)}, bf16[128,2048]{1,0:T(8,128)(2,1)}, u32[]{:S(2)}) copy-start(bf16[128,2048]{1,0:T(8,128)(2,1)} %cotangent.3) | copy-start | bytes 1572868
  113.5 17.8 %all-to-all-start.4 = ((bf16[32,48,128]{2,1,0:T(8,128)(2,1)}), bf16[32,48,128]{2,1,0:T(8,128)(2,1)S(1)}, u32[]{:S(2)}, u32[]{:S(2)}) async-start(bf16[32,48,128]{2,1,0:T(8,128)(2,1)} %bitcast.9), calls=%async_computation.4 | async-start | bytes 786432 | tf_op jit(solution)/shard_map/all_to_all | solution.py:274
  119.3 5.1 %copy-start.10 = (bf16[96,1280]{1,0:T(8,128)(2,1)S(1)}, bf16[96,1280]{1,0:T(8,128)(2,1)}, u32[]{:S(2)}) copy-start(bf16[96,1280]{1,0:T(8,128)(2,1)} %copy-done.9) | copy-start | bytes 737284
  119.3 12.0 %copy-start.7 = (f32[96,128]{1,0:T(8,128)S(1)}, f32[96,128]{1,0:T(8,128)}, u32[]{:S(2)}) copy-start(f32[96,128]{1,0:T(8,128)} %copy-done.6) | copy-start | bytes 147460
  120.4 17.7 %collective-permute-start.5 = (bf16[96,2560]{1,0:T(8,128)(2,1)}, bf16[96,2560]{1,0:T(8,128)(2,1)S(1)}, u32[]{:S(2)}, u32[]{:S(2)}) collective-permute-start(bf16[96,2560]{1,0:T(8,128)(2,1)} %get-tuple-element.72), channel_id=1, source_target_pairs={{0,32},{32,0},{64,96},{96,64},{128,160},{160,128},{192,224},{224,1... | collective-permute-start | bytes 1474568 | tf_op jit(solution)/shard_map/ppermute | solution.py:336
  124.4 13.6 %collective-permute-start.4 = (bf16[96,1280]{1,0:T(8,128)(2,1)S(1)}, bf16[96,1280]{1,0:T(8,128)(2,1)S(1)}, u32[]{:S(2)}, u32[]{:S(2)}) collective-permute-start(bf16[96,1280]{1,0:T(8,128)(2,1)S(1)} %copy-done.10), channel_id=1, source_target_pairs={{0,32},{32,0},{64,96},{96,64},{128,160},{160,128},{192,224},{224,1... | collective-permute-start | bytes 737288 | tf_op jit(solution)/shard_map/ppermute | solution.py:324
  138.8 13.7 %collective-permute-start.6 = (bf16[4,512,128]{2,1,0:T(8,128)(2,1)S(1)}, bf16[4,512,128]{2,1,0:T(8,128)(2,1)S(1)}, u32[]{:S(2)}, u32[]{:S(2)}) collective-permute-start(bf16[4,512,128]{2,1,0:T(8,128)(2,1)S(1)} %get-tuple-element.74), channel_id=1, source_target_pairs={{0,64},{64,128},{128,192},{192,256},{256,320},{320,384},{384,448},... | collective-permute-start | bytes 1572872 | tf_op jit(solution)/shard_map/ppermute | solution.py:350
  140.8 11.7 %collective-permute-start.7 = (bf16[1,512,128]{2,1,0:T(8,128)(2,1)S(1)}, bf16[1,512,128]{2,1,0:T(8,128)(2,1)S(1)}, u32[]{:S(2)}, u32[]{:S(2)}) collective-permute-start(bf16[1,512,128]{2,1,0:T(8,128)(2,1)S(1)} %get-tuple-element.75), channel_id=1, source_target_pairs={{0,128},{32,416},{64,192},{96,480},{128,256},{160,32},{192,320},{2... | collective-permute-start | bytes 393224 | tf_op jit(solution)/shard_map/ppermute | solution.py:350
  152.5 10.1 %collective-permute-start.8 = (bf16[512,128]{1,0:T(8,128)(2,1)S(1)}, bf16[512,128]{1,0:T(8,128)(2,1)S(1)}, u32[]{:S(2)}, u32[]{:S(2)}) collective-permute-start(bf16[512,128]{1,0:T(8,128)(2,1)S(1)} %get-tuple-element.78), channel_id=1, source_target_pairs={{0,128},{32,416},{64,192},{96,480},{128,256},{160,32},{192,320},{2... | collective-permute-start | bytes 393224 | tf_op jit(solution)/shard_map/ppermute | solution.py:352
  155.1 9.1 %collective-permute-start.9 = (bf16[512,128]{1,0:T(8,128)(2,1)S(1)}, bf16[512,128]{1,0:T(8,128)(2,1)S(1)}, u32[]{:S(2)}, u32[]{:S(2)}) collective-permute-start(bf16[512,128]{1,0:T(8,128)(2,1)S(1)} %get-tuple-element.79), channel_id=1, source_target_pairs={{0,160},{32,384},{64,224},{96,448},{128,288},{160,0},{192,352},{22... | collective-permute-start | bytes 393224 | tf_op jit(solution)/shard_map/ppermute | solution.py:353

commit v7 on v6

--- a/solution.py
+++ b/solution.py
@@ -109,28 +109,12 @@
     return upper, grad_expert, grad_pre
 
 
-def dispatch_kernel(tokens, cotangent, ids, out, first, second, packed, sems):
-    loads = []
-    for i, (source, target) in enumerate(((tokens, first), (cotangent, second))):
-        for j in range(4):
-            rows = pl.ds(j * TOK // 4, TOK // 4)
-            copy = pltpu.make_async_copy(source.at[rows, :], target.at[rows, :], sems.at[4 * i + j])
-            copy.start()
-            loads.append(copy)
-    picks = choose(ids[0:1, :]), choose(ids[1:2, :])
-    stores = []
-    for i in range(2):
-        for copy in loads[4 * i : 4 * i + 4]:
-            copy.wait()
-        rows = second[...] if i else normalize(first[...].astype(f32))[0].astype(bf16)
-        packed[i] = pack(to_slots(picks[i], rows)).reshape(EXPERTS, PEER, LANE)
-        copy = pltpu.make_async_copy(
-            packed.at[i], out.at[:, pl.ds(i * PEER, PEER), :], sems.at[8 + i]
-        )
-        copy.start()
-        stores.append(copy)
-    for copy in stores:
-        copy.wait()
+def dispatch_kernel(tokens, cotangent, ids, out):
+    unit, _ = normalize(tokens[...].astype(f32))
+    rows = to_slots(choose(ids[0:1, :]), unit.astype(bf16))
+    out[:, :PEER, :] = pack(rows).reshape(EXPERTS, PEER, LANE)
+    rows = to_slots(choose(ids[1:2, :]), cotangent[...])
+    out[:, PEER:, :] = pack(rows).reshape(EXPERTS, PEER, LANE)
 
 
 def arrive_kernel(taken, rows, upstream):
@@ -288,20 +272,10 @@
         weight_in, weight_out, router.reshape(1, LANE)
     )
     own = both_cores(share)
-    far_away = pl.BlockSpec(memory_space=pl.ANY)
-    leaving = pl.pallas_call(
-        dispatch_kernel,
-        out_shape=jax.ShapeDtypeStruct((EXPERTS, 2 * PEER, LANE), bf16),
-        in_specs=[far_away, far_away, pl.BlockSpec(memory_space=pltpu.VMEM)],
-        out_specs=far_away,
-        scratch_shapes=[
-            pltpu.VMEM((TOK, D), bf16),
-            pltpu.VMEM((TOK, D), bf16),
-            pltpu.VMEM((2, EXPERTS, PEER, LANE), bf16),
-            pltpu.SemaphoreType.DMA((10,)),
-        ],
-        compiler_params=pltpu.CompilerParams(vmem_limit_bytes=60 << 20),
-    )(tokens, cotangent, ids).reshape(2 * EXPERTS * PEER, LANE)
+    (leaving,) = call(dispatch_kernel, [((EXPERTS, 2 * PEER, LANE), bf16)], room=60)(
+        tokens, cotangent, ids
+    )
+    leaving = leaving.reshape(2 * EXPERTS * PEER, LANE)
     two_on = [
         (2 * z + c, 2 * ((z + 2 - 4 * c) % chips) + c) for z in range(chips) for c in range(2)
     ]

time: 166 us -> 165 us (level)
  no operation moved by 1% of the time
where the time goes in v7:
time: 165 us
  blocking collectives  86.7 us (53%)
  starting transfers between devices  47.6 us (29%)
  waiting for transfers between devices  15.4 us (9%)
  Pallas kernels  13.2 us (8%)
    all_to_all x3, blocking collectives, over_exp(): return lax.all_to_all(shaped, 'exp', 0, 0, tiled=True).reshape(buffer.shape)  58.7 us
    all_gather x6, blocking collectives, both_cores(): lax.all_gather(value, 'ctx', axis=0, tiled=True, axis_index_groups=cores)  28.1 us
    all_to_all x2, starting transfers between devices, over_exp(): return lax.all_to_all(shaped, 'exp', 0, 0, tiled=True).reshape(buffer.shape)  15.5 us
    ppermute x1, waiting for transfers between devices, on_device(): lax.ppermute(far, 'ctx', two_on)  7.12 us
    all_to_all x2, waiting for transfers between devices, over_exp(): return lax.all_to_all(shaped, 'exp', 0, 0, tiled=True).reshape(buffer.shape)  5.45 us
    ppermute x1, starting transfers between devices, on_device(): lax.ppermute(cross, 'ctx', [(a, b + 1 - 2 * (b % 2)) for a, b in two_on])  5.44 us
    ppermute x1, starting transfers between devices, on_device(): two = lax.ppermute(own, 'ctx', two_on)  5.27 us
    ppermute x1, starting transfers between devices, on_device(): lax.ppermute(far, 'ctx', two_on)  4.54 us
  transfers between devices with their start and end apart: 12, of which 5 were waited for; matrix products, arithmetic and copies ran while one was open for 0% of the time, Pallas kernels for 3%

profile of v7, /device:TPU:1, one launch (start us, length us, event | category | flops | bytes accessed | tf_op | source)
XLA Modules:
  0.0 164.5 jit_solution(9049958988912747195)
XLA Ops:
  0.6 1.5 shard_map.77
  2.2 8.7 %all_gather.18.own = bf16[1056,128]{1,0:T(8,128)(2,1)S(1)} all-gather(bf16[528,128]{1,0:T(8,128)(2,1)} %shard_map.77), channel_id=1, replica_groups={{0,32},{64,96},{128,160},{192,224},{256,288},{320,352},{384,416},{448,4..., dimensions={0}, use_global_device_ids=true | all-gather | bytes 405504 | tf_op jit(solution)/shard_map/all_gather | solution.py:267
  10.9 5.3 %collective-permute-start = (bf16[1056,128]{1,0:T(8,128)(2,1)S(1)}, bf16[1056,128]{1,0:T(8,128)(2,1)S(1)}, u32[]{:S(2)}, u32[]{:S(2)}) collective-permute-start(bf16[1056,128]{1,0:T(8,128)(2,1)S(1)} %all_gather.18.own), channel_id=1, source_target_pairs={{0,128},{32,416},{64,192},{96,480},{128,256},{160,32},{192,320},{2... | collective-permute-start | bytes 811016 | tf_op jit(solution)/shard_map/ppermute | solution.py:282
  16.2 2.9 %shard_map.79 = bf16[32,96,128]{2,1,0:T(8,128)(2,1)} custom-call(bf16[128,2048]{1,0:T(8,128)(2,1)} %tokens.3, bf16[128,2048]{1,0:T(8,128)(2,1)} %cotangent.3, s32[2,128]{1,0:T(2,128)} %bitcast.19), custom_call_target="tpu_custom_call" | custom-call | tf_op jit(solution)/shard_map/pallas_call | solution.py:275
  19.1 9.7 %all-to-all-start = ((bf16[32,96,128]{2,1,0:T(8,128)(2,1)}), bf16[32,96,128]{2,1,0:T(8,128)(2,1)S(1)}, u32[]{:S(2)}, u32[]{:S(2)}) async-start(bf16[32,96,128]{2,1,0:T(8,128)(2,1)} %shard_map.79), calls=%async_computation | async-start | bytes 1572864 | tf_op jit(solution)/shard_map/all_to_all | solution.py:258
  28.7 2.2 %collective-permute-start.2 = (bf16[1056,128]{1,0:T(8,128)(2,1)S(1)}, bf16[1056,128]{1,0:T(8,128)(2,1)S(1)}, u32[]{:S(2)}, u32[]{:S(2)}) collective-permute-start(bf16[1056,128]{1,0:T(8,128)(2,1)S(1)} %all_gather.18.own), channel_id=1, source_target_pairs={{0,64},{64,128},{128,192},{192,256},{256,320},{320,384},{384,448},... | collective-permute-start | bytes 811016 | tf_op jit(solution)/shard_map/ppermute | solution.py:285
  31.0 1.9 %collective-permute-start.3 = (bf16[1056,128]{1,0:T(8,128)(2,1)S(1)}, bf16[1056,128]{1,0:T(8,128)(2,1)S(1)}, u32[]{:S(2)}, u32[]{:S(2)}) collective-permute-start(bf16[1056,128]{1,0:T(8,128)(2,1)S(1)} %collective-permute-done), channel_id=1, source_target_pairs={{0,128},{32,416},{64,192},{96,480},{128,256},{160,32},{192,320},{2... | collective-permute-start | bytes 811016 | tf_op jit(solution)/shard_map/ppermute | solution.py:286
  32.9 2.2 %collective-permute-start.1 = (bf16[1056,128]{1,0:T(8,128)(2,1)S(1)}, bf16[1056,128]{1,0:T(8,128)(2,1)S(1)}, u32[]{:S(2)}, u32[]{:S(2)}) collective-permute-start(bf16[1056,128]{1,0:T(8,128)(2,1)S(1)} %collective-permute-done), channel_id=1, source_target_pairs={{0,64},{64,128},{128,192},{192,256},{256,320},{320,384},{384,448},... | collective-permute-start | bytes 811016 | tf_op jit(solution)/shard_map/ppermute | solution.py:286
  35.1 5.6 %all_gather.20.pair_2 = bf16[2112,128]{1,0:T(8,128)(2,1)S(1)} all-gather(bf16[1056,128]{1,0:T(8,128)(2,1)S(1)} %collective-permute-done), channel_id=1, replica_groups={{0,32},{64,96},{128,160},{192,224},{256,288},{320,352},{384,416},{448,4..., dimensions={0}, use_global_device_ids=true | all-gather | bytes 811008 | tf_op jit(solution)/shard_map/all_gather | solution.py:267
  40.7 2.3 %all_gather.19.pair_1 = bf16[2112,128]{1,0:T(8,128)(2,1)S(1)} all-gather(bf16[1056,128]{1,0:T(8,128)(2,1)S(1)} %collective-permute-done.2), channel_id=1, replica_groups={{0,32},{64,96},{128,160},{192,224},{256,288},{320,352},{384,416},{448,4..., dimensions={0}, use_global_device_ids=true | all-gather | bytes 811008 | tf_op jit(solution)/shard_map/all_gather | solution.py:267
  43.8 1.1 collective-permute-done.1
  44.9 3.4 %all_gather.21.pair_3 = bf16[2112,128]{1,0:T(8,128)(2,1)S(1)} all-gather(bf16[1056,128]{1,0:T(8,128)(2,1)S(1)} %collective-permute-done.1), channel_id=1, replica_groups={{0,32},{64,96},{128,160},{192,224},{256,288},{320,352},{384,416},{448,4..., dimensions={0}, use_global_device_ids=true | all-gather | bytes 811008 | tf_op jit(solution)/shard_map/all_gather | solution.py:267
  48.9 1.2 shard_map.81
  50.2 22.8 %all_to_all.25 = bf16[32,48,128]{2,1,0:T(8,128)(2,1)S(1)} all-to-all(bf16[32,48,128]{2,1,0:T(8,128)(2,1)S(1)} %bitcast.16), channel_id=1, replica_groups=mesh['ctx'=16,'exp'=32] {'exp'}, dimensions={0} | all-to-all | bytes 786432 | tf_op jit(solution)/shard_map/all_to_all | solution.py:258
  73.8 17.6 %all_to_all.26 = bf16[32,48,128]{2,1,0:T(8,128)(2,1)S(1)} all-to-all(bf16[32,48,128]{2,1,0:T(8,128)(2,1)S(1)} %bitcast.18), channel_id=1, replica_groups=mesh['ctx'=16,'exp'=32] {'exp'}, dimensions={0} | all-to-all | bytes 786432 | tf_op jit(solution)/shard_map/all_to_all | solution.py:258
  91.5 1.7 %shard_map.83 = (bf16[1536,128]{1,0:T(8,128)(2,1)S(1)}, bf16[96,2048]{1,0:T(8,128)(2,1)S(1)}, bf16[96,256]{1,0:T(8,128)(2,1)S(1)}, bf16[96,2048]{1,0:T(8,128)(2,1)S(1)}, bf16[96,256]{1,0:T(8,128)(2,1)S(1)}) custom-call(bf16[1536,128]{1,0:T(8,128)(2,1)S(1)} %bitcast.15, bf16[96,2048]{1,0:T(8,128)(2,1)S(1)} %get-tuple-element.56.upstream, ...), custom_call_target="tpu_custom_call" | custom-call | tf_op jit(solution)/shard_map/pallas_call | solution.py:306
  93.2 18.2 %all_to_all.27 = bf16[32,48,128]{2,1,0:T(8,128)(2,1)S(1)} all-to-all(bf16[32,48,128]{2,1,0:T(8,128)(2,1)S(1)} %bitcast.17), channel_id=1, replica_groups=mesh['ctx'=16,'exp'=32] {'exp'}, dimensions={0} | all-to-all | bytes 786432 | tf_op jit(solution)/shard_map/all_to_all | solution.py:258
  111.4 1.6 shard_map.84
  112.9 5.8 %all-to-all-start.4 = ((bf16[32,48,128]{2,1,0:T(8,128)(2,1)}), bf16[32,48,128]{2,1,0:T(8,128)(2,1)S(1)}, u32[]{:S(2)}, u32[]{:S(2)}) async-start(bf16[32,48,128]{2,1,0:T(8,128)(2,1)} %bitcast.9), calls=%async_computation.4 | async-start | bytes 786432 | tf_op jit(solution)/shard_map/all_to_all | solution.py:258
  118.8 1.0 shard_map.86
  119.8 4.0 %collective-permute-start.5 = (bf16[96,2560]{1,0:T(8,128)(2,1)}, bf16[96,2560]{1,0:T(8,128)(2,1)S(1)}, u32[]{:S(2)}, u32[]{:S(2)}) collective-permute-start(bf16[96,2560]{1,0:T(8,128)(2,1)} %get-tuple-element.72), channel_id=1, source_target_pairs={{0,32},{32,0},{64,96},{96,64},{128,160},{160,128},{192,224},{224,1... | collective-permute-start | bytes 1474568 | tf_op jit(solution)/shard_map/ppermute | solution.py:310
  123.9 1.9 %collective-permute-start.4 = (bf16[96,1280]{1,0:T(8,128)(2,1)S(1)}, bf16[96,1280]{1,0:T(8,128)(2,1)S(1)}, u32[]{:S(2)}, u32[]{:S(2)}) collective-permute-start(bf16[96,1280]{1,0:T(8,128)(2,1)S(1)} %copy-done.10), channel_id=1, source_target_pairs={{0,32},{32,0},{64,96},{96,64},{128,160},{160,128},{192,224},{224,1... | collective-permute-start | bytes 737288 | tf_op jit(solution)/shard_map/ppermute | solution.py:298
  125.8 5.0 %all-to-all-done.4 = bf16[32,48,128]{2,1,0:T(8,128)(2,1)S(1)} async-done(((bf16[32,48,128]{2,1,0:T(8,128)(2,1)}), bf16[32,48,128]{2,1,0:T(8,128)(2,1)S(1)}, u32[]{:S(2)}, u32[]{:S(2)}) %all-to-all-start.4) | async-done | bytes 393248 | tf_op jit(solution)/shard_map/all_to_all | solution.py:258
  131.5 6.0 %all_gather.22.grads_both = bf16[192,1280]{1,0:T(8,128)(2,1)S(1)} all-gather(bf16[96,1280]{1,0:T(8,128)(2,1)S(1)} %get-tuple-element.64), channel_id=1, replica_groups={{0,32},{64,96},{128,160},{192,224},{256,288},{320,352},{384,416},{448,4..., dimensions={0}, use_global_device_ids=true | all-gather | bytes 737280 | tf_op jit(solution)/shard_map/all_gather | solution.py:267
  138.2 2.0 %collective-permute-start.6 = (bf16[4,512,128]{2,1,0:T(8,128)(2,1)S(1)}, bf16[4,512,128]{2,1,0:T(8,128)(2,1)S(1)}, u32[]{:S(2)}, u32[]{:S(2)}) collective-permute-start(bf16[4,512,128]{2,1,0:T(8,128)(2,1)S(1)} %get-tuple-element.74), channel_id=1, source_target_pairs={{0,64},{64,128},{128,192},{192,256},{256,320},{320,384},{384,448},... | collective-permute-start | bytes 1572872 | tf_op jit(solution)/shard_map/ppermute | solution.py:324
  140.2 4.5 %collective-permute-start.7 = (bf16[1,512,128]{2,1,0:T(8,128)(2,1)S(1)}, bf16[1,512,128]{2,1,0:T(8,128)(2,1)S(1)}, u32[]{:S(2)}, u32[]{:S(2)}) collective-permute-start(bf16[1,512,128]{2,1,0:T(8,128)(2,1)S(1)} %get-tuple-element.75), channel_id=1, source_target_pairs={{0,128},{32,416},{64,192},{96,480},{128,256},{160,32},{192,320},{2... | collective-permute-start | bytes 393224 | tf_op jit(solution)/shard_map/ppermute | solution.py:324
  144.8 7.1 %collective-permute-done.7.far = bf16[1,512,128]{2,1,0:T(8,128)(2,1)S(1)} collective-permute-done((bf16[1,512,128]{2,1,0:T(8,128)(2,1)S(1)}, bf16[1,512,128]{2,1,0:T(8,128)(2,1)S(1)}, u32[]{:S(2)}, u32[]{:S(2)}) %collective-permute-start.7) | collective-permute-done | bytes 131104 | tf_op jit(solution)/shard_map/ppermute | solution.py:324
  152.0 2.6 %collective-permute-start.8 = (bf16[512,128]{1,0:T(8,128)(2,1)S(1)}, bf16[512,128]{1,0:T(8,128)(2,1)S(1)}, u32[]{:S(2)}, u32[]{:S(2)}) collective-permute-start(bf16[512,128]{1,0:T(8,128)(2,1)S(1)} %get-tuple-element.78), channel_id=1, source_target_pairs={{0,128},{32,416},{64,192},{96,480},{128,256},{160,32},{192,320},{2... | collective-permute-start | bytes 393224 | tf_op jit(solution)/shard_map/ppermute | solution.py:326
  154.6 5.4 %collective-permute-start.9 = (bf16[512,128]{1,0:T(8,128)(2,1)S(1)}, bf16[512,128]{1,0:T(8,128)(2,1)S(1)}, u32[]{:S(2)}, u32[]{:S(2)}) collective-permute-start(bf16[512,128]{1,0:T(8,128)(2,1)S(1)} %get-tuple-element.79), channel_id=1, source_target_pairs={{0,160},{32,384},{64,224},{96,448},{128,288},{160,0},{192,352},{22... | collective-permute-start | bytes 393224 | tf_op jit(solution)/shard_map/ppermute | solution.py:327
  160.0 2.0 %all_gather.23.gives = bf16[1024,128]{1,0:T(8,128)(2,1)S(1)} all-gather(bf16[512,128]{1,0:T(8,128)(2,1)S(1)} %get-tuple-element.77), channel_id=1, replica_groups={{0,32},{64,96},{128,160},{192,224},{256,288},{320,352},{384,416},{448,4..., dimensions={0}, use_global_device_ids=true | all-gather | bytes 393216 | tf_op jit(solution)/shard_map/all_gather | solution.py:267
  162.0 1.7 %collective-permute-done.9.cross = bf16[512,128]{1,0:T(8,128)(2,1)S(1)} collective-permute-done((bf16[512,128]{1,0:T(8,128)(2,1)S(1)}, bf16[512,128]{1,0:T(8,128)(2,1)S(1)}, u32[]{:S(2)}, u32[]{:S(2)}) %collective-permute-start.9) | collective-permute-done | bytes 131104 | tf_op jit(solution)/shard_map/ppermute | solution.py:327
  163.7 0.8 shard_map.89
  (36 shorter events, 3.7 us)
Async XLA Ops:
  10.9 17.8 %collective-permute-start = (bf16[1056,128]{1,0:T(8,128)(2,1)S(1)}, bf16[1056,128]{1,0:T(8,128)(2,1)S(1)}, u32[]{:S(2)}, u32[]{:S(2)}) collective-permute-start(bf16[1056,128]{1,0:T(8,128)(2,1)S(1)} %all_gather.18.own), channel_id=1, source_target_pairs={{0,128},{32,416},{64,192},{96,480},{128,256},{160,32},{192,320},{2... | collective-permute-start | bytes 811016 | tf_op jit(solution)/shard_map/ppermute | solution.py:282
  19.1 29.7 %all-to-all-start = ((bf16[32,96,128]{2,1,0:T(8,128)(2,1)}), bf16[32,96,128]{2,1,0:T(8,128)(2,1)S(1)}, u32[]{:S(2)}, u32[]{:S(2)}) async-start(bf16[32,96,128]{2,1,0:T(8,128)(2,1)} %shard_map.79), calls=%async_computation | async-start | bytes 1572864 | tf_op jit(solution)/shard_map/all_to_all | solution.py:258
  28.7 12.0 %collective-permute-start.2 = (bf16[1056,128]{1,0:T(8,128)(2,1)S(1)}, bf16[1056,128]{1,0:T(8,128)(2,1)S(1)}, u32[]{:S(2)}, u32[]{:S(2)}) collective-permute-start(bf16[1056,128]{1,0:T(8,128)(2,1)S(1)} %all_gather.18.own), channel_id=1, source_target_pairs={{0,64},{64,128},{128,192},{192,256},{256,320},{320,384},{384,448},... | collective-permute-start | bytes 811016 | tf_op jit(solution)/shard_map/ppermute | solution.py:285
  31.0 18.0 %collective-permute-start.3 = (bf16[1056,128]{1,0:T(8,128)(2,1)S(1)}, bf16[1056,128]{1,0:T(8,128)(2,1)S(1)}, u32[]{:S(2)}, u32[]{:S(2)}) collective-permute-start(bf16[1056,128]{1,0:T(8,128)(2,1)S(1)} %collective-permute-done), channel_id=1, source_target_pairs={{0,128},{32,416},{64,192},{96,480},{128,256},{160,32},{192,320},{2... | collective-permute-start | bytes 811016 | tf_op jit(solution)/shard_map/ppermute | solution.py:286
  32.9 12.0 %collective-permute-start.1 = (bf16[1056,128]{1,0:T(8,128)(2,1)S(1)}, bf16[1056,128]{1,0:T(8,128)(2,1)S(1)}, u32[]{:S(2)}, u32[]{:S(2)}) collective-permute-start(bf16[1056,128]{1,0:T(8,128)(2,1)S(1)} %collective-permute-done), channel_id=1, source_target_pairs={{0,64},{64,128},{128,192},{192,256},{256,320},{320,384},{384,448},... | collective-permute-start | bytes 811016 | tf_op jit(solution)/shard_map/ppermute | solution.py:286
  40.7 2.3 %copy-start.8 = (s32[2,128,1]{1,2,0:T(1,128)S(1)}, s32[2,128,1]{1,2,0:T(1,128)}, u32[]{:S(2)}) copy-start(s32[2,128,1]{1,2,0:T(1,128)} %param.8) | copy-start | bytes 3076
  43.2 0.6 copy-start.2
  43.8 4.5 %copy-start.4 = (bf16[96,128]{1,0:T(8,128)(2,1)}, bf16[96,128]{1,0:T(8,128)(2,1)S(1)}, u32[]{:S(2)}) copy-start(bf16[96,128]{1,0:T(8,128)(2,1)S(1)} %get-tuple-element.47.pick_one) | copy-start | bytes 73732
  50.2 22.9 %copy-start.6 = (f32[96,128]{1,0:T(8,128)}, f32[96,128]{1,0:T(8,128)S(1)}, u32[]{:S(2)}) copy-start(f32[96,128]{1,0:T(8,128)S(1)} %get-tuple-element.62.gate) | copy-start | bytes 147460
  50.2 22.9 %copy-start.9 = (bf16[96,1280]{1,0:T(8,128)(2,1)}, bf16[96,1280]{1,0:T(8,128)(2,1)S(1)}, u32[]{:S(2)}) copy-start(bf16[96,1280]{1,0:T(8,128)(2,1)S(1)} %get-tuple-element.66) | copy-start | bytes 737284
  50.2 22.9 %copy-start.1 = (bf16[128,2048]{1,0:T(8,128)(2,1)S(1)}, bf16[128,2048]{1,0:T(8,128)(2,1)}, u32[]{:S(2)}) copy-start(bf16[128,2048]{1,0:T(8,128)(2,1)} %tokens.3) | copy-start | bytes 1572868
  50.2 22.9 %copy-start.3 = (bf16[96,128]{1,0:T(8,128)(2,1)S(1)}, bf16[96,128]{1,0:T(8,128)(2,1)}, u32[]{:S(2)}) copy-start(bf16[96,128]{1,0:T(8,128)(2,1)} %copy-done.2) | copy-start | bytes 73732
  50.2 22.9 %copy-start.5 = (bf16[96,128]{1,0:T(8,128)(2,1)S(1)}, bf16[96,128]{1,0:T(8,128)(2,1)}, u32[]{:S(2)}) copy-start(bf16[96,128]{1,0:T(8,128)(2,1)} %copy-done.4) | copy-start | bytes 73732
  93.2 18.2 %copy-start = (bf16[128,2048]{1,0:T(8,128)(2,1)S(1)}, bf16[128,2048]{1,0:T(8,128)(2,1)}, u32[]{:S(2)}) copy-start(bf16[128,2048]{1,0:T(8,128)(2,1)} %cotangent.3) | copy-start | bytes 1572868
  112.9 17.8 %all-to-all-start.4 = ((bf16[32,48,128]{2,1,0:T(8,128)(2,1)}), bf16[32,48,128]{2,1,0:T(8,128)(2,1)S(1)}, u32[]{:S(2)}, u32[]{:S(2)}) async-start(bf16[32,48,128]{2,1,0:T(8,128)(2,1)} %bitcast.9), calls=%async_computation.4 | async-start | bytes 786432 | tf_op jit(solution)/shard_map/all_to_all | solution.py:258
  118.7 5.1 %copy-start.10 = (bf16[96,1280]{1,0:T(8,128)(2,1)S(1)}, bf16[96,1280]{1,0:T(8,128)(2,1)}, u32[]{:S(2)}) copy-start(bf16[96,1280]{1,0:T(8,128)(2,1)} %copy-done.9) | copy-start | bytes 737284
  118.8 12.0 %copy-start.7 = (f32[96,128]{1,0:T(8,128)S(1)}, f32[96,128]{1,0:T(8,128)}, u32[]{:S(2)}) copy-start(f32[96,128]{1,0:T(8,128)} %copy-done.6) | copy-start | bytes 147460
  119.8 17.7 %collective-permute-start.5 = (bf16[96,2560]{1,0:T(8,128)(2,1)}, bf16[96,2560]{1,0:T(8,128)(2,1)S(1)}, u32[]{:S(2)}, u32[]{:S(2)}) collective-permute-start(bf16[96,2560]{1,0:T(8,128)(2,1)} %get-tuple-element.72), channel_id=1, source_target_pairs={{0,32},{32,0},{64,96},{96,64},{128,160},{160,128},{192,224},{224,1... | collective-permute-start | bytes 1474568 | tf_op jit(solution)/shard_map/ppermute | solution.py:310
  123.9 13.6 %collective-permute-start.4 = (bf16[96,1280]{1,0:T(8,128)(2,1)S(1)}, bf16[96,1280]{1,0:T(8,128)(2,1)S(1)}, u32[]{:S(2)}, u32[]{:S(2)}) collective-permute-start(bf16[96,1280]{1,0:T(8,128)(2,1)S(1)} %copy-done.10), channel_id=1, source_target_pairs={{0,32},{32,0},{64,96},{96,64},{128,160},{160,128},{192,224},{224,1... | collective-permute-start | bytes 737288 | tf_op jit(solution)/shard_map/ppermute | solution.py:298
  138.2 13.7 %collective-permute-start.6 = (bf16[4,512,128]{2,1,0:T(8,128)(2,1)S(1)}, bf16[4,512,128]{2,1,0:T(8,128)(2,1)S(1)}, u32[]{:S(2)}, u32[]{:S(2)}) collective-permute-start(bf16[4,512,128]{2,1,0:T(8,128)(2,1)S(1)} %get-tuple-element.74), channel_id=1, source_target_pairs={{0,64},{64,128},{128,192},{192,256},{256,320},{320,384},{384,448},... | collective-permute-start | bytes 1572872 | tf_op jit(solution)/shard_map/ppermute | solution.py:324
  140.2 11.7 %collective-permute-start.7 = (bf16[1,512,128]{2,1,0:T(8,128)(2,1)S(1)}, bf16[1,512,128]{2,1,0:T(8,128)(2,1)S(1)}, u32[]{:S(2)}, u32[]{:S(2)}) collective-permute-start(bf16[1,512,128]{2,1,0:T(8,128)(2,1)S(1)} %get-tuple-element.75), channel_id=1, source_target_pairs={{0,128},{32,416},{64,192},{96,480},{128,256},{160,32},{192,320},{2... | collective-permute-start | bytes 393224 | tf_op jit(solution)/shard_map/ppermute | solution.py:324
  152.0 10.1 %collective-permute-start.8 = (bf16[512,128]{1,0:T(8,128)(2,1)S(1)}, bf16[512,128]{1,0:T(8,128)(2,1)S(1)}, u32[]{:S(2)}, u32[]{:S(2)}) collective-permute-start(bf16[512,128]{1,0:T(8,128)(2,1)S(1)} %get-tuple-element.78), channel_id=1, source_target_pairs={{0,128},{32,416},{64,192},{96,480},{128,256},{160,32},{192,320},{2... | collective-permute-start | bytes 393224 | tf_op jit(solution)/shard_map/ppermute | solution.py:326
  154.6 9.2 %collective-permute-start.9 = (bf16[512,128]{1,0:T(8,128)(2,1)S(1)}, bf16[512,128]{1,0:T(8,128)(2,1)S(1)}, u32[]{:S(2)}, u32[]{:S(2)}) collective-permute-start(bf16[512,128]{1,0:T(8,128)(2,1)S(1)} %get-tuple-element.79), channel_id=1, source_target_pairs={{0,160},{32,384},{64,224},{96,448},{128,288},{160,0},{192,352},{22... | collective-permute-start | bytes 393224 | tf_op jit(solution)/shard_map/ppermute | solution.py:327

commit v8 on v7

--- a/solution.py
+++ b/solution.py
@@ -215,13 +215,17 @@
         out[to, G:, :] = part_out[:, at].astype(out.dtype)
 
 
-def relay_kernel(near, far, next_chip, same, cross, give):
+def cross_kernel(near, next_chip, cross, give):
+    core = lax.rem(lax.axis_index("ctx"), 2)
+    cross[...] = (next_chip[1 - core] + near[3 - core].astype(f32)).astype(bf16)
+    give[...] = near[1 - core]
+
+
+def same_kernel(near, far, next_chip, same):
     core = lax.rem(lax.axis_index("ctx"), 2)
     same[...] = (
         next_chip[core] + near[2 + core].astype(f32) + far[0].astype(f32)
     ).astype(bf16)
-    cross[...] = (next_chip[1 - core] + near[3 - core].astype(f32)).astype(bf16)
-    give[...] = near[1 - core]
 
 
 def total_kernel(own_chip, near, gives, same, cross, grad_in, grad_out):
@@ -322,7 +326,8 @@
         [half, narrow, half, narrow],
     )(grads_own, both_cores(grads_mate), kept_own, kept_mate, one_own, one_mate)
     near, far = lax.ppermute(near, "ctx", around), lax.ppermute(far, "ctx", two_on)
-    same, cross, give = call(relay_kernel, [(chunk, bf16)] * 3)(near, far, next_chip)
+    cross, give = call(cross_kernel, [(chunk, bf16)] * 2)(near, next_chip)
+    (same,) = call(same_kernel, [(chunk, bf16)])(near, far, next_chip)
     same = lax.ppermute(same, "ctx", two_on)
     cross = lax.ppermute(cross, "ctx", [(a, b + 1 - 2 * (b % 2)) for a, b in two_on])
     grad_in, grad_out = call(total_kernel, [((1, LANE, G), f32), ((1, G, LANE), f32)])(

time: 165 us -> 164 us (level)
  waiting for transfers between devices: 15.4 us -> 12 us
  starting transfers between devices: 47.6 us -> 49.5 us
    ppermute x1, waiting for transfers between devices: 7.12 us -> 0.01 us  [on_device(): lax.ppermute(far, 'ctx', two_on)]
    ppermute x1, waiting for transfers between devices: 0.01 us -> 3.69 us  [on_device(): lax.ppermute(near, 'ctx', around)]
    ppermute x1, starting transfers between devices: 2.61 us -> 5.96 us  [on_device(): same = lax.ppermute(same, 'ctx', two_on)]
    ppermute x1, waiting for transfers between devices: 0.01 us -> 1.76 us  [on_device(): same = lax.ppermute(same, 'ctx', two_on)]
    ppermute x1, waiting for transfers between devices: 1.71 us -> 0.01 us  [on_device(): lax.ppermute(cross, 'ctx', [(a, b + 1 - 2 * (b % 2)) for a, b in two_on])]
where the time goes in v8:
time: 164 us; the launch traced here: 163 us
  blocking collectives  86.7 us (53%)
  starting transfers between devices  49.5 us (30%)
  Pallas kernels  13.3 us (8%)
  waiting for transfers between devices  12 us (7%)
    all_to_all x3, blocking collectives, over_exp(): return lax.all_to_all(shaped, 'exp', 0, 0, tiled=True).reshape(buffer.shape)  58.7 us
    all_gather x6, blocking collectives, both_cores(): lax.all_gather(value, 'ctx', axis=0, tiled=True, axis_index_groups=cores)  28.1 us
    all_to_all x2, starting transfers between devices, over_exp(): return lax.all_to_all(shaped, 'exp', 0, 0, tiled=True).reshape(buffer.shape)  15.5 us
    ppermute x1, starting transfers between devices, on_device(): same = lax.ppermute(same, 'ctx', two_on)  5.96 us
    all_to_all x2, waiting for transfers between devices, over_exp(): return lax.all_to_all(shaped, 'exp', 0, 0, tiled=True).reshape(buffer.shape)  5.45 us
    ppermute x1, starting transfers between devices, on_device(): two = lax.ppermute(own, 'ctx', two_on)  5.27 us
    ppermute x1, starting transfers between devices, on_device(): lax.ppermute(far, 'ctx', two_on)  4.54 us
    ppermute x1, starting transfers between devices, on_device(): one_mate = lax.ppermute(one_mate, 'ctx', across)  4.04 us
  transfers between devices with their start and end apart: 12, of which 5 were waited for; matrix products, arithmetic and copies ran while one was open for 0% of the time, Pallas kernels for 3%

profile of v8, /device:TPU:1, one launch (start us, length us, event | category | flops | bytes accessed | tf_op | source)
XLA Modules:
  0.0 163.0 jit_solution(3782413422562063607)
XLA Ops:
  0.6 1.5 shard_map.77
  2.2 8.7 %all_gather.18.own = bf16[1056,128]{1,0:T(8,128)(2,1)S(1)} all-gather(bf16[528,128]{1,0:T(8,128)(2,1)} %shard_map.77), channel_id=1, replica_groups={{0,32},{64,96},{128,160},{192,224},{256,288},{320,352},{384,416},{448,4..., dimensions={0}, use_global_device_ids=true | all-gather | bytes 405504 | tf_op jit(solution)/shard_map/all_gather | solution.py:271
  10.9 5.3 %collective-permute-start = (bf16[1056,128]{1,0:T(8,128)(2,1)S(1)}, bf16[1056,128]{1,0:T(8,128)(2,1)S(1)}, u32[]{:S(2)}, u32[]{:S(2)}) collective-permute-start(bf16[1056,128]{1,0:T(8,128)(2,1)S(1)} %all_gather.18.own), channel_id=1, source_target_pairs={{0,128},{32,416},{64,192},{96,480},{128,256},{160,32},{192,320},{2... | collective-permute-start | bytes 811016 | tf_op jit(solution)/shard_map/ppermute | solution.py:286
  16.2 2.9 %shard_map.79 = bf16[32,96,128]{2,1,0:T(8,128)(2,1)} custom-call(bf16[128,2048]{1,0:T(8,128)(2,1)} %tokens.3, bf16[128,2048]{1,0:T(8,128)(2,1)} %cotangent.3, s32[2,128]{1,0:T(2,128)} %bitcast.19), custom_call_target="tpu_custom_call" | custom-call | tf_op jit(solution)/shard_map/pallas_call | solution.py:279
  19.1 9.7 %all-to-all-start = ((bf16[32,96,128]{2,1,0:T(8,128)(2,1)}), bf16[32,96,128]{2,1,0:T(8,128)(2,1)S(1)}, u32[]{:S(2)}, u32[]{:S(2)}) async-start(bf16[32,96,128]{2,1,0:T(8,128)(2,1)} %shard_map.79), calls=%async_computation | async-start | bytes 1572864 | tf_op jit(solution)/shard_map/all_to_all | solution.py:262
  28.7 2.2 %collective-permute-start.2 = (bf16[1056,128]{1,0:T(8,128)(2,1)S(1)}, bf16[1056,128]{1,0:T(8,128)(2,1)S(1)}, u32[]{:S(2)}, u32[]{:S(2)}) collective-permute-start(bf16[1056,128]{1,0:T(8,128)(2,1)S(1)} %all_gather.18.own), channel_id=1, source_target_pairs={{0,64},{64,128},{128,192},{192,256},{256,320},{320,384},{384,448},... | collective-permute-start | bytes 811016 | tf_op jit(solution)/shard_map/ppermute | solution.py:289
  31.0 1.9 %collective-permute-start.3 = (bf16[1056,128]{1,0:T(8,128)(2,1)S(1)}, bf16[1056,128]{1,0:T(8,128)(2,1)S(1)}, u32[]{:S(2)}, u32[]{:S(2)}) collective-permute-start(bf16[1056,128]{1,0:T(8,128)(2,1)S(1)} %collective-permute-done), channel_id=1, source_target_pairs={{0,128},{32,416},{64,192},{96,480},{128,256},{160,32},{192,320},{2... | collective-permute-start | bytes 811016 | tf_op jit(solution)/shard_map/ppermute | solution.py:290
  32.9 2.2 %collective-permute-start.1 = (bf16[1056,128]{1,0:T(8,128)(2,1)S(1)}, bf16[1056,128]{1,0:T(8,128)(2,1)S(1)}, u32[]{:S(2)}, u32[]{:S(2)}) collective-permute-start(bf16[1056,128]{1,0:T(8,128)(2,1)S(1)} %collective-permute-done), channel_id=1, source_target_pairs={{0,64},{64,128},{128,192},{192,256},{256,320},{320,384},{384,448},... | collective-permute-start | bytes 811016 | tf_op jit(solution)/shard_map/ppermute | solution.py:290
  35.1 5.6 %all_gather.20.pair_2 = bf16[2112,128]{1,0:T(8,128)(2,1)S(1)} all-gather(bf16[1056,128]{1,0:T(8,128)(2,1)S(1)} %collective-permute-done), channel_id=1, replica_groups={{0,32},{64,96},{128,160},{192,224},{256,288},{320,352},{384,416},{448,4..., dimensions={0}, use_global_device_ids=true | all-gather | bytes 811008 | tf_op jit(solution)/shard_map/all_gather | solution.py:271
  40.7 2.3 %all_gather.19.pair_1 = bf16[2112,128]{1,0:T(8,128)(2,1)S(1)} all-gather(bf16[1056,128]{1,0:T(8,128)(2,1)S(1)} %collective-permute-done.2), channel_id=1, replica_groups={{0,32},{64,96},{128,160},{192,224},{256,288},{320,352},{384,416},{448,4..., dimensions={0}, use_global_device_ids=true | all-gather | bytes 811008 | tf_op jit(solution)/shard_map/all_gather | solution.py:271
  43.8 1.1 collective-permute-done.1
  44.9 3.4 %all_gather.21.pair_3 = bf16[2112,128]{1,0:T(8,128)(2,1)S(1)} all-gather(bf16[1056,128]{1,0:T(8,128)(2,1)S(1)} %collective-permute-done.1), channel_id=1, replica_groups={{0,32},{64,96},{128,160},{192,224},{256,288},{320,352},{384,416},{448,4..., dimensions={0}, use_global_device_ids=true | all-gather | bytes 811008 | tf_op jit(solution)/shard_map/all_gather | solution.py:271
  48.9 1.2 shard_map.81
  50.2 22.8 %all_to_all.25 = bf16[32,48,128]{2,1,0:T(8,128)(2,1)S(1)} all-to-all(bf16[32,48,128]{2,1,0:T(8,128)(2,1)S(1)} %bitcast.16), channel_id=1, replica_groups=mesh['ctx'=16,'exp'=32] {'exp'}, dimensions={0} | all-to-all | bytes 786432 | tf_op jit(solution)/shard_map/all_to_all | solution.py:262
  73.8 17.6 %all_to_all.26 = bf16[32,48,128]{2,1,0:T(8,128)(2,1)S(1)} all-to-all(bf16[32,48,128]{2,1,0:T(8,128)(2,1)S(1)} %bitcast.18), channel_id=1, replica_groups=mesh['ctx'=16,'exp'=32] {'exp'}, dimensions={0} | all-to-all | bytes 786432 | tf_op jit(solution)/shard_map/all_to_all | solution.py:262
  91.5 1.7 %shard_map.83 = (bf16[1536,128]{1,0:T(8,128)(2,1)S(1)}, bf16[96,2048]{1,0:T(8,128)(2,1)S(1)}, bf16[96,256]{1,0:T(8,128)(2,1)S(1)}, bf16[96,2048]{1,0:T(8,128)(2,1)S(1)}, bf16[96,256]{1,0:T(8,128)(2,1)S(1)}) custom-call(bf16[1536,128]{1,0:T(8,128)(2,1)S(1)} %bitcast.15, bf16[96,2048]{1,0:T(8,128)(2,1)S(1)} %get-tuple-element.55.upstream, ...), custom_call_target="tpu_custom_call" | custom-call | tf_op jit(solution)/shard_map/pallas_call | solution.py:310
  93.2 18.2 %all_to_all.27 = bf16[32,48,128]{2,1,0:T(8,128)(2,1)S(1)} all-to-all(bf16[32,48,128]{2,1,0:T(8,128)(2,1)S(1)} %bitcast.17), channel_id=1, replica_groups=mesh['ctx'=16,'exp'=32] {'exp'}, dimensions={0} | all-to-all | bytes 786432 | tf_op jit(solution)/shard_map/all_to_all | solution.py:262
  111.4 1.6 shard_map.84
  112.9 5.8 %all-to-all-start.4 = ((bf16[32,48,128]{2,1,0:T(8,128)(2,1)}), bf16[32,48,128]{2,1,0:T(8,128)(2,1)S(1)}, u32[]{:S(2)}, u32[]{:S(2)}) async-start(bf16[32,48,128]{2,1,0:T(8,128)(2,1)} %bitcast.9), calls=%async_computation.4 | async-start | bytes 786432 | tf_op jit(solution)/shard_map/all_to_all | solution.py:262
  118.8 1.0 shard_map.86
  119.8 4.0 %collective-permute-start.5 = (bf16[96,2560]{1,0:T(8,128)(2,1)}, bf16[96,2560]{1,0:T(8,128)(2,1)S(1)}, u32[]{:S(2)}, u32[]{:S(2)}) collective-permute-start(bf16[96,2560]{1,0:T(8,128)(2,1)} %get-tuple-element.71), channel_id=1, source_target_pairs={{0,32},{32,0},{64,96},{96,64},{128,160},{160,128},{192,224},{224,1... | collective-permute-start | bytes 1474568 | tf_op jit(solution)/shard_map/ppermute | solution.py:314
  123.9 1.9 %collective-permute-start.4 = (bf16[96,1280]{1,0:T(8,128)(2,1)S(1)}, bf16[96,1280]{1,0:T(8,128)(2,1)S(1)}, u32[]{:S(2)}, u32[]{:S(2)}) collective-permute-start(bf16[96,1280]{1,0:T(8,128)(2,1)S(1)} %copy-done.10), channel_id=1, source_target_pairs={{0,32},{32,0},{64,96},{96,64},{128,160},{160,128},{192,224},{224,1... | collective-permute-start | bytes 737288 | tf_op jit(solution)/shard_map/ppermute | solution.py:302
  125.8 5.0 %all-to-all-done.4 = bf16[32,48,128]{2,1,0:T(8,128)(2,1)S(1)} async-done(((bf16[32,48,128]{2,1,0:T(8,128)(2,1)}), bf16[32,48,128]{2,1,0:T(8,128)(2,1)S(1)}, u32[]{:S(2)}, u32[]{:S(2)}) %all-to-all-start.4) | async-done | bytes 393248 | tf_op jit(solution)/shard_map/all_to_all | solution.py:262
  131.5 6.0 %all_gather.22.grads_both = bf16[192,1280]{1,0:T(8,128)(2,1)S(1)} all-gather(bf16[96,1280]{1,0:T(8,128)(2,1)S(1)} %get-tuple-element.63), channel_id=1, replica_groups={{0,32},{64,96},{128,160},{192,224},{256,288},{320,352},{384,416},{448,4..., dimensions={0}, use_global_device_ids=true | all-gather | bytes 737280 | tf_op jit(solution)/shard_map/all_gather | solution.py:271
  138.2 2.0 %collective-permute-start.6 = (bf16[4,512,128]{2,1,0:T(8,128)(2,1)S(1)}, bf16[4,512,128]{2,1,0:T(8,128)(2,1)S(1)}, u32[]{:S(2)}, u32[]{:S(2)}) collective-permute-start(bf16[4,512,128]{2,1,0:T(8,128)(2,1)S(1)} %get-tuple-element.73), channel_id=1, source_target_pairs={{0,64},{64,128},{128,192},{192,256},{256,320},{320,384},{384,448},... | collective-permute-start | bytes 1572872 | tf_op jit(solution)/shard_map/ppermute | solution.py:328
  140.2 4.5 %collective-permute-start.7 = (bf16[1,512,128]{2,1,0:T(8,128)(2,1)S(1)}, bf16[1,512,128]{2,1,0:T(8,128)(2,1)S(1)}, u32[]{:S(2)}, u32[]{:S(2)}) collective-permute-start(bf16[1,512,128]{2,1,0:T(8,128)(2,1)S(1)} %get-tuple-element.76), channel_id=1, source_target_pairs={{0,128},{32,416},{64,192},{96,480},{128,256},{160,32},{192,320},{2... | collective-permute-start | bytes 393224 | tf_op jit(solution)/shard_map/ppermute | solution.py:328
  144.8 3.7 %collective-permute-done.6.near = bf16[4,512,128]{2,1,0:T(8,128)(2,1)S(1)} collective-permute-done((bf16[4,512,128]{2,1,0:T(8,128)(2,1)S(1)}, bf16[4,512,128]{2,1,0:T(8,128)(2,1)S(1)}, u32[]{:S(2)}, u32[]{:S(2)}) %collective-permute-start.6) | collective-permute-done | bytes 524320 | tf_op jit(solution)/shard_map/ppermute | solution.py:328
  148.5 4.0 %collective-permute-start.9 = (bf16[512,128]{1,0:T(8,128)(2,1)S(1)}, bf16[512,128]{1,0:T(8,128)(2,1)S(1)}, u32[]{:S(2)}, u32[]{:S(2)}) collective-permute-start(bf16[512,128]{1,0:T(8,128)(2,1)S(1)} %get-tuple-element.77), channel_id=1, source_target_pairs={{0,160},{32,384},{64,224},{96,448},{128,288},{160,0},{192,352},{22... | collective-permute-start | bytes 393224 | tf_op jit(solution)/shard_map/ppermute | solution.py:332
  152.5 6.0 %collective-permute-start.8 = (bf16[512,128]{1,0:T(8,128)(2,1)S(1)}, bf16[512,128]{1,0:T(8,128)(2,1)S(1)}, u32[]{:S(2)}, u32[]{:S(2)}) collective-permute-start(bf16[512,128]{1,0:T(8,128)(2,1)S(1)} %shard_map.89), channel_id=1, source_target_pairs={{0,128},{32,416},{64,192},{96,480},{128,256},{160,32},{192,320},{2... | collective-permute-start | bytes 393224 | tf_op jit(solution)/shard_map/ppermute | solution.py:331
  158.5 2.0 %all_gather.23.gives = bf16[1024,128]{1,0:T(8,128)(2,1)S(1)} all-gather(bf16[512,128]{1,0:T(8,128)(2,1)S(1)} %get-tuple-element.75), channel_id=1, replica_groups={{0,32},{64,96},{128,160},{192,224},{256,288},{320,352},{384,416},{448,4..., dimensions={0}, use_global_device_ids=true | all-gather | bytes 393216 | tf_op jit(solution)/shard_map/all_gather | solution.py:271
  160.5 1.8 %collective-permute-done.8.same = bf16[512,128]{1,0:T(8,128)(2,1)S(1)} collective-permute-done((bf16[512,128]{1,0:T(8,128)(2,1)S(1)}, bf16[512,128]{1,0:T(8,128)(2,1)S(1)}, u32[]{:S(2)}, u32[]{:S(2)}) %collective-permute-start.8) | collective-permute-done | bytes 131104 | tf_op jit(solution)/shard_map/ppermute | solution.py:331
  162.3 0.8 shard_map.90
  (37 shorter events, 3.7 us)
Async XLA Ops:
  10.9 17.8 %collective-permute-start = (bf16[1056,128]{1,0:T(8,128)(2,1)S(1)}, bf16[1056,128]{1,0:T(8,128)(2,1)S(1)}, u32[]{:S(2)}, u32[]{:S(2)}) collective-permute-start(bf16[1056,128]{1,0:T(8,128)(2,1)S(1)} %all_gather.18.own), channel_id=1, source_target_pairs={{0,128},{32,416},{64,192},{96,480},{128,256},{160,32},{192,320},{2... | collective-permute-start | bytes 811016 | tf_op jit(solution)/shard_map/ppermute | solution.py:286
  19.1 29.7 %all-to-all-start = ((bf16[32,96,128]{2,1,0:T(8,128)(2,1)}), bf16[32,96,128]{2,1,0:T(8,128)(2,1)S(1)}, u32[]{:S(2)}, u32[]{:S(2)}) async-start(bf16[32,96,128]{2,1,0:T(8,128)(2,1)} %shard_map.79), calls=%async_computation | async-start | bytes 1572864 | tf_op jit(solution)/shard_map/all_to_all | solution.py:262
  28.7 12.0 %collective-permute-start.2 = (bf16[1056,128]{1,0:T(8,128)(2,1)S(1)}, bf16[1056,128]{1,0:T(8,128)(2,1)S(1)}, u32[]{:S(2)}, u32[]{:S(2)}) collective-permute-start(bf16[1056,128]{1,0:T(8,128)(2,1)S(1)} %all_gather.18.own), channel_id=1, source_target_pairs={{0,64},{64,128},{128,192},{192,256},{256,320},{320,384},{384,448},... | collective-permute-start | bytes 811016 | tf_op jit(solution)/shard_map/ppermute | solution.py:289
  31.0 18.0 %collective-permute-start.3 = (bf16[1056,128]{1,0:T(8,128)(2,1)S(1)}, bf16[1056,128]{1,0:T(8,128)(2,1)S(1)}, u32[]{:S(2)}, u32[]{:S(2)}) collective-permute-start(bf16[1056,128]{1,0:T(8,128)(2,1)S(1)} %collective-permute-done), channel_id=1, source_target_pairs={{0,128},{32,416},{64,192},{96,480},{128,256},{160,32},{192,320},{2... | collective-permute-start | bytes 811016 | tf_op jit(solution)/shard_map/ppermute | solution.py:290
  32.9 12.0 %collective-permute-start.1 = (bf16[1056,128]{1,0:T(8,128)(2,1)S(1)}, bf16[1056,128]{1,0:T(8,128)(2,1)S(1)}, u32[]{:S(2)}, u32[]{:S(2)}) collective-permute-start(bf16[1056,128]{1,0:T(8,128)(2,1)S(1)} %collective-permute-done), channel_id=1, source_target_pairs={{0,64},{64,128},{128,192},{192,256},{256,320},{320,384},{384,448},... | collective-permute-start | bytes 811016 | tf_op jit(solution)/shard_map/ppermute | solution.py:290
  40.7 2.3 %copy-start.8 = (s32[2,128,1]{1,2,0:T(1,128)S(1)}, s32[2,128,1]{1,2,0:T(1,128)}, u32[]{:S(2)}) copy-start(s32[2,128,1]{1,2,0:T(1,128)} %param.8) | copy-start | bytes 3076
  43.2 0.6 copy-start.2
  43.8 4.5 %copy-start.4 = (bf16[96,128]{1,0:T(8,128)(2,1)}, bf16[96,128]{1,0:T(8,128)(2,1)S(1)}, u32[]{:S(2)}) copy-start(bf16[96,128]{1,0:T(8,128)(2,1)S(1)} %get-tuple-element.46.pick_one) | copy-start | bytes 73732
  50.2 22.9 %copy-start.6 = (f32[96,128]{1,0:T(8,128)}, f32[96,128]{1,0:T(8,128)S(1)}, u32[]{:S(2)}) copy-start(f32[96,128]{1,0:T(8,128)S(1)} %get-tuple-element.61.gate) | copy-start | bytes 147460
  50.2 22.9 %copy-start.9 = (bf16[96,1280]{1,0:T(8,128)(2,1)}, bf16[96,1280]{1,0:T(8,128)(2,1)S(1)}, u32[]{:S(2)}) copy-start(bf16[96,1280]{1,0:T(8,128)(2,1)S(1)} %get-tuple-element.65) | copy-start | bytes 737284
  50.2 22.9 %copy-start.1 = (bf16[128,2048]{1,0:T(8,128)(2,1)S(1)}, bf16[128,2048]{1,0:T(8,128)(2,1)}, u32[]{:S(2)}) copy-start(bf16[128,2048]{1,0:T(8,128)(2,1)} %tokens.3) | copy-start | bytes 1572868
  50.2 22.9 %copy-start.3 = (bf16[96,128]{1,0:T(8,128)(2,1)S(1)}, bf16[96,128]{1,0:T(8,128)(2,1)}, u32[]{:S(2)}) copy-start(bf16[96,128]{1,0:T(8,128)(2,1)} %copy-done.2) | copy-start | bytes 73732
  50.2 22.9 %copy-start.5 = (bf16[96,128]{1,0:T(8,128)(2,1)S(1)}, bf16[96,128]{1,0:T(8,128)(2,1)}, u32[]{:S(2)}) copy-start(bf16[96,128]{1,0:T(8,128)(2,1)} %copy-done.4) | copy-start | bytes 73732
  93.2 18.2 %copy-start = (bf16[128,2048]{1,0:T(8,128)(2,1)S(1)}, bf16[128,2048]{1,0:T(8,128)(2,1)}, u32[]{:S(2)}) copy-start(bf16[128,2048]{1,0:T(8,128)(2,1)} %cotangent.3) | copy-start | bytes 1572868
  112.9 17.8 %all-to-all-start.4 = ((bf16[32,48,128]{2,1,0:T(8,128)(2,1)}), bf16[32,48,128]{2,1,0:T(8,128)(2,1)S(1)}, u32[]{:S(2)}, u32[]{:S(2)}) async-start(bf16[32,48,128]{2,1,0:T(8,128)(2,1)} %bitcast.9), calls=%async_computation.4 | async-start | bytes 786432 | tf_op jit(solution)/shard_map/all_to_all | solution.py:262
  118.7 5.1 %copy-start.10 = (bf16[96,1280]{1,0:T(8,128)(2,1)S(1)}, bf16[96,1280]{1,0:T(8,128)(2,1)}, u32[]{:S(2)}) copy-start(bf16[96,1280]{1,0:T(8,128)(2,1)} %copy-done.9) | copy-start | bytes 737284
  118.8 12.0 %copy-start.7 = (f32[96,128]{1,0:T(8,128)S(1)}, f32[96,128]{1,0:T(8,128)}, u32[]{:S(2)}) copy-start(f32[96,128]{1,0:T(8,128)} %copy-done.6) | copy-start | bytes 147460
  119.8 17.7 %collective-permute-start.5 = (bf16[96,2560]{1,0:T(8,128)(2,1)}, bf16[96,2560]{1,0:T(8,128)(2,1)S(1)}, u32[]{:S(2)}, u32[]{:S(2)}) collective-permute-start(bf16[96,2560]{1,0:T(8,128)(2,1)} %get-tuple-element.71), channel_id=1, source_target_pairs={{0,32},{32,0},{64,96},{96,64},{128,160},{160,128},{192,224},{224,1... | collective-permute-start | bytes 1474568 | tf_op jit(solution)/shard_map/ppermute | solution.py:314
  123.9 13.6 %collective-permute-start.4 = (bf16[96,1280]{1,0:T(8,128)(2,1)S(1)}, bf16[96,1280]{1,0:T(8,128)(2,1)S(1)}, u32[]{:S(2)}, u32[]{:S(2)}) collective-permute-start(bf16[96,1280]{1,0:T(8,128)(2,1)S(1)} %copy-done.10), channel_id=1, source_target_pairs={{0,32},{32,0},{64,96},{96,64},{128,160},{160,128},{192,224},{224,1... | collective-permute-start | bytes 737288 | tf_op jit(solution)/shard_map/ppermute | solution.py:302
  138.2 10.2 %collective-permute-start.6 = (bf16[4,512,128]{2,1,0:T(8,128)(2,1)S(1)}, bf16[4,512,128]{2,1,0:T(8,128)(2,1)S(1)}, u32[]{:S(2)}, u32[]{:S(2)}) collective-permute-start(bf16[4,512,128]{2,1,0:T(8,128)(2,1)S(1)} %get-tuple-element.73), channel_id=1, source_target_pairs={{0,64},{64,128},{128,192},{192,256},{256,320},{320,384},{384,448},... | collective-permute-start | bytes 1572872 | tf_op jit(solution)/shard_map/ppermute | solution.py:328
  140.2 12.3 %collective-permute-start.7 = (bf16[1,512,128]{2,1,0:T(8,128)(2,1)S(1)}, bf16[1,512,128]{2,1,0:T(8,128)(2,1)S(1)}, u32[]{:S(2)}, u32[]{:S(2)}) collective-permute-start(bf16[1,512,128]{2,1,0:T(8,128)(2,1)S(1)} %get-tuple-element.76), channel_id=1, source_target_pairs={{0,128},{32,416},{64,192},{96,480},{128,256},{160,32},{192,320},{2... | collective-permute-start | bytes 393224 | tf_op jit(solution)/shard_map/ppermute | solution.py:328
  148.5 12.0 %collective-permute-start.9 = (bf16[512,128]{1,0:T(8,128)(2,1)S(1)}, bf16[512,128]{1,0:T(8,128)(2,1)S(1)}, u32[]{:S(2)}, u32[]{:S(2)}) collective-permute-start(bf16[512,128]{1,0:T(8,128)(2,1)S(1)} %get-tuple-element.77), channel_id=1, source_target_pairs={{0,160},{32,384},{64,224},{96,448},{128,288},{160,0},{192,352},{22... | collective-permute-start | bytes 393224 | tf_op jit(solution)/shard_map/ppermute | solution.py:332
  152.5 9.7 %collective-permute-start.8 = (bf16[512,128]{1,0:T(8,128)(2,1)S(1)}, bf16[512,128]{1,0:T(8,128)(2,1)S(1)}, u32[]{:S(2)}, u32[]{:S(2)}) collective-permute-start(bf16[512,128]{1,0:T(8,128)(2,1)S(1)} %shard_map.89), channel_id=1, source_target_pairs={{0,128},{32,416},{64,192},{96,480},{128,256},{160,32},{192,320},{2... | collective-permute-start | bytes 393224 | tf_op jit(solution)/shard_map/ppermute | solution.py:331

commit v9 on v8

--- a/solution.py
+++ b/solution.py
@@ -195,24 +195,31 @@
     split(dense, grad_pre, own, mate)
 
 
-def weight_kernel(
-    grads_own, grads_both, kept_own, kept_mate, one_own, one_mate,
-    near, far, next_chip, own_chip, rows, hidden, grads, pre
-):
+def products(operands, first, targets, rows, hidden, grads, pre):
+    grads_own, grads_both, kept_own, kept_mate, one_own, one_mate = operands
     mate = pl.multiple_of((1 - lax.rem(lax.axis_index("ctx"), 2)) * SLOTS, SLOTS)
     kept = (kept_own[...], kept_mate[...], one_own[:, :HALF], one_mate[:, :HALF])
     grad = (grads_own[...], grads_both[pl.ds(mate, SLOTS), :], one_own[:, HALF:], one_mate[:, HALF:])
+    columns = slice(first * LANE, (first + 4) * LANE)
     for i in range(4):
         to = slice(i * SLOTS, (i + 1) * SLOTS)
-        rows[to, :], hidden[to, :] = kept[i][:, : D // 2], kept[i][:, D // 2 :]
-        grads[to, :], pre[to, :] = grad[i][:, : D // 2], grad[i][:, D // 2 :]
+        rows[to, :], hidden[to, :] = kept[i][:, columns], kept[i][:, D // 2 :]
+        grads[to, :], pre[to, :] = grad[i][:, columns], grad[i][:, D // 2 :]
     part_in = over_rows(pre[...], rows[...])
     part_out = over_rows(hidden[...], grads[...])
-    targets = [(near, i) for i in range(4)] + [(far, 0), (next_chip, 0), (next_chip, 1), (own_chip, 0)]
     for i, (out, to) in enumerate(targets):
         at = slice(i * LANE, (i + 1) * LANE)
         out[to, :G, :] = part_in[:, at].astype(out.dtype)
         out[to, G:, :] = part_out[:, at].astype(out.dtype)
+
+
+def near_kernel(*refs):
+    products(refs[:6], 0, [(refs[6], i) for i in range(4)], *refs[7:])
+
+
+def rest_kernel(*refs):
+    far, next_chip, own_chip = refs[6:9]
+    products(refs[:6], 4, [(far, 0), (next_chip, 0), (next_chip, 1), (own_chip, 0)], *refs[9:])
 
 
 def cross_kernel(near, next_chip, cross, give):
@@ -318,13 +325,14 @@
     grads_own, grads_mate = call(first_grad_kernel, [KEPT, KEPT], [DENSE])(
         over_exp(leaving), wb, positive, gate
     )
-    half, narrow = ((4 * SLOTS, D // 2), bf16), ((4 * SLOTS, G), bf16)
+    half, narrow = ((4 * SLOTS, D // 4), bf16), ((4 * SLOTS, G), bf16)
     chunk = (2 * G, LANE)
-    near, far, next_chip, own_chip = call(
-        weight_kernel,
-        [((4, *chunk), bf16), ((1, *chunk), bf16), ((2, *chunk), f32), ((1, *chunk), f32)],
-        [half, narrow, half, narrow],
-    )(grads_own, both_cores(grads_mate), kept_own, kept_mate, one_own, one_mate)
+    operands = grads_own, both_cores(grads_mate), kept_own, kept_mate, one_own, one_mate
+    buffers = [half, narrow, half, narrow]
+    (near,) = call(near_kernel, [((4, *chunk), bf16)], buffers)(*operands)
+    far, next_chip, own_chip = call(
+        rest_kernel, [((1, *chunk), bf16), ((2, *chunk), f32), ((1, *chunk), f32)], buffers
+    )(*operands)
     near, far = lax.ppermute(near, "ctx", around), lax.ppermute(far, "ctx", two_on)
     cross, give = call(cross_kernel, [(chunk, bf16)] * 2)(near, next_chip)
     (same,) = call(same_kernel, [(chunk, bf16)])(near, far, next_chip)

time: 164 us -> 164 us (level)
  no operation moved by 1% of the time
where the time goes in v9:
time: 164 us; the launch traced here: 163 us
  blocking collectives  86.7 us (53%)
  starting transfers between devices  49.5 us (30%)
  Pallas kernels  14 us (9%)
  waiting for transfers between devices  11.6 us (7%)
    all_to_all x3, blocking collectives, over_exp(): return lax.all_to_all(shaped, 'exp', 0, 0, tiled=True).reshape(buffer.shape)  58.7 us
    all_gather x6, blocking collectives, both_cores(): lax.all_gather(value, 'ctx', axis=0, tiled=True, axis_index_groups=cores)  28 us
    all_to_all x2, starting transfers between devices, over_exp(): return lax.all_to_all(shaped, 'exp', 0, 0, tiled=True).reshape(buffer.shape)  15.5 us
    ppermute x1, starting transfers between devices, on_device(): same = lax.ppermute(same, 'ctx', two_on)  5.95 us
    all_to_all x2, waiting for transfers between devices, over_exp(): return lax.all_to_all(shaped, 'exp', 0, 0, tiled=True).reshape(buffer.shape)  5.48 us
    ppermute x1, starting transfers between devices, on_device(): two = lax.ppermute(own, 'ctx', two_on)  5.27 us
    ppermute x1, starting transfers between devices, on_device(): lax.ppermute(far, 'ctx', two_on)  4.55 us
    ppermute x1, starting transfers between devices, on_device(): one_mate = lax.ppermute(one_mate, 'ctx', across)  4.04 us
  transfers between devices with their start and end apart: 12, of which 5 were waited for; matrix products, arithmetic and copies ran while one was open for 0% of the time, Pallas kernels for 3%

profile of v9, /device:TPU:1, one launch (start us, length us, event | category | flops | bytes accessed | tf_op | source)
XLA Modules:
  0.0 163.3 jit_solution(10208281665990220536)
XLA Ops:
  0.6 1.5 shard_map.77
  2.2 8.7 %all_gather.18.own = bf16[1056,128]{1,0:T(8,128)(2,1)S(1)} all-gather(bf16[528,128]{1,0:T(8,128)(2,1)} %shard_map.77), channel_id=1, replica_groups={{0,32},{64,96},{128,160},{192,224},{256,288},{320,352},{384,416},{448,4..., dimensions={0}, use_global_device_ids=true | all-gather | bytes 405504 | tf_op jit(solution)/shard_map/all_gather | solution.py:278
  10.9 5.3 %collective-permute-start = (bf16[1056,128]{1,0:T(8,128)(2,1)S(1)}, bf16[1056,128]{1,0:T(8,128)(2,1)S(1)}, u32[]{:S(2)}, u32[]{:S(2)}) collective-permute-start(bf16[1056,128]{1,0:T(8,128)(2,1)S(1)} %all_gather.18.own), channel_id=1, source_target_pairs={{0,128},{32,416},{64,192},{96,480},{128,256},{160,32},{192,320},{2... | collective-permute-start | bytes 811016 | tf_op jit(solution)/shard_map/ppermute | solution.py:293
  16.2 2.9 %shard_map.79 = bf16[32,96,128]{2,1,0:T(8,128)(2,1)} custom-call(bf16[128,2048]{1,0:T(8,128)(2,1)} %tokens.3, bf16[128,2048]{1,0:T(8,128)(2,1)} %cotangent.3, s32[2,128]{1,0:T(2,128)} %bitcast.19), custom_call_target="tpu_custom_call" | custom-call | tf_op jit(solution)/shard_map/pallas_call | solution.py:286
  19.0 9.7 %all-to-all-start = ((bf16[32,96,128]{2,1,0:T(8,128)(2,1)}), bf16[32,96,128]{2,1,0:T(8,128)(2,1)S(1)}, u32[]{:S(2)}, u32[]{:S(2)}) async-start(bf16[32,96,128]{2,1,0:T(8,128)(2,1)} %shard_map.79), calls=%async_computation | async-start | bytes 1572864 | tf_op jit(solution)/shard_map/all_to_all | solution.py:269
  28.7 2.2 %collective-permute-start.2 = (bf16[1056,128]{1,0:T(8,128)(2,1)S(1)}, bf16[1056,128]{1,0:T(8,128)(2,1)S(1)}, u32[]{:S(2)}, u32[]{:S(2)}) collective-permute-start(bf16[1056,128]{1,0:T(8,128)(2,1)S(1)} %all_gather.18.own), channel_id=1, source_target_pairs={{0,64},{64,128},{128,192},{192,256},{256,320},{320,384},{384,448},... | collective-permute-start | bytes 811016 | tf_op jit(solution)/shard_map/ppermute | solution.py:296
  30.9 1.9 %collective-permute-start.3 = (bf16[1056,128]{1,0:T(8,128)(2,1)S(1)}, bf16[1056,128]{1,0:T(8,128)(2,1)S(1)}, u32[]{:S(2)}, u32[]{:S(2)}) collective-permute-start(bf16[1056,128]{1,0:T(8,128)(2,1)S(1)} %collective-permute-done), channel_id=1, source_target_pairs={{0,128},{32,416},{64,192},{96,480},{128,256},{160,32},{192,320},{2... | collective-permute-start | bytes 811016 | tf_op jit(solution)/shard_map/ppermute | solution.py:297
  32.9 2.2 %collective-permute-start.1 = (bf16[1056,128]{1,0:T(8,128)(2,1)S(1)}, bf16[1056,128]{1,0:T(8,128)(2,1)S(1)}, u32[]{:S(2)}, u32[]{:S(2)}) collective-permute-start(bf16[1056,128]{1,0:T(8,128)(2,1)S(1)} %collective-permute-done), channel_id=1, source_target_pairs={{0,64},{64,128},{128,192},{192,256},{256,320},{320,384},{384,448},... | collective-permute-start | bytes 811016 | tf_op jit(solution)/shard_map/ppermute | solution.py:297
  35.1 5.6 %all_gather.20.pair_2 = bf16[2112,128]{1,0:T(8,128)(2,1)S(1)} all-gather(bf16[1056,128]{1,0:T(8,128)(2,1)S(1)} %collective-permute-done), channel_id=1, replica_groups={{0,32},{64,96},{128,160},{192,224},{256,288},{320,352},{384,416},{448,4..., dimensions={0}, use_global_device_ids=true | all-gather | bytes 811008 | tf_op jit(solution)/shard_map/all_gather | solution.py:278
  40.7 2.3 %all_gather.19.pair_1 = bf16[2112,128]{1,0:T(8,128)(2,1)S(1)} all-gather(bf16[1056,128]{1,0:T(8,128)(2,1)S(1)} %collective-permute-done.2), channel_id=1, replica_groups={{0,32},{64,96},{128,160},{192,224},{256,288},{320,352},{384,416},{448,4..., dimensions={0}, use_global_device_ids=true | all-gather | bytes 811008 | tf_op jit(solution)/shard_map/all_gather | solution.py:278
  43.8 1.1 collective-permute-done.1
  44.9 3.4 %all_gather.21.pair_3 = bf16[2112,128]{1,0:T(8,128)(2,1)S(1)} all-gather(bf16[1056,128]{1,0:T(8,128)(2,1)S(1)} %collective-permute-done.1), channel_id=1, replica_groups={{0,32},{64,96},{128,160},{192,224},{256,288},{320,352},{384,416},{448,4..., dimensions={0}, use_global_device_ids=true | all-gather | bytes 811008 | tf_op jit(solution)/shard_map/all_gather | solution.py:278
  48.9 1.8 %shard_map.81 = (bf16[1536,128]{1,0:T(8,128)(2,1)S(1)}, f32[96,256]{1,0:T(8,128)S(1)}, bf16[96,1280]{1,0:T(8,128)(2,1)S(1)}, bf16[96,1280]{1,0:T(8,128)(2,1)}, f...) custom-call(bf16[96,2048]{1,0:T(8,128)(2,1)S(1)} %get-tuple-element., ...), custom_call_target="tpu_custom_call" | custom-call | tf_op jit(solution)/shard_map/pallas_call | solution.py:304
  50.7 22.8 %all_to_all.25 = bf16[32,48,128]{2,1,0:T(8,128)(2,1)S(1)} all-to-all(bf16[32,48,128]{2,1,0:T(8,128)(2,1)S(1)} %bitcast.16), channel_id=1, replica_groups=mesh['ctx'=16,'exp'=32] {'exp'}, dimensions={0} | all-to-all | bytes 786432 | tf_op jit(solution)/shard_map/all_to_all | solution.py:269
  74.3 17.6 %all_to_all.26 = bf16[32,48,128]{2,1,0:T(8,128)(2,1)S(1)} all-to-all(bf16[32,48,128]{2,1,0:T(8,128)(2,1)S(1)} %bitcast.18), channel_id=1, replica_groups=mesh['ctx'=16,'exp'=32] {'exp'}, dimensions={0} | all-to-all | bytes 786432 | tf_op jit(solution)/shard_map/all_to_all | solution.py:269
  92.0 1.7 %shard_map.83 = (bf16[1536,128]{1,0:T(8,128)(2,1)S(1)}, bf16[96,2048]{1,0:T(8,128)(2,1)S(1)}, bf16[96,256]{1,0:T(8,128)(2,1)S(1)}, bf16[96,2048]{1,0:T(8,128)(2,1)S(1)}, bf16[96,256]{1,0:T(8,128)(2,1)S(1)}) custom-call(bf16[1536,128]{1,0:T(8,128)(2,1)S(1)} %bitcast.15, bf16[96,2048]{1,0:T(8,128)(2,1)S(1)} %get-tuple-element.54.upstream, ...), custom_call_target="tpu_custom_call" | custom-call | tf_op jit(solution)/shard_map/pallas_call | solution.py:317
  93.7 18.2 %all_to_all.27 = bf16[32,48,128]{2,1,0:T(8,128)(2,1)S(1)} all-to-all(bf16[32,48,128]{2,1,0:T(8,128)(2,1)S(1)} %bitcast.17), channel_id=1, replica_groups=mesh['ctx'=16,'exp'=32] {'exp'}, dimensions={0} | all-to-all | bytes 786432 | tf_op jit(solution)/shard_map/all_to_all | solution.py:269
  111.9 1.6 shard_map.84
  113.4 5.8 %all-to-all-start.4 = ((bf16[32,48,128]{2,1,0:T(8,128)(2,1)}), bf16[32,48,128]{2,1,0:T(8,128)(2,1)S(1)}, u32[]{:S(2)}, u32[]{:S(2)}) async-start(bf16[32,48,128]{2,1,0:T(8,128)(2,1)} %bitcast.9), calls=%async_computation.4 | async-start | bytes 786432 | tf_op jit(solution)/shard_map/all_to_all | solution.py:269
  119.2 1.0 shard_map.86
  120.3 4.0 %collective-permute-start.5 = (bf16[96,2560]{1,0:T(8,128)(2,1)}, bf16[96,2560]{1,0:T(8,128)(2,1)S(1)}, u32[]{:S(2)}, u32[]{:S(2)}) collective-permute-start(bf16[96,2560]{1,0:T(8,128)(2,1)} %get-tuple-element.70), channel_id=1, source_target_pairs={{0,32},{32,0},{64,96},{96,64},{128,160},{160,128},{192,224},{224,1... | collective-permute-start | bytes 1474568 | tf_op jit(solution)/shard_map/ppermute | solution.py:321
  124.3 1.9 %collective-permute-start.4 = (bf16[96,1280]{1,0:T(8,128)(2,1)}, bf16[96,1280]{1,0:T(8,128)(2,1)S(1)}, u32[]{:S(2)}, u32[]{:S(2)}) collective-permute-start(bf16[96,1280]{1,0:T(8,128)(2,1)} %get-tuple-element.64), channel_id=1, source_target_pairs={{0,32},{32,0},{64,96},{96,64},{128,160},{160,128},{192,224},{224,1... | collective-permute-start | bytes 737288 | tf_op jit(solution)/shard_map/ppermute | solution.py:309
  126.2 5.0 %all-to-all-done.4 = bf16[32,48,128]{2,1,0:T(8,128)(2,1)S(1)} async-done(((bf16[32,48,128]{2,1,0:T(8,128)(2,1)}), bf16[32,48,128]{2,1,0:T(8,128)(2,1)S(1)}, u32[]{:S(2)}, u32[]{:S(2)}) %all-to-all-start.4) | async-done | bytes 393248 | tf_op jit(solution)/shard_map/all_to_all | solution.py:269
  132.0 6.0 %all_gather.22.refs_1_ = bf16[192,1280]{1,0:T(8,128)(2,1)S(1)} all-gather(bf16[96,1280]{1,0:T(8,128)(2,1)S(1)} %get-tuple-element.62), channel_id=1, replica_groups={{0,32},{64,96},{128,160},{192,224},{256,288},{320,352},{384,416},{448,4..., dimensions={0}, use_global_device_ids=true | all-gather | bytes 737280 | tf_op jit(solution)/shard_map/all_gather | solution.py:278
  138.4 2.0 %collective-permute-start.6 = (bf16[4,512,128]{2,1,0:T(8,128)(2,1)S(1)}, bf16[4,512,128]{2,1,0:T(8,128)(2,1)S(1)}, u32[]{:S(2)}, u32[]{:S(2)}) collective-permute-start(bf16[4,512,128]{2,1,0:T(8,128)(2,1)S(1)} %shard_map.88), channel_id=1, source_target_pairs={{0,64},{64,128},{128,192},{192,256},{256,320},{320,384},{384,448},... | collective-permute-start | bytes 1572872 | tf_op jit(solution)/shard_map/ppermute | solution.py:336
  140.9 4.5 %collective-permute-start.7 = (bf16[1,512,128]{2,1,0:T(8,128)(2,1)S(1)}, bf16[1,512,128]{2,1,0:T(8,128)(2,1)S(1)}, u32[]{:S(2)}, u32[]{:S(2)}) collective-permute-start(bf16[1,512,128]{2,1,0:T(8,128)(2,1)S(1)} %get-tuple-element.74), channel_id=1, source_target_pairs={{0,128},{32,416},{64,192},{96,480},{128,256},{160,32},{192,320},{2... | collective-permute-start | bytes 393224 | tf_op jit(solution)/shard_map/ppermute | solution.py:336
  145.5 3.2 %collective-permute-done.6.near = bf16[4,512,128]{2,1,0:T(8,128)(2,1)S(1)} collective-permute-done((bf16[4,512,128]{2,1,0:T(8,128)(2,1)S(1)}, bf16[4,512,128]{2,1,0:T(8,128)(2,1)S(1)}, u32[]{:S(2)}, u32[]{:S(2)}) %collective-permute-start.6) | collective-permute-done | bytes 524320 | tf_op jit(solution)/shard_map/ppermute | solution.py:336
  148.7 4.0 %collective-permute-start.9 = (bf16[512,128]{1,0:T(8,128)(2,1)S(1)}, bf16[512,128]{1,0:T(8,128)(2,1)S(1)}, u32[]{:S(2)}, u32[]{:S(2)}) collective-permute-start(bf16[512,128]{1,0:T(8,128)(2,1)S(1)} %get-tuple-element.75), channel_id=1, source_target_pairs={{0,160},{32,384},{64,224},{96,448},{128,288},{160,0},{192,352},{22... | collective-permute-start | bytes 393224 | tf_op jit(solution)/shard_map/ppermute | solution.py:340
  152.8 6.0 %collective-permute-start.8 = (bf16[512,128]{1,0:T(8,128)(2,1)S(1)}, bf16[512,128]{1,0:T(8,128)(2,1)S(1)}, u32[]{:S(2)}, u32[]{:S(2)}) collective-permute-start(bf16[512,128]{1,0:T(8,128)(2,1)S(1)} %shard_map.90), channel_id=1, source_target_pairs={{0,128},{32,416},{64,192},{96,480},{128,256},{160,32},{192,320},{2... | collective-permute-start | bytes 393224 | tf_op jit(solution)/shard_map/ppermute | solution.py:339
  158.7 2.0 %all_gather.23.gives = bf16[1024,128]{1,0:T(8,128)(2,1)S(1)} all-gather(bf16[512,128]{1,0:T(8,128)(2,1)S(1)} %get-tuple-element.73), channel_id=1, replica_groups={{0,32},{64,96},{128,160},{192,224},{256,288},{320,352},{384,416},{448,4..., dimensions={0}, use_global_device_ids=true | all-gather | bytes 393216 | tf_op jit(solution)/shard_map/all_gather | solution.py:278
  160.7 1.8 %collective-permute-done.8.same = bf16[512,128]{1,0:T(8,128)(2,1)S(1)} collective-permute-done((bf16[512,128]{1,0:T(8,128)(2,1)S(1)}, bf16[512,128]{1,0:T(8,128)(2,1)S(1)}, u32[]{:S(2)}, u32[]{:S(2)}) %collective-permute-start.8) | collective-permute-done | bytes 131104 | tf_op jit(solution)/shard_map/ppermute | solution.py:339
  162.5 0.8 shard_map.91
  (34 shorter events, 3.9 us)
Async XLA Ops:
  10.9 17.8 %collective-permute-start = (bf16[1056,128]{1,0:T(8,128)(2,1)S(1)}, bf16[1056,128]{1,0:T(8,128)(2,1)S(1)}, u32[]{:S(2)}, u32[]{:S(2)}) collective-permute-start(bf16[1056,128]{1,0:T(8,128)(2,1)S(1)} %all_gather.18.own), channel_id=1, source_target_pairs={{0,128},{32,416},{64,192},{96,480},{128,256},{160,32},{192,320},{2... | collective-permute-start | bytes 811016 | tf_op jit(solution)/shard_map/ppermute | solution.py:293
  19.0 29.7 %all-to-all-start = ((bf16[32,96,128]{2,1,0:T(8,128)(2,1)}), bf16[32,96,128]{2,1,0:T(8,128)(2,1)S(1)}, u32[]{:S(2)}, u32[]{:S(2)}) async-start(bf16[32,96,128]{2,1,0:T(8,128)(2,1)} %shard_map.79), calls=%async_computation | async-start | bytes 1572864 | tf_op jit(solution)/shard_map/all_to_all | solution.py:269
  28.7 12.0 %collective-permute-start.2 = (bf16[1056,128]{1,0:T(8,128)(2,1)S(1)}, bf16[1056,128]{1,0:T(8,128)(2,1)S(1)}, u32[]{:S(2)}, u32[]{:S(2)}) collective-permute-start(bf16[1056,128]{1,0:T(8,128)(2,1)S(1)} %all_gather.18.own), channel_id=1, source_target_pairs={{0,64},{64,128},{128,192},{192,256},{256,320},{320,384},{384,448},... | collective-permute-start | bytes 811016 | tf_op jit(solution)/shard_map/ppermute | solution.py:296
  30.9 18.0 %collective-permute-start.3 = (bf16[1056,128]{1,0:T(8,128)(2,1)S(1)}, bf16[1056,128]{1,0:T(8,128)(2,1)S(1)}, u32[]{:S(2)}, u32[]{:S(2)}) collective-permute-start(bf16[1056,128]{1,0:T(8,128)(2,1)S(1)} %collective-permute-done), channel_id=1, source_target_pairs={{0,128},{32,416},{64,192},{96,480},{128,256},{160,32},{192,320},{2... | collective-permute-start | bytes 811016 | tf_op jit(solution)/shard_map/ppermute | solution.py:297
  32.9 12.0 %collective-permute-start.1 = (bf16[1056,128]{1,0:T(8,128)(2,1)S(1)}, bf16[1056,128]{1,0:T(8,128)(2,1)S(1)}, u32[]{:S(2)}, u32[]{:S(2)}) collective-permute-start(bf16[1056,128]{1,0:T(8,128)(2,1)S(1)} %collective-permute-done), channel_id=1, source_target_pairs={{0,64},{64,128},{128,192},{192,256},{256,320},{320,384},{384,448},... | collective-permute-start | bytes 811016 | tf_op jit(solution)/shard_map/ppermute | solution.py:297
  40.7 2.3 %copy-start.8 = (s32[2,128,1]{1,2,0:T(1,128)S(1)}, s32[2,128,1]{1,2,0:T(1,128)}, u32[]{:S(2)}) copy-start(s32[2,128,1]{1,2,0:T(1,128)} %param.8) | copy-start | bytes 3076
  43.2 0.6 copy-start.2
  43.8 4.5 %copy-start.4 = (bf16[96,128]{1,0:T(8,128)(2,1)}, bf16[96,128]{1,0:T(8,128)(2,1)S(1)}, u32[]{:S(2)}) copy-start(bf16[96,128]{1,0:T(8,128)(2,1)S(1)} %get-tuple-element.45.pick_one) | copy-start | bytes 73732
  50.7 22.8 %copy-start.6 = (f32[96,128]{1,0:T(8,128)}, f32[96,128]{1,0:T(8,128)S(1)}, u32[]{:S(2)}) copy-start(f32[96,128]{1,0:T(8,128)S(1)} %get-tuple-element.60.gate) | copy-start | bytes 147460
  50.7 22.8 %copy-start.1 = (bf16[128,2048]{1,0:T(8,128)(2,1)S(1)}, bf16[128,2048]{1,0:T(8,128)(2,1)}, u32[]{:S(2)}) copy-start(bf16[128,2048]{1,0:T(8,128)(2,1)} %tokens.3) | copy-start | bytes 1572868
  50.7 22.8 %copy-start.3 = (bf16[96,128]{1,0:T(8,128)(2,1)S(1)}, bf16[96,128]{1,0:T(8,128)(2,1)}, u32[]{:S(2)}) copy-start(bf16[96,128]{1,0:T(8,128)(2,1)} %copy-done.2) | copy-start | bytes 73732
  50.7 22.8 %copy-start.5 = (bf16[96,128]{1,0:T(8,128)(2,1)S(1)}, bf16[96,128]{1,0:T(8,128)(2,1)}, u32[]{:S(2)}) copy-start(bf16[96,128]{1,0:T(8,128)(2,1)} %copy-done.4) | copy-start | bytes 73732
  93.6 18.2 %copy-start = (bf16[128,2048]{1,0:T(8,128)(2,1)S(1)}, bf16[128,2048]{1,0:T(8,128)(2,1)}, u32[]{:S(2)}) copy-start(bf16[128,2048]{1,0:T(8,128)(2,1)} %cotangent.3) | copy-start | bytes 1572868
  113.4 17.8 %all-to-all-start.4 = ((bf16[32,48,128]{2,1,0:T(8,128)(2,1)}), bf16[32,48,128]{2,1,0:T(8,128)(2,1)S(1)}, u32[]{:S(2)}, u32[]{:S(2)}) async-start(bf16[32,48,128]{2,1,0:T(8,128)(2,1)} %bitcast.9), calls=%async_computation.4 | async-start | bytes 786432 | tf_op jit(solution)/shard_map/all_to_all | solution.py:269
  119.2 12.0 %copy-start.7 = (f32[96,128]{1,0:T(8,128)S(1)}, f32[96,128]{1,0:T(8,128)}, u32[]{:S(2)}) copy-start(f32[96,128]{1,0:T(8,128)} %copy-done.6) | copy-start | bytes 147460
  120.3 17.7 %collective-permute-start.5 = (bf16[96,2560]{1,0:T(8,128)(2,1)}, bf16[96,2560]{1,0:T(8,128)(2,1)S(1)}, u32[]{:S(2)}, u32[]{:S(2)}) collective-permute-start(bf16[96,2560]{1,0:T(8,128)(2,1)} %get-tuple-element.70), channel_id=1, source_target_pairs={{0,32},{32,0},{64,96},{96,64},{128,160},{160,128},{192,224},{224,1... | collective-permute-start | bytes 1474568 | tf_op jit(solution)/shard_map/ppermute | solution.py:321
  124.3 13.6 %collective-permute-start.4 = (bf16[96,1280]{1,0:T(8,128)(2,1)}, bf16[96,1280]{1,0:T(8,128)(2,1)S(1)}, u32[]{:S(2)}, u32[]{:S(2)}) collective-permute-start(bf16[96,1280]{1,0:T(8,128)(2,1)} %get-tuple-element.64), channel_id=1, source_target_pairs={{0,32},{32,0},{64,96},{96,64},{128,160},{160,128},{192,224},{224,1... | collective-permute-start | bytes 737288 | tf_op jit(solution)/shard_map/ppermute | solution.py:309
  138.4 10.2 %collective-permute-start.6 = (bf16[4,512,128]{2,1,0:T(8,128)(2,1)S(1)}, bf16[4,512,128]{2,1,0:T(8,128)(2,1)S(1)}, u32[]{:S(2)}, u32[]{:S(2)}) collective-permute-start(bf16[4,512,128]{2,1,0:T(8,128)(2,1)S(1)} %shard_map.88), channel_id=1, source_target_pairs={{0,64},{64,128},{128,192},{192,256},{256,320},{320,384},{384,448},... | collective-permute-start | bytes 1572872 | tf_op jit(solution)/shard_map/ppermute | solution.py:336
  140.9 11.8 %collective-permute-start.7 = (bf16[1,512,128]{2,1,0:T(8,128)(2,1)S(1)}, bf16[1,512,128]{2,1,0:T(8,128)(2,1)S(1)}, u32[]{:S(2)}, u32[]{:S(2)}) collective-permute-start(bf16[1,512,128]{2,1,0:T(8,128)(2,1)S(1)} %get-tuple-element.74), channel_id=1, source_target_pairs={{0,128},{32,416},{64,192},{96,480},{128,256},{160,32},{192,320},{2... | collective-permute-start | bytes 393224 | tf_op jit(solution)/shard_map/ppermute | solution.py:336
  148.7 12.0 %collective-permute-start.9 = (bf16[512,128]{1,0:T(8,128)(2,1)S(1)}, bf16[512,128]{1,0:T(8,128)(2,1)S(1)}, u32[]{:S(2)}, u32[]{:S(2)}) collective-permute-start(bf16[512,128]{1,0:T(8,128)(2,1)S(1)} %get-tuple-element.75), channel_id=1, source_target_pairs={{0,160},{32,384},{64,224},{96,448},{128,288},{160,0},{192,352},{22... | collective-permute-start | bytes 393224 | tf_op jit(solution)/shard_map/ppermute | solution.py:340
  152.8 9.7 %collective-permute-start.8 = (bf16[512,128]{1,0:T(8,128)(2,1)S(1)}, bf16[512,128]{1,0:T(8,128)(2,1)S(1)}, u32[]{:S(2)}, u32[]{:S(2)}) collective-permute-start(bf16[512,128]{1,0:T(8,128)(2,1)S(1)} %shard_map.90), channel_id=1, source_target_pairs={{0,128},{32,416},{64,192},{96,480},{128,256},{160,32},{192,320},{2... | collective-permute-start | bytes 393224 | tf_op jit(solution)/shard_map/ppermute | solution.py:339
